TPU v7x, 128 devices: a whole 4x4x4 slice. The times are simulated.
128 devices in a mesh: row: 16 (over z, y), col: 8 (over x, core).
Axes of the slice: x: 4, y: 4, z: 4, core: 2. Of those that a mesh axis runs over, the one named last changes fastest.
Arguments:
- sub_field: float32 [262144, 128], P(('row', 'col')), may hold values from -2.4 to 2.4
- reluctivity: float32 [2, 262144, 128], P(None, ('row', 'col')), may hold values from 0.3 to 3
- stride: int32 [128], P(('row', 'col')), may hold values from 2 to 511
- counts: int32 [128, 16], P(('row', 'col')), may hold values from 1 to 32, as said below
- source_cell: int32 [128, 16, 32], P(('row', 'col')), may hold values from 0 to 2047
- target_row: int32 [16, 8, 16, 32], P('row', 'col'), may hold values from 0 to 2047
- lower_tiles: float32 [28, 4096, 4096], P(None, 'row', 'col'), may hold values from -0.03125 to 0.03125
- diag_inverse: float32 [8, 4096, 4096], P(None, 'col', 'row'), may hold values from -1 to 2, as said below
Outputs:
- solution: float32 [8, 8, 512, 128], P(None, 'col', 'row')
Inputs may be any that keep to these rules, and one draw needn't show every extreme that they name: `counts`: every subdomain sends at least one contribution to every grid row; in every draw one grid row receives 32 contributions from every subdomain. `diag_inverse`: block i is the given inverse of the window's diagonal block i.
All inputs are finite; a program needn't handle non-finite values.
Results may differ from a plain program's by a relative error of at most 0.0003.
Values sent between devices are 32-bit elements; how exact they have to be, the bound alone decides.
No kernel may reach another device: no remote copies, remote signals or barrier semaphores. Data moves between devices by JAX's collectives and lax.ppermute only.
A program may use at most 128 MiB of HBM per device.

v0:
```python
import jax
import jax.numpy as jnp
from jax import lax
from jax.sharding import PartitionSpec as P


def sent_to_all(value, axis):
    copies = jnp.broadcast_to(value, (lax.axis_size(axis), *value.shape))
    return lax.all_to_all(copies, axis, split_axis=0, concat_axis=0, tiled=True)


def taken_together(value, axis):
    return sent_to_all(value, axis).sum(axis=0)


def in_blocks(value, dim, peers):
    shape = value.shape
    tiles = value.reshape(*shape[:dim], peers, shape[dim] // peers, *shape[dim + 1 :])
    return jnp.moveaxis(tiles, dim, 0)


def sum_at_owner(value, axis, dim):
    peers = lax.axis_size(axis)
    tiles = lax.all_to_all(in_blocks(value, dim, peers), axis, 0, 0, tiled=True)
    return jnp.sum(tiles, axis=0)


def joined_along(tiles, dim):
    tiles = jnp.moveaxis(tiles, 0, dim)
    shape = tiles.shape
    return tiles.reshape(*shape[:dim], shape[dim] * shape[dim + 1], *shape[dim + 2 :])


def gathered_copies(value, axis, dim):
    return joined_along(sent_to_all(value, axis), dim)


def exact_dot(left, right):
    return jnp.dot(left, right, precision=lax.Precision.HIGHEST, preferred_element_type=jnp.float32)


def sweep_subdomain(field, radial_nu, tangent_nu, stride_value):
    cell_index = jnp.arange(field.shape[0], dtype=jnp.int32)[:, None]
    radial_prev = jnp.where(cell_index >= stride_value, jnp.roll(field, stride_value, axis=0), 0.0)
    tangent_prev = jnp.where(cell_index >= 1, jnp.roll(field, 1, axis=0), 0.0)
    return radial_nu * (field - radial_prev) + tangent_nu * (field - tangent_prev)


def column_total(partial_rows):
    return taken_together(partial_rows, "col")


def pair_index(later_block, earlier_block):
    return later_block * (later_block - 1) // 2 + earlier_block


def fold_step(tiles, carry, arrived):
    return carry - jnp.einsum(
        "mtc,cr->mtr",
        tiles,
        arrived,
        precision=lax.Precision.HIGHEST,
        preferred_element_type=jnp.float32,
    )


def per_device(
    sub_field, reluctivity, stride, counts, source_cell, target_row, lower_tiles, diag_inverse
):
    blocks = diag_inverse.shape[0]
    tile_rows = lower_tiles.shape[1]
    rotor = sub_field.shape[1]
    swept = sweep_subdomain(sub_field, reluctivity[0], reluctivity[1], stride[0])
    picked = swept[source_cell[0]]
    slots = source_cell.shape[2]
    live = jnp.arange(slots, dtype=jnp.int32)[None, :] < counts[0][:, None]
    picked = jnp.where(live[:, :, None], picked, 0.0)
    received = lax.all_to_all(picked, "row", split_axis=0, concat_axis=0, tiled=True)
    targets = target_row[0, 0].reshape(-1)
    interface = (
        jnp.zeros((blocks * tile_rows, rotor), jnp.float32)
        .at[targets]
        .add(received.reshape(-1, rotor))
    )
    interface = interface.reshape(blocks, tile_rows, rotor)
    pieces = []
    pending = [interface[row_block] for row_block in range(blocks)]
    for row_block in range(blocks):
        residual = column_total(pending[row_block])
        piece = sum_at_owner(exact_dot(diag_inverse[row_block], residual), "row", 0)
        pieces.append(piece)
        later = list(range(row_block + 1, blocks))
        if later:
            tiles = jnp.stack([lower_tiles[pair_index(target, row_block)] for target in later])
            started = jnp.stack([pending[target] for target in later])
            updated = fold_step(tiles, started, gathered_copies(piece, "row", 0))
            for position, target in enumerate(later):
                pending[target] = updated[position]
    return jnp.stack(pieces)[:, None]


def solution(mesh):
    placed = (
        P(("row", "col"), None),
        P(None, ("row", "col"), None),
        P(("row", "col")),
        P(("row", "col"), None),
        P(("row", "col"), None, None),
        P("row", "col", None, None),
        P(None, "row", "col"),
        P(None, "col", "row"),
    )
    return jax.shard_map(
        per_device,
        mesh=mesh,
        in_specs=placed,
        out_specs=P(None, "col", "row", None),
        check_vma=False,
    )
```

profile of v0, /device:TPU:1, one launch (start us, length us, event | category | flops | bytes accessed | tf_op | source)
XLA Modules:
  0.0 415.2 jit_solution(9468775093965223709)
XLA Ops:
  9.2 8.4 %all-to-all-start = ((f32[16,32,128]{2,1,0:T(8,128)}), f32[16,32,128]{2,1,0:T(8,128)S(1)}, u32[]{:S(2)}, u32[]{:S(2)}) async-start(f32[16,32,128]{2,1,0:T(8,128)} %broadcast_select_fusion), calls=%async_computation | async-start | bytes 524288 | tf_op jit(solution)/shard_map/all_to_all | solution.py:78
  36.4 5.5 %all-to-all-start.1 = ((f32[8,256,128]{2,1,0:T(8,128)}), f32[8,256,128]{2,1,0:T(8,128)}, u32[]{:S(2)}, u32[]{:S(2)}) async-start(f32[8,256,128]{2,1,0:T(8,128)} %broadcast_in_dim.89), calls=%async_computation.1 | async-start | bytes 2097152 | tf_op jit(solution)/shard_map/all_to_all | solution.py:9
  61.0 6.9 %all-to-all-start.2 = ((f32[16,32,128]{2,1,0:T(8,128)}), f32[16,32,128]{2,1,0:T(8,128)S(1)}, u32[]{:S(2)}, u32[]{:S(2)}) async-start(f32[16,32,128]{2,1,0:T(8,128)} %bitcast.182), calls=%async_computation.2 | async-start | bytes 524288 | tf_op jit(solution)/shard_map/all_to_all | solution.py:24
  93.8 21.6 %all_to_all.120 = f32[8,256,128]{2,1,0:T(8,128)} all-to-all(f32[8,256,128]{2,1,0:T(8,128)S(1)} %broadcast_in_dim.91), channel_id=1, replica_groups=mesh['row'=16,'col'=8] {'col'}, dimensions={0} | all-to-all | bytes 2097152 | tf_op jit(solution)/shard_map/all_to_all | solution.py:9
  119.2 11.0 %all_to_all.121 = f32[16,32,128]{2,1,0:T(8,128)S(1)} all-to-all(f32[16,32,128]{2,1,0:T(8,128)} %bitcast.183), channel_id=1, replica_groups=mesh['row'=16,'col'=8] {'row'}, dimensions={0} | all-to-all | bytes 524288 | tf_op jit(solution)/shard_map/all_to_all | solution.py:24
  130.3 10.5 %all_to_all.122 = f32[16,32,128]{2,1,0:T(8,128)S(1)} all-to-all(f32[16,32,128]{2,1,0:T(8,128)S(1)} %broadcast_in_dim.92), channel_id=1, replica_groups=mesh['row'=16,'col'=8] {'row'}, dimensions={0} | all-to-all | bytes 524288 | tf_op jit(solution)/shard_map/all_to_all | solution.py:9
  145.6 20.9 %all_to_all.123 = f32[8,256,128]{2,1,0:T(8,128)S(1)} all-to-all(f32[8,256,128]{2,1,0:T(8,128)S(1)} %broadcast_in_dim.93), channel_id=1, replica_groups=mesh['row'=16,'col'=8] {'col'}, dimensions={0} | all-to-all | bytes 2097152 | tf_op jit(solution)/shard_map/all_to_all | solution.py:9
  168.5 10.3 %all_to_all.124 = f32[16,32,128]{2,1,0:T(8,128)S(1)} all-to-all(f32[16,32,128]{2,1,0:T(8,128)S(1)} %bitcast.184), channel_id=1, replica_groups=mesh['row'=16,'col'=8] {'row'}, dimensions={0} | all-to-all | bytes 524288 | tf_op jit(solution)/shard_map/all_to_all | solution.py:24
  178.8 10.3 %all_to_all.125 = f32[16,32,128]{2,1,0:T(8,128)S(1)} all-to-all(f32[16,32,128]{2,1,0:T(8,128)S(1)} %broadcast_in_dim.94), channel_id=1, replica_groups=mesh['row'=16,'col'=8] {'row'}, dimensions={0} | all-to-all | bytes 524288 | tf_op jit(solution)/shard_map/all_to_all | solution.py:9
  193.3 21.2 %all_to_all.126 = f32[8,256,128]{2,1,0:T(8,128)S(1)} all-to-all(f32[8,256,128]{2,1,0:T(8,128)S(1)} %broadcast_in_dim.95), channel_id=1, replica_groups=mesh['row'=16,'col'=8] {'col'}, dimensions={0} | all-to-all | bytes 2097152 | tf_op jit(solution)/shard_map/all_to_all | solution.py:9
  216.4 10.3 %all_to_all.127 = f32[16,32,128]{2,1,0:T(8,128)S(1)} all-to-all(f32[16,32,128]{2,1,0:T(8,128)S(1)} %bitcast.185), channel_id=1, replica_groups=mesh['row'=16,'col'=8] {'row'}, dimensions={0} | all-to-all | bytes 524288 | tf_op jit(solution)/shard_map/all_to_all | solution.py:24
  227.4 10.3 %all_to_all.128 = f32[16,32,128]{2,1,0:T(8,128)S(1)} all-to-all(f32[16,32,128]{2,1,0:T(8,128)S(1)} %broadcast_in_dim.96), channel_id=1, replica_groups=mesh['row'=16,'col'=8] {'row'}, dimensions={0} | all-to-all | bytes 524288 | tf_op jit(solution)/shard_map/all_to_all | solution.py:9
  241.4 21.2 %all_to_all.129 = f32[8,256,128]{2,1,0:T(8,128)S(1)} all-to-all(f32[8,256,128]{2,1,0:T(8,128)S(1)} %broadcast_in_dim.97), channel_id=1, replica_groups=mesh['row'=16,'col'=8] {'col'}, dimensions={0} | all-to-all | bytes 2097152 | tf_op jit(solution)/shard_map/all_to_all | solution.py:9
  264.6 10.3 %all_to_all.130 = f32[16,32,128]{2,1,0:T(8,128)S(1)} all-to-all(f32[16,32,128]{2,1,0:T(8,128)S(1)} %bitcast.186), channel_id=1, replica_groups=mesh['row'=16,'col'=8] {'row'}, dimensions={0} | all-to-all | bytes 524288 | tf_op jit(solution)/shard_map/all_to_all | solution.py:24
  275.0 10.3 %all_to_all.131 = f32[16,32,128]{2,1,0:T(8,128)S(1)} all-to-all(f32[16,32,128]{2,1,0:T(8,128)S(1)} %broadcast_in_dim.98), channel_id=1, replica_groups=mesh['row'=16,'col'=8] {'row'}, dimensions={0} | all-to-all | bytes 524288 | tf_op jit(solution)/shard_map/all_to_all | solution.py:9
  286.8 21.2 %all_to_all.132 = f32[8,256,128]{2,1,0:T(8,128)S(1)} all-to-all(f32[8,256,128]{2,1,0:T(8,128)S(1)} %broadcast_in_dim.99), channel_id=1, replica_groups=mesh['row'=16,'col'=8] {'col'}, dimensions={0} | all-to-all | bytes 2097152 | tf_op jit(solution)/shard_map/all_to_all | solution.py:9
  310.0 10.3 %all_to_all.133 = f32[16,32,128]{2,1,0:T(8,128)S(1)} all-to-all(f32[16,32,128]{2,1,0:T(8,128)S(1)} %bitcast.187), channel_id=1, replica_groups=mesh['row'=16,'col'=8] {'row'}, dimensions={0} | all-to-all | bytes 524288 | tf_op jit(solution)/shard_map/all_to_all | solution.py:24
  320.4 10.3 %all_to_all.134 = f32[16,32,128]{2,1,0:T(8,128)S(1)} all-to-all(f32[16,32,128]{2,1,0:T(8,128)S(1)} %broadcast_in_dim.100), channel_id=1, replica_groups=mesh['row'=16,'col'=8] {'row'}, dimensions={0} | all-to-all | bytes 524288 | tf_op jit(solution)/shard_map/all_to_all | solution.py:9
  331.8 21.1 %all_to_all.135 = f32[8,256,128]{2,1,0:T(8,128)S(1)} all-to-all(f32[8,256,128]{2,1,0:T(8,128)S(1)} %broadcast_in_dim.101), channel_id=1, replica_groups=mesh['row'=16,'col'=8] {'col'}, dimensions={0} | all-to-all | bytes 2097152 | tf_op jit(solution)/shard_map/all_to_all | solution.py:9
  354.9 10.4 %all_to_all.136 = f32[16,32,128]{2,1,0:T(8,128)S(1)} all-to-all(f32[16,32,128]{2,1,0:T(8,128)S(1)} %bitcast.188), channel_id=1, replica_groups=mesh['row'=16,'col'=8] {'row'}, dimensions={0} | all-to-all | bytes 524288 | tf_op jit(solution)/shard_map/all_to_all | solution.py:24
  365.3 10.3 %all_to_all.137 = f32[16,32,128]{2,1,0:T(8,128)S(1)} all-to-all(f32[16,32,128]{2,1,0:T(8,128)S(1)} %broadcast_in_dim.102), channel_id=1, replica_groups=mesh['row'=16,'col'=8] {'row'}, dimensions={0} | all-to-all | bytes 524288 | tf_op jit(solution)/shard_map/all_to_all | solution.py:9
  378.3 7.1 %all-to-all-start.22 = ((f32[8,256,128]{2,1,0:T(8,128)}), f32[8,256,128]{2,1,0:T(8,128)S(1)}, u32[]{:S(2)}, u32[]{:S(2)}) async-start(f32[8,256,128]{2,1,0:T(8,128)} %broadcast_in_dim.103), calls=%async_computation.22 | async-start | bytes 2097152 | tf_op jit(solution)/shard_map/all_to_all | solution.py:9
  385.5 15.0 %all-to-all-done.22 = f32[8,256,128]{2,1,0:T(8,128)S(1)} async-done(((f32[8,256,128]{2,1,0:T(8,128)}), f32[8,256,128]{2,1,0:T(8,128)S(1)}, u32[]{:S(2)}, u32[]{:S(2)}) %all-to-all-start.22) | async-done | bytes 1048608 | tf_op jit(solution)/shard_map/all_to_all | solution.py:9
  406.7 7.8 %all-to-all-done.23 = f32[16,32,128]{2,1,0:T(8,128)S(1)} async-done(((f32[16,32,128]{2,1,0:T(8,128)}), f32[16,32,128]{2,1,0:T(8,128)S(1)}, u32[]{:S(2)}, u32[]{:S(2)}) %all-to-all-start.23) | async-done | bytes 262176 | tf_op jit(solution)/shard_map/all_to_all | solution.py:24
  (147 shorter events, 111.2 us)
Async XLA Ops:
  9.2 21.9 %all-to-all-start = ((f32[16,32,128]{2,1,0:T(8,128)}), f32[16,32,128]{2,1,0:T(8,128)S(1)}, u32[]{:S(2)}, u32[]{:S(2)}) async-start(f32[16,32,128]{2,1,0:T(8,128)} %broadcast_select_fusion), calls=%async_computation | async-start | bytes 524288 | tf_op jit(solution)/shard_map/all_to_all | solution.py:78
  25.9 5.1 %copy-start.21 = (s32[1,1,16,32]{3,2,1,0:T(8,128)S(1)}, s32[1,1,16,32]{3,2,1,0:T(8,128)}, u32[]{:S(2)}) copy-start(s32[1,1,16,32]{3,2,1,0:T(8,128)} %param.13) | copy-start | bytes 6148
  36.4 20.7 %all-to-all-start.1 = ((f32[8,256,128]{2,1,0:T(8,128)}), f32[8,256,128]{2,1,0:T(8,128)}, u32[]{:S(2)}, u32[]{:S(2)}) async-start(f32[8,256,128]{2,1,0:T(8,128)} %broadcast_in_dim.89), calls=%async_computation.1 | async-start | bytes 2097152 | tf_op jit(solution)/shard_map/all_to_all | solution.py:9
  61.0 14.5 %all-to-all-start.2 = ((f32[16,32,128]{2,1,0:T(8,128)}), f32[16,32,128]{2,1,0:T(8,128)S(1)}, u32[]{:S(2)}, u32[]{:S(2)}) async-start(f32[16,32,128]{2,1,0:T(8,128)} %bitcast.182), calls=%async_computation.2 | async-start | bytes 524288 | tf_op jit(solution)/shard_map/all_to_all | solution.py:24
  76.3 11.0 %all-to-all-start.3 = ((f32[16,32,128]{2,1,0:T(8,128)}), f32[16,32,128]{2,1,0:T(8,128)S(1)}, u32[]{:S(2)}, u32[]{:S(2)}) async-start(f32[16,32,128]{2,1,0:T(8,128)} %broadcast_in_dim.90), calls=%async_computation.3 | async-start | bytes 524288 | tf_op jit(solution)/shard_map/all_to_all | solution.py:9
  130.3 15.3 %copy-start.13 = (f32[32,128]{1,0:T(8,128)}, f32[32,128]{1,0:T(8,128)S(1)}, u32[]{:S(2)}) copy-start(f32[32,128]{1,0:T(8,128)S(1)} %reduce_sum.147) | copy-start | bytes 49156
  145.6 43.6 %copy-start.2 = (f32[6,256,128]{2,1,0:T(8,128)S(1)}, f32[6,256,128]{2,1,0:T(8,128)}, u32[]{:S(2)}) copy-start(f32[6,256,128]{2,1,0:T(8,128)} %copy-done.1) | copy-start | bytes 2359300
  178.8 14.3 %copy-start.15 = (f32[32,128]{1,0:T(8,128)}, f32[32,128]{1,0:T(8,128)S(1)}, u32[]{:S(2)}) copy-start(f32[32,128]{1,0:T(8,128)S(1)} %reduce_sum.149) | copy-start | bytes 49156
  193.2 44.5 %copy-start.8 = (f32[1,256,512]{2,1,0:T(8,128)S(1)}, f32[1,256,512]{2,1,0:T(8,128)}, u32[]{:S(2)}) copy-start(f32[1,256,512]{2,1,0:T(8,128)} %get-tuple-element.9) | copy-start | bytes 1572868
  193.2 44.5 %copy-start.9 = (f32[1,256,512]{2,1,0:T(8,128)S(1)}, f32[1,256,512]{2,1,0:T(8,128)}, u32[]{:S(2)}) copy-start(f32[1,256,512]{2,1,0:T(8,128)} %get-tuple-element.10) | copy-start | bytes 1572868
  193.2 44.4 %copy-start.10 = (f32[1,256,512]{2,1,0:T(8,128)S(1)}, f32[1,256,512]{2,1,0:T(8,128)}, u32[]{:S(2)}) copy-start(f32[1,256,512]{2,1,0:T(8,128)} %get-tuple-element.11) | copy-start | bytes 1572868
  241.4 43.9 %copy-start.5 = (f32[1,256,512]{2,1,0:T(8,128)S(1)}, f32[1,256,512]{2,1,0:T(8,128)}, u32[]{:S(2)}) copy-start(f32[1,256,512]{2,1,0:T(8,128)} %get-tuple-element.6) | copy-start | bytes 1572868
  241.4 43.9 %copy-start.6 = (f32[1,256,512]{2,1,0:T(8,128)S(1)}, f32[1,256,512]{2,1,0:T(8,128)}, u32[]{:S(2)}) copy-start(f32[1,256,512]{2,1,0:T(8,128)} %get-tuple-element.7) | copy-start | bytes 1572868
  241.4 43.9 %copy-start.7 = (f32[1,256,512]{2,1,0:T(8,128)S(1)}, f32[1,256,512]{2,1,0:T(8,128)}, u32[]{:S(2)}) copy-start(f32[1,256,512]{2,1,0:T(8,128)} %get-tuple-element.8) | copy-start | bytes 1572868
  241.4 43.9 %copy-start.12 = (f32[4,256,128]{2,1,0:T(8,128)S(1)}, f32[4,256,128]{2,1,0:T(8,128)}, u32[]{:S(2)}) copy-start(f32[4,256,128]{2,1,0:T(8,128)} %copy-done.11) | copy-start | bytes 1572868
  274.9 10.4 %copy-start.19 = (f32[32,128]{1,0:T(8,128)}, f32[32,128]{1,0:T(8,128)S(1)}, u32[]{:S(2)}) copy-start(f32[32,128]{1,0:T(8,128)S(1)} %reduce_sum.153) | copy-start | bytes 49156
  286.8 43.9 %copy-start.3 = (f32[1,256,512]{2,1,0:T(8,128)S(1)}, f32[1,256,512]{2,1,0:T(8,128)}, u32[]{:S(2)}) copy-start(f32[1,256,512]{2,1,0:T(8,128)} %get-tuple-element.5) | copy-start | bytes 1572868
  286.8 43.9 %copy-start.4 = (f32[1,256,512]{2,1,0:T(8,128)S(1)}, f32[1,256,512]{2,1,0:T(8,128)}, u32[]{:S(2)}) copy-start(f32[1,256,512]{2,1,0:T(8,128)} %get-tuple-element.16) | copy-start | bytes 1572868
  354.7 30.7 %copy-start.14 = (f32[32,128]{1,0:T(8,128)S(1)}, f32[32,128]{1,0:T(8,128)}, u32[]{:S(2)}) copy-start(f32[32,128]{1,0:T(8,128)} %copy-done.13) | copy-start | bytes 49156
  354.7 30.7 %copy-start.16 = (f32[32,128]{1,0:T(8,128)S(1)}, f32[32,128]{1,0:T(8,128)}, u32[]{:S(2)}) copy-start(f32[32,128]{1,0:T(8,128)} %copy-done.15) | copy-start | bytes 49156
  354.8 30.6 %copy-start.18 = (f32[32,128]{1,0:T(8,128)S(1)}, f32[32,128]{1,0:T(8,128)}, u32[]{:S(2)}) copy-start(f32[32,128]{1,0:T(8,128)} %copy-done.17) | copy-start | bytes 49156
  354.8 30.6 %copy-start.20 = (f32[32,128]{1,0:T(8,128)S(1)}, f32[32,128]{1,0:T(8,128)}, u32[]{:S(2)}) copy-start(f32[32,128]{1,0:T(8,128)} %copy-done.19) | copy-start | bytes 49156
  378.3 22.2 %all-to-all-start.22 = ((f32[8,256,128]{2,1,0:T(8,128)}), f32[8,256,128]{2,1,0:T(8,128)S(1)}, u32[]{:S(2)}, u32[]{:S(2)}) async-start(f32[8,256,128]{2,1,0:T(8,128)} %broadcast_in_dim.103), calls=%async_computation.22 | async-start | bytes 2097152 | tf_op jit(solution)/shard_map/all_to_all | solution.py:9
  403.2 11.4 %all-to-all-start.23 = ((f32[16,32,128]{2,1,0:T(8,128)}), f32[16,32,128]{2,1,0:T(8,128)S(1)}, u32[]{:S(2)}, u32[]{:S(2)}) async-start(f32[16,32,128]{2,1,0:T(8,128)} %bitcast.68), calls=%async_computation.23 | async-start | bytes 524288 | tf_op jit(solution)/shard_map/all_to_all | solution.py:24
  (5 other events, 3.9 us)
where the time goes:
time: 418 us; the launch traced here: 415 us
  blocking collectives  252 us (60%)
  local copies, waits for them, and re-layouts  43 us (10%)
  waiting for transfers between devices  36.9 us (9%)
  starting transfers between devices  34.9 us (8%)
  matrix products  34.1 us (8%)
  other arithmetic  13 us (3%)
    all_to_all x12, blocking collectives, sent_to_all(): return lax.all_to_all(copies, axis, split_axis=0, concat_axis=0, tiled=True)  189 us
    all_to_all x6, blocking collectives, sum_at_owner(): tiles = lax.all_to_all(in_blocks(value, dim, peers), axis, 0, 0, tiled=True)  62.6 us
    unnamed x65, local copies, waits for them, and re-layouts  26.7 us
    all_to_all x3, waiting for transfers between devices, sent_to_all(): return lax.all_to_all(copies, axis, split_axis=0, concat_axis=0, tiled=True)  24.7 us
    dot_general x7, matrix products, fold_step(): jnp.einsum('mtc,cr->mtr', tiles, arrived, precision=lax.Precision.HIGHEST...  20 us
    all_to_all x3, starting transfers between devices, sent_to_all(): return lax.all_to_all(copies, axis, split_axis=0, concat_axis=0, tiled=True)  16.1 us
    dot_general x8, matrix products, exact_dot(): jnp.dot(left, right, precision=lax.Precision.HIGHEST, preferred_element_t...  14.1 us
    all_to_all x2, waiting for transfers between devices, sum_at_owner(): tiles = lax.all_to_all(in_blocks(value, dim, peers), axis, 0, 0, tiled=True)  12.3 us
  transfers between devices with their start and end apart: 6, of which 5 were waited for; matrix products, arithmetic and copies ran while one was open for 7% of the time, Pallas kernels for 0%

commit v1 on v0

v1 whole, which is shorter than its diff:
```python
import jax
import jax.numpy as jnp
from jax import lax
from jax.sharding import PartitionSpec as P


def product(left, right, precision=lax.Precision.HIGH):
    return jnp.dot(left, right, precision=precision, preferred_element_type=jnp.float32)


def sweep_subdomain(field, radial_nu, tangent_nu, stride_value):
    cell_index = jnp.arange(field.shape[0], dtype=jnp.int32)[:, None]
    radial_prev = jnp.where(cell_index >= stride_value, jnp.roll(field, stride_value, axis=0), 0.0)
    tangent_prev = jnp.where(cell_index >= 1, jnp.roll(field, 1, axis=0), 0.0)
    return radial_nu * (field - radial_prev) + tangent_nu * (field - tangent_prev)


def pair_index(later_block, earlier_block):
    return later_block * (later_block - 1) // 2 + earlier_block


def other_core(value):
    peers = lax.axis_size("col")
    return lax.ppermute(value, "col", [(i, i ^ 1) for i in range(peers)])


def total_along_x(value):
    peers = lax.axis_size("col")
    arrived = [
        lax.ppermute(value, "col", [(i, (i + hop) % peers) for i in range(peers)])
        for hop in range(2, peers, 2)
    ]
    for part in arrived:
        value = value + part
    return value


def column_total(partial_rows):
    core = lax.axis_index("col") % 2
    half = partial_rows.shape[0] // 2
    low, high = partial_rows[:half], partial_rows[half:]
    mine = jnp.where(core == 0, low, high)
    theirs = jnp.where(core == 0, high, low)
    mine = total_along_x(mine + other_core(theirs))
    theirs = other_core(mine)
    return jnp.concatenate(
        [jnp.where(core == 0, mine, theirs), jnp.where(core == 0, theirs, mine)], axis=0
    )


def row_share(partial_share):
    peers = lax.axis_size("row")
    tiles = partial_share.reshape(peers, -1, partial_share.shape[1])
    return jnp.sum(lax.all_to_all(tiles, "row", 0, 0, tiled=True), axis=0)


def row_gather(piece):
    peers = lax.axis_size("row")
    copies = jnp.broadcast_to(piece, (peers, *piece.shape))
    return lax.all_to_all(copies, "row", 0, 0, tiled=True).reshape(-1, piece.shape[1])


def per_device(
    sub_field, reluctivity, stride, counts, source_cell, target_row, lower_tiles, diag_inverse
):
    blocks = diag_inverse.shape[0]
    tile_rows = lower_tiles.shape[1]
    rotor = sub_field.shape[1]
    swept = sweep_subdomain(sub_field, reluctivity[0], reluctivity[1], stride[0])
    picked = swept[source_cell[0]]
    slots = source_cell.shape[2]
    live = jnp.arange(slots, dtype=jnp.int32)[None, :] < counts[0][:, None]
    picked = jnp.where(live[:, :, None], picked, 0.0)
    received = lax.all_to_all(picked, "row", split_axis=0, concat_axis=0, tiled=True)
    received = received.reshape(-1, rotor)
    targets = target_row[0, 0].reshape(1, -1)

    def interface(block):
        rows = block * tile_rows + jnp.arange(tile_rows, dtype=jnp.int32)[:, None]
        return product(
            (rows == targets).astype(jnp.float32), received, lax.Precision.HIGHEST
        )

    shares = []
    pieces = []
    pending = interface(0)
    for block in range(blocks):
        residual = column_total(pending)
        piece = row_share(product(diag_inverse[block], residual))
        pieces.append(piece)
        if block + 1 < blocks:
            started = interface(block + 1)
            for earlier in range(block):
                started = started - product(
                    lower_tiles[pair_index(block + 1, earlier)], shares[earlier]
                )
            shares.append(row_gather(piece))
            pending = started - product(lower_tiles[pair_index(block + 1, block)], shares[block])
    return jnp.stack(pieces)[:, None]


def solution(mesh):
    placed = (
        P(("row", "col"), None),
        P(None, ("row", "col"), None),
        P(("row", "col")),
        P(("row", "col"), None),
        P(("row", "col"), None, None),
        P("row", "col", None, None),
        P(None, "row", "col"),
        P(None, "col", "row"),
    )
    return jax.shard_map(
        per_device,
        mesh=mesh,
        in_specs=placed,
        out_specs=P(None, "col", "row", None),
        check_vma=False,
    )
```

time: 418 us -> 342 us (0.82)
  blocking collectives: 252 us -> 0 us
  waiting for transfers between devices: 36.9 us -> 155 us
  starting transfers between devices: 34.9 us -> 105 us
  local copies, waits for them, and re-layouts: 43 us -> 14.9 us
  matrix products: 34.1 us -> 54.9 us
  other arithmetic: 13 us -> 7.04 us
    all_to_all x18 -> x0, blocking collectives: 252 us -> none  [the longest x12 189 us: sent_to_all(): return lax.all_to_all(copies, axis, split_axis=0, concat_axis=0, tiled=True)]
    all_to_all x5 -> x15, waiting for transfers between devices: 36.9 us -> 103 us  [the longest x8 59.7 us: row_share(): return jnp.sum(lax.all_to_all(tiles, 'row', 0, 0, tiled=True), axis=0)]
    ppermute x0 -> x40, waiting for transfers between devices: none -> 45 us  [the longest x24 37.2 us: total_along_x(): lax.ppermute(value, 'col', [(i, (i + hop) % peers) for i in range(peers)])]
    ppermute x0 -> x40, starting transfers between devices: none -> 43.6 us  [the longest x16 27.1 us: other_core(): return lax.ppermute(value, 'col', [(i, i ^ 1) for i in range(peers)])]
    all_to_all x5 -> x15, starting transfers between devices: 26.5 us -> 53 us  [the longest x8 28.2 us: row_share(): return jnp.sum(lax.all_to_all(tiles, 'row', 0, 0, tiled=True), axis=0)]
    unnamed x65 -> x9, local copies, waits for them, and re-layouts: 26.7 us -> 0.67 us
    dot_general x15 -> x44, matrix products: 34.1 us -> 54.9 us  [product(): jnp.dot(left, right, precision=precision, preferred_element_type=jnp.floa...]
    all_to_all x1, waiting for transfers between devices: 0.01 us -> 6.76 us  [per_device(): lax.all_to_all(picked, 'row', split_axis=0, concat_axis=0, tiled=True)]
  transfers between devices with their start and end apart: 6 -> 56, of which waited for: 5 -> 50; matrix products, arithmetic and copies ran while one was open for 7% -> 10% of each run, Pallas kernels for 0% -> 0%
where the time goes in v1:
time: 342 us; the launch traced here: 339 us
  waiting for transfers between devices  155 us (45%)
  starting transfers between devices  105 us (31%)
  matrix products  54.9 us (16%)
  local copies, waits for them, and re-layouts  14.9 us (4%)
  other arithmetic  7.04 us (2%)
    all_to_all x8, waiting for transfers between devices, row_share(): return jnp.sum(lax.all_to_all(tiles, 'row', 0, 0, tiled=True), axis=0)  59.7 us
    dot_general x44, matrix products, product(): jnp.dot(left, right, precision=precision, preferred_element_type=jnp.floa...  54.9 us
    all_to_all x7, waiting for transfers between devices, row_gather(): lax.all_to_all(copies, 'row', 0, 0, tiled=True).reshape(-1, piece.shape[1])  43.7 us
    ppermute x24, waiting for transfers between devices, total_along_x(): lax.ppermute(value, 'col', [(i, (i + hop) % peers) for i in range(peers)])  37.2 us
    all_to_all x8, starting transfers between devices, row_share(): return jnp.sum(lax.all_to_all(tiles, 'row', 0, 0, tiled=True), axis=0)  28.2 us
    ppermute x16, starting transfers between devices, other_core(): return lax.ppermute(value, 'col', [(i, i ^ 1) for i in range(peers)])  27.1 us
    all_to_all x7, starting transfers between devices, row_gather(): lax.all_to_all(copies, 'row', 0, 0, tiled=True).reshape(-1, piece.shape[1])  24.7 us
    ppermute x24, starting transfers between devices, total_along_x(): lax.ppermute(value, 'col', [(i, (i + hop) % peers) for i in range(peers)])  16.5 us
  transfers between devices with their start and end apart: 56, of which 50 were waited for; matrix products, arithmetic and copies ran while one was open for 10% of the time, Pallas kernels for 0%

profile of v1, /device:TPU:1, one launch (start us, length us, event | category | flops | bytes accessed | tf_op | source)
XLA Modules:
  0.0 338.6 jit_solution(1120329118598924246)
XLA Ops:
  2.9 4.1 %fusion.32 = f32[2048,128]{1,0:T(8,128)S(1)} fusion(f32[2048,128]{1,0:T(8,128)} %param.8, s32[]{:T(128)S(6)} %select_n.189, f32[2047,128]{1,0:T(8,128)} %bitcast.353, f32[1,128]{1,0:T(1,128)S(1)} %slice.172, f32[2,2048,128]{2,1,0:T(8,128)} %param.9, pred[2048]{0:T(1024)(128)(4,1)S(1)} %get-tuple-element.21, pred[2048]{0:T(1024)(128)(4,1)S(1)} %get-tuple-element.22), kind=kLoop, calls=%fused_computation.71 | loop fusion | flops 2359296 | bytes 5246980 | tf_op jit(solution)/shard_map/add | solution.py:15
  8.9 8.6 %all-to-all-start = ((f32[16,32,128]{2,1,0:T(8,128)}), f32[16,32,128]{2,1,0:T(8,128)S(1)}, u32[]{:S(2)}, u32[]{:S(2)}) async-start(f32[16,32,128]{2,1,0:T(8,128)} %broadcast_select_fusion), calls=%async_computation | async-start | bytes 524288 | tf_op jit(solution)/shard_map/all_to_all | solution.py:74
  18.4 6.8 %all-to-all-done = f32[16,32,128]{2,1,0:T(8,128)S(1)} async-done(((f32[16,32,128]{2,1,0:T(8,128)}), f32[16,32,128]{2,1,0:T(8,128)S(1)}, u32[]{:S(2)}, u32[]{:S(2)}) %all-to-all-start) | async-done | bytes 262176 | tf_op jit(solution)/shard_map/all_to_all | solution.py:74
  42.0 3.5 %all-to-all-start.1 = ((f32[16,32,128]{2,1,0:T(8,128)}), f32[16,32,128]{2,1,0:T(8,128)S(1)}, u32[]{:S(2)}, u32[]{:S(2)}) async-start(f32[16,32,128]{2,1,0:T(8,128)} %bitcast.9), calls=%async_computation.1 | async-start | bytes 524288 | tf_op jit(solution)/shard_map/all_to_all | solution.py:54
  45.6 8.4 %all-to-all-done.1 = f32[16,32,128]{2,1,0:T(8,128)S(1)} async-done(((f32[16,32,128]{2,1,0:T(8,128)}), f32[16,32,128]{2,1,0:T(8,128)S(1)}, u32[]{:S(2)}, u32[]{:S(2)}) %all-to-all-start.1) | async-done | bytes 262176 | tf_op jit(solution)/shard_map/all_to_all | solution.py:54
  54.7 3.5 %all-to-all-start.2 = ((f32[16,32,128]{2,1,0:T(8,128)}), f32[16,32,128]{2,1,0:T(8,128)S(1)}, u32[]{:S(2)}, u32[]{:S(2)}) async-start(f32[16,32,128]{2,1,0:T(8,128)} %broadcast_in_dim.71), calls=%async_computation.2 | async-start | bytes 524288 | tf_op jit(solution)/shard_map/all_to_all | solution.py:60
  58.6 7.1 %all-to-all-done.2 = f32[16,32,128]{2,1,0:T(8,128)S(1)} async-done(((f32[16,32,128]{2,1,0:T(8,128)}), f32[16,32,128]{2,1,0:T(8,128)S(1)}, u32[]{:S(2)}, u32[]{:S(2)}) %all-to-all-start.2) | async-done | bytes 262176 | tf_op jit(solution)/shard_map/all_to_all | solution.py:60
  81.6 3.5 %all-to-all-start.3 = ((f32[16,32,128]{2,1,0:T(8,128)}), f32[16,32,128]{2,1,0:T(8,128)S(1)}, u32[]{:S(2)}, u32[]{:S(2)}) async-start(f32[16,32,128]{2,1,0:T(8,128)} %bitcast.16), calls=%async_computation.3 | async-start | bytes 524288 | tf_op jit(solution)/shard_map/all_to_all | solution.py:54
  86.0 7.6 %all-to-all-done.3 = f32[16,32,128]{2,1,0:T(8,128)S(1)} async-done(((f32[16,32,128]{2,1,0:T(8,128)}), f32[16,32,128]{2,1,0:T(8,128)S(1)}, u32[]{:S(2)}, u32[]{:S(2)}) %all-to-all-start.3) | async-done | bytes 262176 | tf_op jit(solution)/shard_map/all_to_all | solution.py:54
  99.3 6.1 %all-to-all-done.4 = f32[16,32,128]{2,1,0:T(8,128)S(1)} async-done(((f32[16,32,128]{2,1,0:T(8,128)}), f32[16,32,128]{2,1,0:T(8,128)S(1)}, u32[]{:S(2)}, u32[]{:S(2)}) %all-to-all-start.4) | async-done | bytes 262176 | tf_op jit(solution)/shard_map/all_to_all | solution.py:60
  127.4 7.0 %all-to-all-done.5 = f32[16,32,128]{2,1,0:T(8,128)S(1)} async-done(((f32[16,32,128]{2,1,0:T(8,128)}), f32[16,32,128]{2,1,0:T(8,128)S(1)}, u32[]{:S(2)}, u32[]{:S(2)}) %all-to-all-start.5) | async-done | bytes 262176 | tf_op jit(solution)/shard_map/all_to_all | solution.py:54
  140.1 6.1 %all-to-all-done.6 = f32[16,32,128]{2,1,0:T(8,128)S(1)} async-done(((f32[16,32,128]{2,1,0:T(8,128)}), f32[16,32,128]{2,1,0:T(8,128)S(1)}, u32[]{:S(2)}, u32[]{:S(2)}) %all-to-all-start.6) | async-done | bytes 262176 | tf_op jit(solution)/shard_map/all_to_all | solution.py:60
  167.6 7.1 %all-to-all-done.7 = f32[16,32,128]{2,1,0:T(8,128)S(1)} async-done(((f32[16,32,128]{2,1,0:T(8,128)}), f32[16,32,128]{2,1,0:T(8,128)S(1)}, u32[]{:S(2)}, u32[]{:S(2)}) %all-to-all-start.7) | async-done | bytes 262176 | tf_op jit(solution)/shard_map/all_to_all | solution.py:54
  175.5 3.5 %all-to-all-start.8 = ((f32[16,32,128]{2,1,0:T(8,128)}), f32[16,32,128]{2,1,0:T(8,128)S(1)}, u32[]{:S(2)}, u32[]{:S(2)}) async-start(f32[16,32,128]{2,1,0:T(8,128)} %broadcast_in_dim.74), calls=%async_computation.8 | async-start | bytes 524288 | tf_op jit(solution)/shard_map/all_to_all | solution.py:60
  180.4 6.1 %all-to-all-done.8 = f32[16,32,128]{2,1,0:T(8,128)S(1)} async-done(((f32[16,32,128]{2,1,0:T(8,128)}), f32[16,32,128]{2,1,0:T(8,128)S(1)}, u32[]{:S(2)}, u32[]{:S(2)}) %all-to-all-start.8) | async-done | bytes 262176 | tf_op jit(solution)/shard_map/all_to_all | solution.py:60
  204.4 3.5 %all-to-all-start.9 = ((f32[16,32,128]{2,1,0:T(8,128)}), f32[16,32,128]{2,1,0:T(8,128)S(1)}, u32[]{:S(2)}, u32[]{:S(2)}) async-start(f32[16,32,128]{2,1,0:T(8,128)} %bitcast.49), calls=%async_computation.9 | async-start | bytes 524288 | tf_op jit(solution)/shard_map/all_to_all | solution.py:54
  209.3 7.1 %all-to-all-done.9 = f32[16,32,128]{2,1,0:T(8,128)S(1)} async-done(((f32[16,32,128]{2,1,0:T(8,128)}), f32[16,32,128]{2,1,0:T(8,128)S(1)}, u32[]{:S(2)}, u32[]{:S(2)}) %all-to-all-start.9) | async-done | bytes 262176 | tf_op jit(solution)/shard_map/all_to_all | solution.py:54
  222.1 6.1 %all-to-all-done.10 = f32[16,32,128]{2,1,0:T(8,128)S(1)} async-done(((f32[16,32,128]{2,1,0:T(8,128)}), f32[16,32,128]{2,1,0:T(8,128)S(1)}, u32[]{:S(2)}, u32[]{:S(2)}) %all-to-all-start.10) | async-done | bytes 262176 | tf_op jit(solution)/shard_map/all_to_all | solution.py:60
  249.6 7.1 %all-to-all-done.11 = f32[16,32,128]{2,1,0:T(8,128)S(1)} async-done(((f32[16,32,128]{2,1,0:T(8,128)}), f32[16,32,128]{2,1,0:T(8,128)S(1)}, u32[]{:S(2)}, u32[]{:S(2)}) %all-to-all-start.11) | async-done | bytes 262176 | tf_op jit(solution)/shard_map/all_to_all | solution.py:54
  262.4 6.1 %all-to-all-done.12 = f32[16,32,128]{2,1,0:T(8,128)S(1)} async-done(((f32[16,32,128]{2,1,0:T(8,128)}), f32[16,32,128]{2,1,0:T(8,128)S(1)}, u32[]{:S(2)}, u32[]{:S(2)}) %all-to-all-start.12) | async-done | bytes 262176 | tf_op jit(solution)/shard_map/all_to_all | solution.py:60
  291.2 7.1 %all-to-all-done.13 = f32[16,32,128]{2,1,0:T(8,128)S(1)} async-done(((f32[16,32,128]{2,1,0:T(8,128)}), f32[16,32,128]{2,1,0:T(8,128)S(1)}, u32[]{:S(2)}, u32[]{:S(2)}) %all-to-all-start.13) | async-done | bytes 262176 | tf_op jit(solution)/shard_map/all_to_all | solution.py:54
  304.1 6.1 %all-to-all-done.14 = f32[16,32,128]{2,1,0:T(8,128)S(1)} async-done(((f32[16,32,128]{2,1,0:T(8,128)}), f32[16,32,128]{2,1,0:T(8,128)S(1)}, u32[]{:S(2)}, u32[]{:S(2)}) %all-to-all-start.14) | async-done | bytes 262176 | tf_op jit(solution)/shard_map/all_to_all | solution.py:60
  326.0 3.5 %all-to-all-start.15 = ((f32[16,32,128]{2,1,0:T(8,128)}), f32[16,32,128]{2,1,0:T(8,128)S(1)}, u32[]{:S(2)}, u32[]{:S(2)}) async-start(f32[16,32,128]{2,1,0:T(8,128)} %bitcast.100), calls=%async_computation.15 | async-start | bytes 524288 | tf_op jit(solution)/shard_map/all_to_all | solution.py:54
  329.5 8.4 %all-to-all-done.15 = f32[16,32,128]{2,1,0:T(8,128)S(1)} async-done(((f32[16,32,128]{2,1,0:T(8,128)}), f32[16,32,128]{2,1,0:T(8,128)S(1)}, u32[]{:S(2)}, u32[]{:S(2)}) %all-to-all-start.15) | async-done | bytes 262176 | tf_op jit(solution)/shard_map/all_to_all | solution.py:54
  (214 shorter events, 193.0 us)
Async XLA Ops:
  8.9 16.2 %all-to-all-start = ((f32[16,32,128]{2,1,0:T(8,128)}), f32[16,32,128]{2,1,0:T(8,128)S(1)}, u32[]{:S(2)}, u32[]{:S(2)}) async-start(f32[16,32,128]{2,1,0:T(8,128)} %broadcast_select_fusion), calls=%async_computation | async-start | bytes 524288 | tf_op jit(solution)/shard_map/all_to_all | solution.py:74
  31.8 5.4 %collective-permute-start.1 = (f32[128,128]{1,0:T(8,128)S(1)}, f32[128,128]{1,0:T(8,128)S(1)}, u32[]{:S(2)}, u32[]{:S(2)}) collective-permute-start(f32[128,128]{1,0:T(8,128)S(1)} %select_add_fusion.7), channel_id=1, source_target_pairs={{0,2},{1,3},{2,4},{3,5},{4,6},{5,7},{6,0},{7,1},{8,10},{9,11},{10,... | collective-permute-start | bytes 196616 | tf_op jit(solution)/shard_map/ppermute | solution.py:30
  42.0 12.0 %all-to-all-start.1 = ((f32[16,32,128]{2,1,0:T(8,128)}), f32[16,32,128]{2,1,0:T(8,128)S(1)}, u32[]{:S(2)}, u32[]{:S(2)}) async-start(f32[16,32,128]{2,1,0:T(8,128)} %bitcast.9), calls=%async_computation.1 | async-start | bytes 524288 | tf_op jit(solution)/shard_map/all_to_all | solution.py:54
  54.7 11.1 %all-to-all-start.2 = ((f32[16,32,128]{2,1,0:T(8,128)}), f32[16,32,128]{2,1,0:T(8,128)S(1)}, u32[]{:S(2)}, u32[]{:S(2)}) async-start(f32[16,32,128]{2,1,0:T(8,128)} %broadcast_in_dim.71), calls=%async_computation.2 | async-start | bytes 524288 | tf_op jit(solution)/shard_map/all_to_all | solution.py:60
  71.4 6.0 %collective-permute-start.6 = (f32[128,128]{1,0:T(8,128)S(1)}, f32[128,128]{1,0:T(8,128)S(1)}, u32[]{:S(2)}, u32[]{:S(2)}) collective-permute-start(f32[128,128]{1,0:T(8,128)S(1)} %select_add_fusion.6), channel_id=1, source_target_pairs={{0,2},{1,3},{2,4},{3,5},{4,6},{5,7},{6,0},{7,1},{8,10},{9,11},{10,... | collective-permute-start | bytes 196616 | tf_op jit(solution)/shard_map/ppermute | solution.py:30
  81.6 12.0 %all-to-all-start.3 = ((f32[16,32,128]{2,1,0:T(8,128)}), f32[16,32,128]{2,1,0:T(8,128)S(1)}, u32[]{:S(2)}, u32[]{:S(2)}) async-start(f32[16,32,128]{2,1,0:T(8,128)} %bitcast.16), calls=%async_computation.3 | async-start | bytes 524288 | tf_op jit(solution)/shard_map/all_to_all | solution.py:54
  94.3 11.1 %all-to-all-start.4 = ((f32[16,32,128]{2,1,0:T(8,128)}), f32[16,32,128]{2,1,0:T(8,128)S(1)}, u32[]{:S(2)}, u32[]{:S(2)}) async-start(f32[16,32,128]{2,1,0:T(8,128)} %broadcast_in_dim.72), calls=%async_computation.4 | async-start | bytes 524288 | tf_op jit(solution)/shard_map/all_to_all | solution.py:60
  112.1 5.4 %collective-permute-start.11 = (f32[128,128]{1,0:T(8,128)S(1)}, f32[128,128]{1,0:T(8,128)S(1)}, u32[]{:S(2)}, u32[]{:S(2)}) collective-permute-start(f32[128,128]{1,0:T(8,128)S(1)} %select_add_fusion.5), channel_id=1, source_target_pairs={{0,2},{1,3},{2,4},{3,5},{4,6},{5,7},{6,0},{7,1},{8,10},{9,11},{10,... | collective-permute-start | bytes 196616 | tf_op jit(solution)/shard_map/ppermute | solution.py:30
  122.5 12.0 %all-to-all-start.5 = ((f32[16,32,128]{2,1,0:T(8,128)}), f32[16,32,128]{2,1,0:T(8,128)S(1)}, u32[]{:S(2)}, u32[]{:S(2)}) async-start(f32[16,32,128]{2,1,0:T(8,128)} %bitcast.25), calls=%async_computation.5 | async-start | bytes 524288 | tf_op jit(solution)/shard_map/all_to_all | solution.py:54
  135.2 11.1 %all-to-all-start.6 = ((f32[16,32,128]{2,1,0:T(8,128)}), f32[16,32,128]{2,1,0:T(8,128)S(1)}, u32[]{:S(2)}, u32[]{:S(2)}) async-start(f32[16,32,128]{2,1,0:T(8,128)} %broadcast_in_dim.73), calls=%async_computation.6 | async-start | bytes 524288 | tf_op jit(solution)/shard_map/all_to_all | solution.py:60
  152.0 6.0 %collective-permute-start.16 = (f32[128,128]{1,0:T(8,128)S(1)}, f32[128,128]{1,0:T(8,128)S(1)}, u32[]{:S(2)}, u32[]{:S(2)}) collective-permute-start(f32[128,128]{1,0:T(8,128)S(1)} %select_add_fusion.4), channel_id=1, source_target_pairs={{0,2},{1,3},{2,4},{3,5},{4,6},{5,7},{6,0},{7,1},{8,10},{9,11},{10,... | collective-permute-start | bytes 196616 | tf_op jit(solution)/shard_map/ppermute | solution.py:30
  162.7 12.1 %all-to-all-start.7 = ((f32[16,32,128]{2,1,0:T(8,128)}), f32[16,32,128]{2,1,0:T(8,128)S(1)}, u32[]{:S(2)}, u32[]{:S(2)}) async-start(f32[16,32,128]{2,1,0:T(8,128)} %bitcast.36), calls=%async_computation.7 | async-start | bytes 524288 | tf_op jit(solution)/shard_map/all_to_all | solution.py:54
  175.5 11.0 %all-to-all-start.8 = ((f32[16,32,128]{2,1,0:T(8,128)}), f32[16,32,128]{2,1,0:T(8,128)S(1)}, u32[]{:S(2)}, u32[]{:S(2)}) async-start(f32[16,32,128]{2,1,0:T(8,128)} %broadcast_in_dim.74), calls=%async_computation.8 | async-start | bytes 524288 | tf_op jit(solution)/shard_map/all_to_all | solution.py:60
  193.7 6.0 %collective-permute-start.21 = (f32[128,128]{1,0:T(8,128)S(1)}, f32[128,128]{1,0:T(8,128)S(1)}, u32[]{:S(2)}, u32[]{:S(2)}) collective-permute-start(f32[128,128]{1,0:T(8,128)S(1)} %select_add_fusion.3), channel_id=1, source_target_pairs={{0,2},{1,3},{2,4},{3,5},{4,6},{5,7},{6,0},{7,1},{8,10},{9,11},{10,... | collective-permute-start | bytes 196616 | tf_op jit(solution)/shard_map/ppermute | solution.py:30
  204.4 12.0 %all-to-all-start.9 = ((f32[16,32,128]{2,1,0:T(8,128)}), f32[16,32,128]{2,1,0:T(8,128)S(1)}, u32[]{:S(2)}, u32[]{:S(2)}) async-start(f32[16,32,128]{2,1,0:T(8,128)} %bitcast.49), calls=%async_computation.9 | async-start | bytes 524288 | tf_op jit(solution)/shard_map/all_to_all | solution.py:54
  217.2 11.0 %all-to-all-start.10 = ((f32[16,32,128]{2,1,0:T(8,128)}), f32[16,32,128]{2,1,0:T(8,128)S(1)}, u32[]{:S(2)}, u32[]{:S(2)}) async-start(f32[16,32,128]{2,1,0:T(8,128)} %broadcast_in_dim.75), calls=%async_computation.10 | async-start | bytes 524288 | tf_op jit(solution)/shard_map/all_to_all | solution.py:60
  233.9 6.0 %collective-permute-start.26 = (f32[128,128]{1,0:T(8,128)S(1)}, f32[128,128]{1,0:T(8,128)S(1)}, u32[]{:S(2)}, u32[]{:S(2)}) collective-permute-start(f32[128,128]{1,0:T(8,128)S(1)} %select_add_fusion.2), channel_id=1, source_target_pairs={{0,2},{1,3},{2,4},{3,5},{4,6},{5,7},{6,0},{7,1},{8,10},{9,11},{10,... | collective-permute-start | bytes 196616 | tf_op jit(solution)/shard_map/ppermute | solution.py:30
  244.6 12.1 %all-to-all-start.11 = ((f32[16,32,128]{2,1,0:T(8,128)}), f32[16,32,128]{2,1,0:T(8,128)S(1)}, u32[]{:S(2)}, u32[]{:S(2)}) async-start(f32[16,32,128]{2,1,0:T(8,128)} %bitcast.64), calls=%async_computation.11 | async-start | bytes 524288 | tf_op jit(solution)/shard_map/all_to_all | solution.py:54
  257.4 11.0 %all-to-all-start.12 = ((f32[16,32,128]{2,1,0:T(8,128)}), f32[16,32,128]{2,1,0:T(8,128)S(1)}, u32[]{:S(2)}, u32[]{:S(2)}) async-start(f32[16,32,128]{2,1,0:T(8,128)} %broadcast_in_dim.76), calls=%async_computation.12 | async-start | bytes 524288 | tf_op jit(solution)/shard_map/all_to_all | solution.py:60
  275.6 6.1 %collective-permute-start.31 = (f32[128,128]{1,0:T(8,128)S(1)}, f32[128,128]{1,0:T(8,128)S(1)}, u32[]{:S(2)}, u32[]{:S(2)}) collective-permute-start(f32[128,128]{1,0:T(8,128)S(1)} %select_add_fusion.1), channel_id=1, source_target_pairs={{0,2},{1,3},{2,4},{3,5},{4,6},{5,7},{6,0},{7,1},{8,10},{9,11},{10,... | collective-permute-start | bytes 196616 | tf_op jit(solution)/shard_map/ppermute | solution.py:30
  286.3 12.0 %all-to-all-start.13 = ((f32[16,32,128]{2,1,0:T(8,128)}), f32[16,32,128]{2,1,0:T(8,128)S(1)}, u32[]{:S(2)}, u32[]{:S(2)}) async-start(f32[16,32,128]{2,1,0:T(8,128)} %bitcast.81), calls=%async_computation.13 | async-start | bytes 524288 | tf_op jit(solution)/shard_map/all_to_all | solution.py:54
  299.1 11.0 %all-to-all-start.14 = ((f32[16,32,128]{2,1,0:T(8,128)}), f32[16,32,128]{2,1,0:T(8,128)S(1)}, u32[]{:S(2)}, u32[]{:S(2)}) async-start(f32[16,32,128]{2,1,0:T(8,128)} %broadcast_in_dim.77), calls=%async_computation.14 | async-start | bytes 524288 | tf_op jit(solution)/shard_map/all_to_all | solution.py:60
  315.8 6.0 %collective-permute-start.36 = (f32[128,128]{1,0:T(8,128)S(1)}, f32[128,128]{1,0:T(8,128)S(1)}, u32[]{:S(2)}, u32[]{:S(2)}) collective-permute-start(f32[128,128]{1,0:T(8,128)S(1)} %select_add_fusion), channel_id=1, source_target_pairs={{0,2},{1,3},{2,4},{3,5},{4,6},{5,7},{6,0},{7,1},{8,10},{9,11},{10,... | collective-permute-start | bytes 196616 | tf_op jit(solution)/shard_map/ppermute | solution.py:30
  326.0 12.0 %all-to-all-start.15 = ((f32[16,32,128]{2,1,0:T(8,128)}), f32[16,32,128]{2,1,0:T(8,128)S(1)}, u32[]{:S(2)}, u32[]{:S(2)}) async-start(f32[16,32,128]{2,1,0:T(8,128)} %bitcast.100), calls=%async_computation.15 | async-start | bytes 524288 | tf_op jit(solution)/shard_map/all_to_all | solution.py:54
  (33 other events, 110.0 us)

commit v2 on v1

v2 whole, which is shorter than its diff:
```python
import functools

import jax
import jax.numpy as jnp
from jax import lax
from jax.experimental import pallas as pl
from jax.experimental.pallas import tpu as pltpu
from jax.sharding import PartitionSpec as P

F32 = jnp.float32
BF16 = jnp.bfloat16
VMEM_LIMIT = 32 * 1024 * 1024
VMEM = pl.BlockSpec(memory_space=pltpu.VMEM)
SMEM = pl.BlockSpec(memory_space=pltpu.SMEM)
ANY = pl.BlockSpec(memory_space=pl.ANY)


def kernel_params():
    return pltpu.CompilerParams(vmem_limit_bytes=VMEM_LIMIT)


def dot(left, right):
    return jnp.dot(left, right, preferred_element_type=F32)


def split(value):
    high = value.astype(BF16)
    return high, (value - high.astype(F32)).astype(BF16)


def split_product(left_high, left_low, right):
    width = right.shape[1]
    high, low = split(right)
    both = dot(left_high, jnp.concatenate([high, low], axis=1))
    return both[:, :width] + both[:, width:] + dot(left_low, high)


def pick_kernel(stride_ref, counts_ref, source_ref, field_hbm, nu_hbm, out_ref, field, nu, sems):
    cells = nu.shape[1]
    pad = field.shape[0] - cells
    loads = [
        pltpu.make_async_copy(field_hbm, field.at[pl.ds(pad, cells)], sems.at[0]),
        pltpu.make_async_copy(nu_hbm, nu, sems.at[1]),
    ]
    for load in loads:
        load.start()
    field[0:pad, :] = jnp.zeros((pad, field.shape[1]), F32)
    for load in loads:
        load.wait()
    stride = stride_ref[0]
    slots = source_ref.shape[2]

    @pl.loop(0, source_ref.shape[1])
    def _(grid_row):
        live = counts_ref[0, grid_row]
        for slot in range(slots):
            cell = source_ref[0, grid_row, slot]
            here = field[pl.ds(pad + cell, 1), :]
            radial = here - field[pl.ds(pad + cell - stride, 1), :]
            tangent = here - field[pl.ds(pad - 1 + cell, 1), :]
            swept = nu[0, pl.ds(cell, 1), :] * radial + nu[1, pl.ds(cell, 1), :] * tangent
            out_ref[grid_row, pl.ds(slot, 1), :] = jnp.where(slot < live, swept, 0.0)


def pick(sub_field, reluctivity, stride, counts, source_cell):
    cells, rotor = sub_field.shape
    _, grid_rows, slots = source_cell.shape
    pad = 512
    return pl.pallas_call(
        pick_kernel,
        out_shape=jax.ShapeDtypeStruct((grid_rows, slots, rotor), F32),
        in_specs=[SMEM, SMEM, SMEM, ANY, ANY],
        out_specs=VMEM,
        scratch_shapes=[
            pltpu.VMEM((pad + cells, rotor), F32),
            pltpu.VMEM((2, cells, rotor), F32),
            pltpu.SemaphoreType.DMA((2,)),
        ],
        compiler_params=kernel_params(),
        name="pick",
    )(stride, counts, source_cell, sub_field, reluctivity)


def interface_rows(block, rows, targets_ref, received_ref):
    received = received_ref[...]
    high, low = split(received)
    rest = (received - high.astype(F32) - low.astype(F32)).astype(BF16)
    row = block * rows + lax.broadcasted_iota(jnp.int32, (rows, received.shape[0]), 0)
    chosen = jnp.where(row == targets_ref[...], 1.0, 0.0).astype(BF16)
    both = dot(chosen, jnp.concatenate([high, low], axis=1))
    width = received.shape[1]
    return both[:, :width] + both[:, width:] + dot(chosen, rest)


def halves_out(core_ref, value, mine_ref, theirs_ref, whole):
    whole[...] = value
    half = mine_ref.shape[0]
    core = core_ref[0]
    mine_ref[...] = whole[pl.ds(pl.multiple_of(core * half, half), half), :]
    theirs_ref[...] = whole[pl.ds(pl.multiple_of((1 - core) * half, half), half), :]


def half_shapes(rows, rotor):
    return [jax.ShapeDtypeStruct((rows // 2, rotor), F32)] * 2


def first_kernel(core_ref, targets_ref, received_ref, mine_ref, theirs_ref, whole):
    rows = whole.shape[0]
    value = interface_rows(0, rows, targets_ref, received_ref)
    halves_out(core_ref, value, mine_ref, theirs_ref, whole)


def first_residual(core, targets, received, rows):
    rotor = received.shape[1]
    return pl.pallas_call(
        first_kernel,
        out_shape=half_shapes(rows, rotor),
        in_specs=[SMEM, VMEM, VMEM],
        out_specs=[VMEM, VMEM],
        scratch_shapes=[pltpu.VMEM((rows, rotor), F32)],
        compiler_params=kernel_params(),
        name="first",
    )(core, targets, received)


def fold_kernel(block, first, *refs):
    earlier = block - 1
    targets_ref, received_ref, lower_hbm, diag_hbm = refs[:4]
    shares = refs[4 : 4 + earlier]
    outs = refs[4 + earlier : -3]
    tiles, diags, sems = refs[-3:]
    base = block * (block - 1) // 2
    loads = [
        pltpu.make_async_copy(lower_hbm.at[base + j], tiles.at[j], sems.at[j])
        for j in range(block)
    ]
    loads += [
        pltpu.make_async_copy(diag_hbm.at[first + j], diags.at[j], sems.at[block + j])
        for j in range(block - first + 1)
    ]
    for load in loads:
        load.start()
    started_ref, lower_high, lower_low = outs[:3]
    total = interface_rows(block, started_ref.shape[0], targets_ref, received_ref)
    for j in range(earlier):
        loads[j].wait()
        high, low = split(tiles[j])
        total = total - split_product(high, low, shares[j][...])
    started_ref[...] = total
    loads[earlier].wait()
    lower_high[...], lower_low[...] = split(tiles[earlier])
    for j in range(block - first + 1):
        loads[block + j].wait()
        outs[3 + 2 * j][...], outs[4 + 2 * j][...] = split(diags[j])


def fold(block, first, targets, received, lower_tiles, diag_inverse, shares):
    _, rows, columns = lower_tiles.shape
    _, out_rows, depth = diag_inverse.shape
    rotor = received.shape[1]
    n_diag = block - first + 1
    shapes = [jax.ShapeDtypeStruct((rows, rotor), F32)]
    shapes += [jax.ShapeDtypeStruct((rows, columns), BF16)] * 2
    shapes += [jax.ShapeDtypeStruct((out_rows, depth), BF16)] * (2 * n_diag)
    return pl.pallas_call(
        functools.partial(fold_kernel, block, first),
        out_shape=shapes,
        in_specs=[VMEM, VMEM, ANY, ANY] + [VMEM] * len(shares),
        out_specs=[VMEM] * len(shapes),
        scratch_shapes=[
            pltpu.VMEM((block, rows, columns), F32),
            pltpu.VMEM((n_diag, out_rows, depth), F32),
            pltpu.SemaphoreType.DMA((block + n_diag,)),
        ],
        compiler_params=kernel_params(),
        cost_estimate=pl.CostEstimate(
            flops=6 * block * rows * columns * rotor,
            bytes_accessed=4 * (block + n_diag) * rows * columns,
            transcendentals=0,
        ),
        name="fold",
    )(targets, received, lower_tiles, diag_inverse, *shares)


def lower_kernel(core_ref, share_ref, high_ref, low_ref, started_ref, mine_ref, theirs_ref, whole):
    value = started_ref[...] - split_product(high_ref[...], low_ref[...], share_ref[...])
    halves_out(core_ref, value, mine_ref, theirs_ref, whole)


def lower_product(core, share, high, low, started):
    rows, rotor = started.shape
    return pl.pallas_call(
        lower_kernel,
        out_shape=half_shapes(rows, rotor),
        in_specs=[SMEM] + [VMEM] * 4,
        out_specs=[VMEM, VMEM],
        scratch_shapes=[pltpu.VMEM((rows, rotor), F32)],
        compiler_params=kernel_params(),
        name="lower",
    )(core, share, high, low, started)


def diag_kernel(core_ref, mine_ref, theirs_ref, high_ref, low_ref, out_ref, whole):
    half = mine_ref.shape[0]
    core = core_ref[0]
    whole[pl.ds(pl.multiple_of(core * half, half), half), :] = mine_ref[...]
    whole[pl.ds(pl.multiple_of((1 - core) * half, half), half), :] = theirs_ref[...]
    out_ref[...] = split_product(high_ref[...], low_ref[...], whole[...])


def diag_product(core, mine, theirs, high, low):
    half, rotor = mine.shape
    return pl.pallas_call(
        diag_kernel,
        out_shape=jax.ShapeDtypeStruct((high.shape[0], rotor), F32),
        in_specs=[SMEM] + [VMEM] * 4,
        out_specs=VMEM,
        scratch_shapes=[pltpu.VMEM((2 * half, rotor), F32)],
        compiler_params=kernel_params(),
        name="diag",
    )(core, mine, theirs, high, low)


def piece_kernel(parts_ref, piece_ref, copies_ref):
    piece = jnp.sum(parts_ref[...], axis=0)
    piece_ref[...] = piece
    for peer in range(copies_ref.shape[0]):
        copies_ref[peer] = piece


def piece_and_copies(parts):
    return pl.pallas_call(
        piece_kernel,
        out_shape=[
            jax.ShapeDtypeStruct(parts.shape[1:], F32),
            jax.ShapeDtypeStruct(parts.shape, F32),
        ],
        in_specs=[VMEM],
        out_specs=[VMEM, VMEM],
        compiler_params=kernel_params(),
        name="piece",
    )(parts)


def other_core(value):
    peers = lax.axis_size("col")
    return lax.ppermute(value, "col", [(i, i ^ 1) for i in range(peers)])


def total_along_x(value):
    peers = lax.axis_size("col")
    arrived = [
        lax.ppermute(value, "col", [(i, (i + hop) % peers) for i in range(peers)])
        for hop in range(2, peers, 2)
    ]
    for part in arrived:
        value = value + part
    return value


def per_row(value):
    return lax.all_to_all(value, "row", 0, 0, tiled=True)


def per_device(
    sub_field, reluctivity, stride, counts, source_cell, target_row, lower_tiles, diag_inverse
):
    blocks = diag_inverse.shape[0]
    tile_rows = lower_tiles.shape[1]
    rotor = sub_field.shape[1]
    peers = lax.axis_size("row")
    core = (lax.axis_index("col") % 2).astype(jnp.int32).reshape(1)
    received = per_row(pick(sub_field, reluctivity, stride, counts, source_cell))
    received = received.reshape(-1, rotor)
    targets = target_row.reshape(1, -1)

    shares = []
    pieces = []
    mine, theirs = first_residual(core, targets, received, tile_rows)
    for block in range(blocks):
        mine = total_along_x(mine + other_core(theirs))
        if block + 1 < blocks:
            started, lower_high, lower_low, *diags = fold(
                block + 1,
                block + 1 if block else 0,
                targets,
                received,
                lower_tiles,
                diag_inverse,
                shares,
            )
            if block == 0:
                diag_high, diag_low, *diags = diags
        partial = diag_product(core, mine, other_core(mine), diag_high, diag_low)
        parts = per_row(partial.reshape(peers, -1, rotor))
        piece, copies = piece_and_copies(parts)
        pieces.append(piece)
        if block + 1 < blocks:
            share = per_row(copies).reshape(-1, rotor)
            shares.append(share)
            mine, theirs = lower_product(core, share, lower_high, lower_low, started)
            diag_high, diag_low = diags
    return jnp.stack(pieces)[:, None]


def solution(mesh):
    placed = (
        P(("row", "col"), None),
        P(None, ("row", "col"), None),
        P(("row", "col")),
        P(("row", "col"), None),
        P(("row", "col"), None, None),
        P("row", "col", None, None),
        P(None, "row", "col"),
        P(None, "col", "row"),
    )
    return jax.shard_map(
        per_device,
        mesh=mesh,
        in_specs=placed,
        out_specs=P(None, "col", "row", None),
        check_vma=False,
    )
```

time: 342 us -> 340 us (level)
  blocking collectives: 0 us -> 110 us
  waiting for transfers between devices: 155 us -> 70.4 us
  matrix products: 54.9 us -> 0 us
  local copies, waits for them, and re-layouts: 14.9 us -> 62.2 us
  starting transfers between devices: 105 us -> 74.3 us
  Pallas kernels: 0 us -> 20.4 us
  other arithmetic: 7.04 us -> 0.19 us
    all_to_all x0 -> x8, blocking collectives: none -> 110 us  [per_row(): return lax.all_to_all(value, 'row', 0, 0, tiled=True)]
    all_to_all x16 -> x8, waiting for transfers between devices: 110 us -> 15.2 us  [per_row(): return lax.all_to_all(value, 'row', 0, 0, tiled=True)]
    unnamed x9 -> x39, local copies, waits for them, and re-layouts: 0.67 us -> 56.3 us
    dot_general x44 -> x0, matrix products: 54.9 us -> none  [product(): jnp.dot(left, right, precision=precision, preferred_element_type=jnp.floa...]
    all_to_all x16 -> x8, starting transfers between devices: 61.6 us -> 33.3 us  [per_row(): return lax.all_to_all(value, 'row', 0, 0, tiled=True)]
    pallas_call x0 -> x25, Pallas kernels: none -> 20.4 us  [the longest x7 11.6 us: fold(): pl.pallas_call(functools.partial(fold_kernel, block, first), out_shape=sh...]
    dot_general x8 -> x0, local copies, waits for them, and re-layouts: 6.63 us -> none  [product(): jnp.dot(left, right, precision=precision, preferred_element_type=jnp.floa...]
    ppermute x16, waiting for transfers between devices: 7.75 us -> 13.5 us  [other_core(): return lax.ppermute(value, 'col', [(i, i ^ 1) for i in range(peers)])]
  transfers between devices with their start and end apart: 56 -> 48, of which waited for: 50 -> 41; matrix products, arithmetic and copies ran while one was open for 10% -> 0% of each run, Pallas kernels for 0% -> 3%
where the time goes in v2:
time: 340 us; the launch traced here: 339 us
  blocking collectives  110 us (32%)
  starting transfers between devices  74.3 us (22%)
  waiting for transfers between devices  70.4 us (21%)
  local copies, waits for them, and re-layouts  62.2 us (18%)
  Pallas kernels  20.4 us (6%)
    all_to_all x8, blocking collectives, per_row(): return lax.all_to_all(value, 'row', 0, 0, tiled=True)  110 us
    unnamed x39, local copies, waits for them, and re-layouts  56.3 us
    ppermute x24, waiting for transfers between devices, total_along_x(): lax.ppermute(value, 'col', [(i, (i + hop) % peers) for i in range(peers)])  41.7 us
    all_to_all x8, starting transfers between devices, per_row(): return lax.all_to_all(value, 'row', 0, 0, tiled=True)  33.3 us
    ppermute x16, starting transfers between devices, other_core(): return lax.ppermute(value, 'col', [(i, i ^ 1) for i in range(peers)])  24.4 us
    ppermute x24, starting transfers between devices, total_along_x(): lax.ppermute(value, 'col', [(i, (i + hop) % peers) for i in range(peers)])  16.6 us
    all_to_all x8, waiting for transfers between devices, per_row(): return lax.all_to_all(value, 'row', 0, 0, tiled=True)  15.2 us
    ppermute x16, waiting for transfers between devices, other_core(): return lax.ppermute(value, 'col', [(i, i ^ 1) for i in range(peers)])  13.5 us
  transfers between devices with their start and end apart: 48, of which 41 were waited for; matrix products, arithmetic and copies ran while one was open for 0% of the time, Pallas kernels for 3%

profile of v2, /device:TPU:1, one launch (start us, length us, event | category | flops | bytes accessed | tf_op | source)
XLA Modules:
  0.0 338.6 jit_solution(11530107598125668317)
XLA Ops:
  8.0 8.6 %all-to-all-start = ((f32[16,32,128]{2,1,0:T(8,128)}), f32[16,32,128]{2,1,0:T(8,128)S(1)}, u32[]{:S(2)}, u32[]{:S(2)}) async-start(f32[16,32,128]{2,1,0:T(8,128)} %pick.1), calls=%async_computation | async-start | bytes 524288 | tf_op jit(solution)/shard_map/all_to_all | solution.py:262
  17.4 6.8 %all-to-all-done = f32[16,32,128]{2,1,0:T(8,128)S(1)} async-done(((f32[16,32,128]{2,1,0:T(8,128)}), f32[16,32,128]{2,1,0:T(8,128)S(1)}, u32[]{:S(2)}, u32[]{:S(2)}) %all-to-all-start) | async-done | bytes 262176 | tf_op jit(solution)/shard_map/all_to_all | solution.py:262
  37.6 5.2 %copy-done = f32[28,256,512]{2,1,0:T(8,128)S(1)} copy-done((f32[28,256,512]{2,1,0:T(8,128)S(1)}, f32[28,256,512]{2,1,0:T(8,128)}, u32[]{:S(2)}) %copy-start) | copy-done | bytes 14680088
  46.0 11.2 %all_to_all.80.parts_ref = f32[16,32,128]{2,1,0:T(8,128)S(1)} all-to-all(f32[16,32,128]{2,1,0:T(8,128)S(1)} %bitcast.76), channel_id=1, replica_groups=mesh['row'=16,'col'=8] {'row'}, dimensions={0} | all-to-all | bytes 524288 | tf_op jit(solution)/shard_map/all_to_all | solution.py:262
  57.2 10.2 %all_to_all.81 = f32[16,32,128]{2,1,0:T(8,128)S(1)} all-to-all(f32[16,32,128]{2,1,0:T(8,128)S(1)} %get-tuple-element.78), channel_id=1, replica_groups=mesh['row'=16,'col'=8] {'row'}, dimensions={0} | all-to-all | bytes 524288 | tf_op jit(solution)/shard_map/all_to_all | solution.py:262
  81.0 3.5 %all-to-all-start.3 = ((f32[16,32,128]{2,1,0:T(8,128)}), f32[16,32,128]{2,1,0:T(8,128)S(1)}, u32[]{:S(2)}, u32[]{:S(2)}) async-start(f32[16,32,128]{2,1,0:T(8,128)} %bitcast.5), calls=%async_computation.3 | async-start | bytes 524288 | tf_op jit(solution)/shard_map/all_to_all | solution.py:262
  84.6 8.4 %all-to-all-done.3 = f32[16,32,128]{2,1,0:T(8,128)S(1)} async-done(((f32[16,32,128]{2,1,0:T(8,128)}), f32[16,32,128]{2,1,0:T(8,128)S(1)}, u32[]{:S(2)}, u32[]{:S(2)}) %all-to-all-start.3) | async-done | bytes 262176 | tf_op jit(solution)/shard_map/all_to_all | solution.py:262
  93.7 3.5 %all-to-all-start.4 = ((f32[16,32,128]{2,1,0:T(8,128)}), f32[16,32,128]{2,1,0:T(8,128)S(1)}, u32[]{:S(2)}, u32[]{:S(2)}) async-start(f32[16,32,128]{2,1,0:T(8,128)} %get-tuple-element.152), calls=%async_computation.4 | async-start | bytes 524288 | tf_op jit(solution)/shard_map/all_to_all | solution.py:262
  97.3 5.2 %copy-done.1 = f32[28,256,512]{2,1,0:T(8,128)S(1)} copy-done((f32[28,256,512]{2,1,0:T(8,128)S(1)}, f32[28,256,512]{2,1,0:T(8,128)}, u32[]{:S(2)}) %copy-start.1) | copy-done | bytes 14680088
  118.5 14.5 %all_to_all.82 = f32[16,32,128]{2,1,0:T(8,128)S(1)} all-to-all(f32[16,32,128]{2,1,0:T(8,128)S(1)} %bitcast.77), channel_id=1, replica_groups=mesh['row'=16,'col'=8] {'row'}, dimensions={0} | all-to-all | bytes 524288 | tf_op jit(solution)/shard_map/all_to_all | solution.py:262
  133.8 3.5 %all-to-all-start.6 = ((f32[16,32,128]{2,1,0:T(8,128)}), f32[16,32,128]{2,1,0:T(8,128)S(1)}, u32[]{:S(2)}, u32[]{:S(2)}) async-start(f32[16,32,128]{2,1,0:T(8,128)} %get-tuple-element.156), calls=%async_computation.6 | async-start | bytes 524288 | tf_op jit(solution)/shard_map/all_to_all | solution.py:262
  137.3 5.2 %copy-done.2 = f32[28,256,512]{2,1,0:T(8,128)S(1)} copy-done((f32[28,256,512]{2,1,0:T(8,128)S(1)}, f32[28,256,512]{2,1,0:T(8,128)}, u32[]{:S(2)}) %copy-start.2) | copy-done | bytes 14680088
  157.9 14.8 %all_to_all.83 = f32[16,32,128]{2,1,0:T(8,128)S(1)} all-to-all(f32[16,32,128]{2,1,0:T(8,128)S(1)} %bitcast.78), channel_id=1, replica_groups=mesh['row'=16,'col'=8] {'row'}, dimensions={0} | all-to-all | bytes 524288 | tf_op jit(solution)/shard_map/all_to_all | solution.py:262
  173.4 3.5 %all-to-all-start.8 = ((f32[16,32,128]{2,1,0:T(8,128)}), f32[16,32,128]{2,1,0:T(8,128)S(1)}, u32[]{:S(2)}, u32[]{:S(2)}) async-start(f32[16,32,128]{2,1,0:T(8,128)} %get-tuple-element.148), calls=%async_computation.8 | async-start | bytes 524288 | tf_op jit(solution)/shard_map/all_to_all | solution.py:262
  177.0 5.2 %copy-done.3 = f32[28,256,512]{2,1,0:T(8,128)S(1)} copy-done((f32[28,256,512]{2,1,0:T(8,128)S(1)}, f32[28,256,512]{2,1,0:T(8,128)}, u32[]{:S(2)}) %copy-start.3) | copy-done | bytes 14680088
  198.9 14.8 %all_to_all.84 = f32[16,32,128]{2,1,0:T(8,128)S(1)} all-to-all(f32[16,32,128]{2,1,0:T(8,128)S(1)} %bitcast.79), channel_id=1, replica_groups=mesh['row'=16,'col'=8] {'row'}, dimensions={0} | all-to-all | bytes 524288 | tf_op jit(solution)/shard_map/all_to_all | solution.py:262
  214.5 3.5 %all-to-all-start.10 = ((f32[16,32,128]{2,1,0:T(8,128)}), f32[16,32,128]{2,1,0:T(8,128)S(1)}, u32[]{:S(2)}, u32[]{:S(2)}) async-start(f32[16,32,128]{2,1,0:T(8,128)} %get-tuple-element.144), calls=%async_computation.10 | async-start | bytes 524288 | tf_op jit(solution)/shard_map/all_to_all | solution.py:262
  218.0 5.2 %copy-done.4 = f32[28,256,512]{2,1,0:T(8,128)S(1)} copy-done((f32[28,256,512]{2,1,0:T(8,128)S(1)}, f32[28,256,512]{2,1,0:T(8,128)}, u32[]{:S(2)}) %copy-start.4) | copy-done | bytes 14680088
  239.3 14.8 %all_to_all.85 = f32[16,32,128]{2,1,0:T(8,128)S(1)} all-to-all(f32[16,32,128]{2,1,0:T(8,128)S(1)} %bitcast.80), channel_id=1, replica_groups=mesh['row'=16,'col'=8] {'row'}, dimensions={0} | all-to-all | bytes 524288 | tf_op jit(solution)/shard_map/all_to_all | solution.py:262
  258.4 5.2 %copy-done.5 = f32[28,256,512]{2,1,0:T(8,128)S(1)} copy-done((f32[28,256,512]{2,1,0:T(8,128)S(1)}, f32[28,256,512]{2,1,0:T(8,128)}, u32[]{:S(2)}) %copy-start.5) | copy-done | bytes 14680088
  281.2 14.8 %all_to_all.86 = f32[16,32,128]{2,1,0:T(8,128)S(1)} all-to-all(f32[16,32,128]{2,1,0:T(8,128)S(1)} %bitcast.81), channel_id=1, replica_groups=mesh['row'=16,'col'=8] {'row'}, dimensions={0} | all-to-all | bytes 524288 | tf_op jit(solution)/shard_map/all_to_all | solution.py:262
  296.8 3.5 %all-to-all-start.14 = ((f32[16,32,128]{2,1,0:T(8,128)}), f32[16,32,128]{2,1,0:T(8,128)S(1)}, u32[]{:S(2)}, u32[]{:S(2)}) async-start(f32[16,32,128]{2,1,0:T(8,128)} %get-tuple-element.164), calls=%async_computation.14 | async-start | bytes 524288 | tf_op jit(solution)/shard_map/all_to_all | solution.py:262
  300.4 5.2 %copy-done.6 = f32[28,256,512]{2,1,0:T(8,128)S(1)} copy-done((f32[28,256,512]{2,1,0:T(8,128)S(1)}, f32[28,256,512]{2,1,0:T(8,128)}, u32[]{:S(2)}) %copy-start.6) | copy-done | bytes 14680088
  322.4 14.8 %all_to_all.87 = f32[16,32,128]{2,1,0:T(8,128)S(1)} all-to-all(f32[16,32,128]{2,1,0:T(8,128)S(1)} %bitcast.75), channel_id=1, replica_groups=mesh['row'=16,'col'=8] {'row'}, dimensions={0} | all-to-all | bytes 524288 | tf_op jit(solution)/shard_map/all_to_all | solution.py:262
  (168 shorter events, 146.5 us)
Async XLA Ops:
  8.0 16.2 %all-to-all-start = ((f32[16,32,128]{2,1,0:T(8,128)}), f32[16,32,128]{2,1,0:T(8,128)S(1)}, u32[]{:S(2)}, u32[]{:S(2)}) async-start(f32[16,32,128]{2,1,0:T(8,128)} %pick.1), calls=%async_computation | async-start | bytes 524288 | tf_op jit(solution)/shard_map/all_to_all | solution.py:262
  30.1 4.7 %collective-permute-start.2 = (f32[128,128]{1,0:T(8,128)S(1)}, f32[128,128]{1,0:T(8,128)S(1)}, u32[]{:S(2)}, u32[]{:S(2)}) collective-permute-start(f32[128,128]{1,0:T(8,128)S(1)} %add.101), channel_id=1, source_target_pairs={{0,4},{1,5},{2,6},{3,7},{4,0},{5,1},{6,2},{7,3},{8,12},{9,13},{10,... | collective-permute-start | bytes 196616 | tf_op jit(solution)/shard_map/ppermute | solution.py:253
  30.6 5.4 %collective-permute-start.1 = (f32[128,128]{1,0:T(8,128)S(1)}, f32[128,128]{1,0:T(8,128)S(1)}, u32[]{:S(2)}, u32[]{:S(2)}) collective-permute-start(f32[128,128]{1,0:T(8,128)S(1)} %add.101), channel_id=1, source_target_pairs={{0,2},{1,3},{2,4},{3,5},{4,6},{5,7},{6,0},{7,1},{8,10},{9,11},{10,... | collective-permute-start | bytes 196616 | tf_op jit(solution)/shard_map/ppermute | solution.py:253
  36.0 9.7 %collective-permute-start.4 = (f32[128,128]{1,0:T(8,128)S(1)}, f32[128,128]{1,0:T(8,128)S(1)}, u32[]{:S(2)}, u32[]{:S(2)}) collective-permute-start(f32[128,128]{1,0:T(8,128)S(1)} %add_add_fusion.7.mine_ref), channel_id=1, source_target_pairs={{0,1},{1,0},{2,3},{3,2},{4,5},{5,4},{6,7},{7,6},{8,9},{9,8},{10,11... | collective-permute-start | bytes 196616 | tf_op jit(solution)/shard_map/ppermute | solution.py:247
  72.2 6.0 %collective-permute-start.6 = (f32[128,128]{1,0:T(8,128)S(1)}, f32[128,128]{1,0:T(8,128)S(1)}, u32[]{:S(2)}, u32[]{:S(2)}) collective-permute-start(f32[128,128]{1,0:T(8,128)S(1)} %add.105), channel_id=1, source_target_pairs={{0,2},{1,3},{2,4},{3,5},{4,6},{5,7},{6,0},{7,1},{8,10},{9,11},{10,... | collective-permute-start | bytes 196616 | tf_op jit(solution)/shard_map/ppermute | solution.py:253
  81.0 12.0 %all-to-all-start.3 = ((f32[16,32,128]{2,1,0:T(8,128)}), f32[16,32,128]{2,1,0:T(8,128)S(1)}, u32[]{:S(2)}, u32[]{:S(2)}) async-start(f32[16,32,128]{2,1,0:T(8,128)} %bitcast.5), calls=%async_computation.3 | async-start | bytes 524288 | tf_op jit(solution)/shard_map/all_to_all | solution.py:262
  93.7 11.9 %all-to-all-start.4 = ((f32[16,32,128]{2,1,0:T(8,128)}), f32[16,32,128]{2,1,0:T(8,128)S(1)}, u32[]{:S(2)}, u32[]{:S(2)}) async-start(f32[16,32,128]{2,1,0:T(8,128)} %get-tuple-element.152), calls=%async_computation.4 | async-start | bytes 524288 | tf_op jit(solution)/shard_map/all_to_all | solution.py:262
  109.8 4.7 %collective-permute-start.12 = (f32[128,128]{1,0:T(8,128)S(1)}, f32[128,128]{1,0:T(8,128)S(1)}, u32[]{:S(2)}, u32[]{:S(2)}) collective-permute-start(f32[128,128]{1,0:T(8,128)S(1)} %add.109), channel_id=1, source_target_pairs={{0,4},{1,5},{2,6},{3,7},{4,0},{5,1},{6,2},{7,3},{8,12},{9,13},{10,... | collective-permute-start | bytes 196616 | tf_op jit(solution)/shard_map/ppermute | solution.py:253
  110.4 5.4 %collective-permute-start.11 = (f32[128,128]{1,0:T(8,128)S(1)}, f32[128,128]{1,0:T(8,128)S(1)}, u32[]{:S(2)}, u32[]{:S(2)}) collective-permute-start(f32[128,128]{1,0:T(8,128)S(1)} %add.109), channel_id=1, source_target_pairs={{0,2},{1,3},{2,4},{3,5},{4,6},{5,7},{6,0},{7,1},{8,10},{9,11},{10,... | collective-permute-start | bytes 196616 | tf_op jit(solution)/shard_map/ppermute | solution.py:253
  133.8 12.2 %all-to-all-start.6 = ((f32[16,32,128]{2,1,0:T(8,128)}), f32[16,32,128]{2,1,0:T(8,128)S(1)}, u32[]{:S(2)}, u32[]{:S(2)}) async-start(f32[16,32,128]{2,1,0:T(8,128)} %get-tuple-element.156), calls=%async_computation.6 | async-start | bytes 524288 | tf_op jit(solution)/shard_map/all_to_all | solution.py:262
  149.2 4.6 %collective-permute-start.17 = (f32[128,128]{1,0:T(8,128)S(1)}, f32[128,128]{1,0:T(8,128)S(1)}, u32[]{:S(2)}, u32[]{:S(2)}) collective-permute-start(f32[128,128]{1,0:T(8,128)S(1)} %add.113), channel_id=1, source_target_pairs={{0,4},{1,5},{2,6},{3,7},{4,0},{5,1},{6,2},{7,3},{8,12},{9,13},{10,... | collective-permute-start | bytes 196616 | tf_op jit(solution)/shard_map/ppermute | solution.py:253
  149.9 5.8 %collective-permute-start.16 = (f32[128,128]{1,0:T(8,128)S(1)}, f32[128,128]{1,0:T(8,128)S(1)}, u32[]{:S(2)}, u32[]{:S(2)}) collective-permute-start(f32[128,128]{1,0:T(8,128)S(1)} %add.113), channel_id=1, source_target_pairs={{0,2},{1,3},{2,4},{3,5},{4,6},{5,7},{6,0},{7,1},{8,10},{9,11},{10,... | collective-permute-start | bytes 196616 | tf_op jit(solution)/shard_map/ppermute | solution.py:253
  173.4 12.5 %all-to-all-start.8 = ((f32[16,32,128]{2,1,0:T(8,128)}), f32[16,32,128]{2,1,0:T(8,128)S(1)}, u32[]{:S(2)}, u32[]{:S(2)}) async-start(f32[16,32,128]{2,1,0:T(8,128)} %get-tuple-element.148), calls=%async_computation.8 | async-start | bytes 524288 | tf_op jit(solution)/shard_map/all_to_all | solution.py:262
  190.2 4.7 %collective-permute-start.22 = (f32[128,128]{1,0:T(8,128)S(1)}, f32[128,128]{1,0:T(8,128)S(1)}, u32[]{:S(2)}, u32[]{:S(2)}) collective-permute-start(f32[128,128]{1,0:T(8,128)S(1)} %add.117), channel_id=1, source_target_pairs={{0,4},{1,5},{2,6},{3,7},{4,0},{5,1},{6,2},{7,3},{8,12},{9,13},{10,... | collective-permute-start | bytes 196616 | tf_op jit(solution)/shard_map/ppermute | solution.py:253
  190.8 5.3 %collective-permute-start.21 = (f32[128,128]{1,0:T(8,128)S(1)}, f32[128,128]{1,0:T(8,128)S(1)}, u32[]{:S(2)}, u32[]{:S(2)}) collective-permute-start(f32[128,128]{1,0:T(8,128)S(1)} %add.117), channel_id=1, source_target_pairs={{0,2},{1,3},{2,4},{3,5},{4,6},{5,7},{6,0},{7,1},{8,10},{9,11},{10,... | collective-permute-start | bytes 196616 | tf_op jit(solution)/shard_map/ppermute | solution.py:253
  214.5 12.9 %all-to-all-start.10 = ((f32[16,32,128]{2,1,0:T(8,128)}), f32[16,32,128]{2,1,0:T(8,128)S(1)}, u32[]{:S(2)}, u32[]{:S(2)}) async-start(f32[16,32,128]{2,1,0:T(8,128)} %get-tuple-element.144), calls=%async_computation.10 | async-start | bytes 524288 | tf_op jit(solution)/shard_map/all_to_all | solution.py:262
  230.6 4.6 %collective-permute-start.27 = (f32[128,128]{1,0:T(8,128)S(1)}, f32[128,128]{1,0:T(8,128)S(1)}, u32[]{:S(2)}, u32[]{:S(2)}) collective-permute-start(f32[128,128]{1,0:T(8,128)S(1)} %add.121), channel_id=1, source_target_pairs={{0,4},{1,5},{2,6},{3,7},{4,0},{5,1},{6,2},{7,3},{8,12},{9,13},{10,... | collective-permute-start | bytes 196616 | tf_op jit(solution)/shard_map/ppermute | solution.py:253
  231.2 6.0 %collective-permute-start.26 = (f32[128,128]{1,0:T(8,128)S(1)}, f32[128,128]{1,0:T(8,128)S(1)}, u32[]{:S(2)}, u32[]{:S(2)}) collective-permute-start(f32[128,128]{1,0:T(8,128)S(1)} %add.121), channel_id=1, source_target_pairs={{0,2},{1,3},{2,4},{3,5},{4,6},{5,7},{6,0},{7,1},{8,10},{9,11},{10,... | collective-permute-start | bytes 196616 | tf_op jit(solution)/shard_map/ppermute | solution.py:253
  254.9 13.2 %all-to-all-start.12 = ((f32[16,32,128]{2,1,0:T(8,128)}), f32[16,32,128]{2,1,0:T(8,128)S(1)}, u32[]{:S(2)}, u32[]{:S(2)}) async-start(f32[16,32,128]{2,1,0:T(8,128)} %get-tuple-element.160), calls=%async_computation.12 | async-start | bytes 524288 | tf_op jit(solution)/shard_map/all_to_all | solution.py:262
  272.5 4.7 %collective-permute-start.32 = (f32[128,128]{1,0:T(8,128)S(1)}, f32[128,128]{1,0:T(8,128)S(1)}, u32[]{:S(2)}, u32[]{:S(2)}) collective-permute-start(f32[128,128]{1,0:T(8,128)S(1)} %add.125), channel_id=1, source_target_pairs={{0,4},{1,5},{2,6},{3,7},{4,0},{5,1},{6,2},{7,3},{8,12},{9,13},{10,... | collective-permute-start | bytes 196616 | tf_op jit(solution)/shard_map/ppermute | solution.py:253
  273.1 5.3 %collective-permute-start.31 = (f32[128,128]{1,0:T(8,128)S(1)}, f32[128,128]{1,0:T(8,128)S(1)}, u32[]{:S(2)}, u32[]{:S(2)}) collective-permute-start(f32[128,128]{1,0:T(8,128)S(1)} %add.125), channel_id=1, source_target_pairs={{0,2},{1,3},{2,4},{3,5},{4,6},{5,7},{6,0},{7,1},{8,10},{9,11},{10,... | collective-permute-start | bytes 196616 | tf_op jit(solution)/shard_map/ppermute | solution.py:253
  296.8 13.6 %all-to-all-start.14 = ((f32[16,32,128]{2,1,0:T(8,128)}), f32[16,32,128]{2,1,0:T(8,128)S(1)}, u32[]{:S(2)}, u32[]{:S(2)}) async-start(f32[16,32,128]{2,1,0:T(8,128)} %get-tuple-element.164), calls=%async_computation.14 | async-start | bytes 524288 | tf_op jit(solution)/shard_map/all_to_all | solution.py:262
  313.7 4.6 %collective-permute-start.37 = (f32[128,128]{1,0:T(8,128)S(1)}, f32[128,128]{1,0:T(8,128)S(1)}, u32[]{:S(2)}, u32[]{:S(2)}) collective-permute-start(f32[128,128]{1,0:T(8,128)S(1)} %add.129), channel_id=1, source_target_pairs={{0,4},{1,5},{2,6},{3,7},{4,0},{5,1},{6,2},{7,3},{8,12},{9,13},{10,... | collective-permute-start | bytes 196616 | tf_op jit(solution)/shard_map/ppermute | solution.py:253
  314.2 6.0 %collective-permute-start.36 = (f32[128,128]{1,0:T(8,128)S(1)}, f32[128,128]{1,0:T(8,128)S(1)}, u32[]{:S(2)}, u32[]{:S(2)}) collective-permute-start(f32[128,128]{1,0:T(8,128)S(1)} %add.129), channel_id=1, source_target_pairs={{0,2},{1,3},{2,4},{3,5},{4,6},{5,7},{6,0},{7,1},{8,10},{9,11},{10,... | collective-permute-start | bytes 196616 | tf_op jit(solution)/shard_map/ppermute | solution.py:253
  (43 other events, 123.5 us)

commit v3 on v2

--- a/solution.py
+++ b/solution.py
@@ -10,13 +10,15 @@
 F32 = jnp.float32
 BF16 = jnp.bfloat16
 VMEM_LIMIT = 32 * 1024 * 1024
+WIDE_LIMIT = 50 * 1024 * 1024
+PICK_LIMIT = 54 * 1024 * 1024
 VMEM = pl.BlockSpec(memory_space=pltpu.VMEM)
 SMEM = pl.BlockSpec(memory_space=pltpu.SMEM)
-ANY = pl.BlockSpec(memory_space=pl.ANY)
-
-
-def kernel_params():
-    return pltpu.CompilerParams(vmem_limit_bytes=VMEM_LIMIT)
+HBM = pl.BlockSpec(memory_space=pltpu.HBM)
+
+
+def kernel_params(limit=VMEM_LIMIT):
+    return pltpu.CompilerParams(vmem_limit_bytes=limit)
 
 
 def dot(left, right):
@@ -35,16 +37,25 @@
     return both[:, :width] + both[:, width:] + dot(left_low, high)
 
 
-def pick_kernel(stride_ref, counts_ref, source_ref, field_hbm, nu_hbm, out_ref, field, nu, sems):
+def pick_kernel(
+    stride_hbm, counts_hbm, source_hbm, target_ref, field_hbm, nu_hbm,
+    out_ref, targets_ref, stride_ref, counts_ref, source_ref, field, nu, sems,
+):
     cells = nu.shape[1]
     pad = field.shape[0] - cells
     loads = [
+        pltpu.make_async_copy(stride_hbm, stride_ref, sems.at[2]),
+        pltpu.make_async_copy(counts_hbm, counts_ref, sems.at[3]),
+        pltpu.make_async_copy(source_hbm, source_ref, sems.at[4]),
         pltpu.make_async_copy(field_hbm, field.at[pl.ds(pad, cells)], sems.at[0]),
         pltpu.make_async_copy(nu_hbm, nu, sems.at[1]),
     ]
     for load in loads:
         load.start()
     field[0:pad, :] = jnp.zeros((pad, field.shape[1]), F32)
+    width = target_ref.shape[1]
+    for sender in range(target_ref.shape[0]):
+        targets_ref[0:1, sender * width : (sender + 1) * width] = target_ref[sender : sender + 1, :]
     for load in loads:
         load.wait()
     stride = stride_ref[0]
@@ -62,23 +73,29 @@
             out_ref[grid_row, pl.ds(slot, 1), :] = jnp.where(slot < live, swept, 0.0)
 
 
-def pick(sub_field, reluctivity, stride, counts, source_cell):
+def pick(sub_field, reluctivity, stride, counts, source_cell, target_row):
     cells, rotor = sub_field.shape
     _, grid_rows, slots = source_cell.shape
     pad = 512
     return pl.pallas_call(
         pick_kernel,
-        out_shape=jax.ShapeDtypeStruct((grid_rows, slots, rotor), F32),
-        in_specs=[SMEM, SMEM, SMEM, ANY, ANY],
-        out_specs=VMEM,
+        out_shape=[
+            jax.ShapeDtypeStruct((grid_rows, slots, rotor), F32),
+            jax.ShapeDtypeStruct((1, target_row.size), jnp.int32),
+        ],
+        in_specs=[HBM, HBM, HBM, VMEM, HBM, HBM],
+        out_specs=[VMEM, VMEM],
         scratch_shapes=[
+            pltpu.SMEM(stride.shape, jnp.int32),
+            pltpu.SMEM(counts.shape, jnp.int32),
+            pltpu.SMEM(source_cell.shape, jnp.int32),
             pltpu.VMEM((pad + cells, rotor), F32),
             pltpu.VMEM((2, cells, rotor), F32),
-            pltpu.SemaphoreType.DMA((2,)),
+            pltpu.SemaphoreType.DMA((5,)),
         ],
-        compiler_params=kernel_params(),
+        compiler_params=kernel_params(PICK_LIMIT),
         name="pick",
-    )(stride, counts, source_cell, sub_field, reluctivity)
+    )(stride, counts, source_cell, target_row, sub_field, reluctivity)
 
 
 def interface_rows(block, rows, targets_ref, received_ref):
@@ -123,7 +140,7 @@
     )(core, targets, received)
 
 
-def fold_kernel(block, first, *refs):
+def fold_kernel(block, first, last, *refs):
     earlier = block - 1
     targets_ref, received_ref, lower_hbm, diag_hbm = refs[:4]
     shares = refs[4 : 4 + earlier]
@@ -136,7 +153,7 @@
     ]
     loads += [
         pltpu.make_async_copy(diag_hbm.at[first + j], diags.at[j], sems.at[block + j])
-        for j in range(block - first + 1)
+        for j in range(last - first + 1)
     ]
     for load in loads:
         load.start()
@@ -149,30 +166,30 @@
     started_ref[...] = total
     loads[earlier].wait()
     lower_high[...], lower_low[...] = split(tiles[earlier])
-    for j in range(block - first + 1):
+    for j in range(last - first + 1):
         loads[block + j].wait()
         outs[3 + 2 * j][...], outs[4 + 2 * j][...] = split(diags[j])
 
 
-def fold(block, first, targets, received, lower_tiles, diag_inverse, shares):
+def fold(block, first, last, targets, received, lower_tiles, diag_inverse, shares):
     _, rows, columns = lower_tiles.shape
     _, out_rows, depth = diag_inverse.shape
     rotor = received.shape[1]
-    n_diag = block - first + 1
+    n_diag = last - first + 1
     shapes = [jax.ShapeDtypeStruct((rows, rotor), F32)]
     shapes += [jax.ShapeDtypeStruct((rows, columns), BF16)] * 2
     shapes += [jax.ShapeDtypeStruct((out_rows, depth), BF16)] * (2 * n_diag)
     return pl.pallas_call(
-        functools.partial(fold_kernel, block, first),
+        functools.partial(fold_kernel, block, first, last),
         out_shape=shapes,
-        in_specs=[VMEM, VMEM, ANY, ANY] + [VMEM] * len(shares),
+        in_specs=[VMEM, VMEM, HBM, HBM] + [VMEM] * len(shares),
         out_specs=[VMEM] * len(shapes),
         scratch_shapes=[
             pltpu.VMEM((block, rows, columns), F32),
             pltpu.VMEM((n_diag, out_rows, depth), F32),
             pltpu.SemaphoreType.DMA((block + n_diag,)),
         ],
-        compiler_params=kernel_params(),
+        compiler_params=kernel_params(WIDE_LIMIT),
         cost_estimate=pl.CostEstimate(
             flops=6 * block * rows * columns * rotor,
             bytes_accessed=4 * (block + n_diag) * rows * columns,
@@ -240,6 +257,24 @@
         compiler_params=kernel_params(),
         name="piece",
     )(parts)
+
+
+def stacked_kernel(parts_ref, *refs):
+    *piece_refs, out_ref = refs
+    for block, piece_ref in enumerate(piece_refs):
+        out_ref[block] = piece_ref[...]
+    out_ref[len(piece_refs)] = jnp.sum(parts_ref[...], axis=0)
+
+
+def stacked(parts, pieces):
+    return pl.pallas_call(
+        stacked_kernel,
+        out_shape=jax.ShapeDtypeStruct((len(pieces) + 1, *parts.shape[1:]), F32),
+        in_specs=[VMEM] * (1 + len(pieces)),
+        out_specs=VMEM,
+        compiler_params=kernel_params(),
+        name="stacked",
+    )(parts, *pieces)
 
 
 def other_core(value):
@@ -270,9 +305,10 @@
     rotor = sub_field.shape[1]
     peers = lax.axis_size("row")
     core = (lax.axis_index("col") % 2).astype(jnp.int32).reshape(1)
-    received = per_row(pick(sub_field, reluctivity, stride, counts, source_cell))
-    received = received.reshape(-1, rotor)
-    targets = target_row.reshape(1, -1)
+    picked, targets = pick(
+        sub_field, reluctivity, stride, counts, source_cell, target_row[0, 0]
+    )
+    received = per_row(picked).reshape(-1, rotor)
 
     shares = []
     pieces = []
@@ -280,27 +316,20 @@
     for block in range(blocks):
         mine = total_along_x(mine + other_core(theirs))
         if block + 1 < blocks:
+            last = block if block + 2 < blocks else block + 1
             started, lower_high, lower_low, *diags = fold(
-                block + 1,
-                block + 1 if block else 0,
-                targets,
-                received,
-                lower_tiles,
-                diag_inverse,
-                shares,
+                block + 1, block, last, targets, received, lower_tiles, diag_inverse, shares
             )
-            if block == 0:
-                diag_high, diag_low, *diags = diags
+        diag_high, diag_low, *diags = diags
         partial = diag_product(core, mine, other_core(mine), diag_high, diag_low)
         parts = per_row(partial.reshape(peers, -1, rotor))
-        piece, copies = piece_and_copies(parts)
-        pieces.append(piece)
         if block + 1 < blocks:
+            piece, copies = piece_and_copies(parts)
+            pieces.append(piece)
             share = per_row(copies).reshape(-1, rotor)
             shares.append(share)
             mine, theirs = lower_product(core, share, lower_high, lower_low, started)
-            diag_high, diag_low = diags
-    return jnp.stack(pieces)[:, None]
+    return stacked(parts, pieces)[:, None]
 
 
 def solution(mesh):

time: 340 us -> 303 us (0.89)
  local copies, waits for them, and re-layouts: 62.2 us -> 1.36 us
  blocking collectives: 110 us -> 160 us
  starting transfers between devices: 74.3 us -> 55.6 us
  waiting for transfers between devices: 70.4 us -> 57.4 us
  Pallas kernels: 20.4 us -> 26.4 us
    unnamed x39 -> x4, local copies, waits for them, and re-layouts: 56.3 us -> 1.36 us
    all_to_all x8 -> x15, blocking collectives: 110 us -> 160 us  [per_row(): return lax.all_to_all(value, 'row', 0, 0, tiled=True)]
    all_to_all x8 -> x1, starting transfers between devices: 33.3 us -> 8.61 us  [per_row(): return lax.all_to_all(value, 'row', 0, 0, tiled=True)]
    all_to_all x8 -> x1, waiting for transfers between devices: 15.2 us -> 7.53 us  [per_row(): return lax.all_to_all(value, 'row', 0, 0, tiled=True)]
    pallas_call x8 -> x9, Pallas kernels: 14.7 us -> 21.2 us  [the longest x7 15.6 us: fold(): pl.pallas_call(functools.partial(fold_kernel, block, first, last), out_sh...]
    ppermute x16, starting transfers between devices: 24.4 us -> 30.4 us  [other_core(): return lax.ppermute(value, 'col', [(i, i ^ 1) for i in range(peers)])]
    ppermute x16, waiting for transfers between devices: 13.5 us -> 8.14 us  [other_core(): return lax.ppermute(value, 'col', [(i, i ^ 1) for i in range(peers)])]
    pallas_call x7 -> x0, local copies, waits for them, and re-layouts: 5.15 us -> none  [piece_and_copies(): pl.pallas_call(piece_kernel, out_shape=[jax.ShapeDtypeStruct(parts.shape[...]
  transfers between devices with their start and end apart: 48 -> 41, of which waited for: 41 -> 34; matrix products, arithmetic and copies ran while one was open for 0% -> 0% of each run, Pallas kernels for 3% -> 5%
where the time goes in v3:
time: 303 us; the launch traced here: 302 us
  blocking collectives  160 us (53%)
  waiting for transfers between devices  57.4 us (19%)
  starting transfers between devices  55.6 us (18%)
  Pallas kernels  26.4 us (9%)
    all_to_all x15, blocking collectives, per_row(): return lax.all_to_all(value, 'row', 0, 0, tiled=True)  160 us
    ppermute x24, waiting for transfers between devices, total_along_x(): lax.ppermute(value, 'col', [(i, (i + hop) % peers) for i in range(peers)])  41.7 us
    ppermute x16, starting transfers between devices, other_core(): return lax.ppermute(value, 'col', [(i, i ^ 1) for i in range(peers)])  30.4 us
    ppermute x24, starting transfers between devices, total_along_x(): lax.ppermute(value, 'col', [(i, (i + hop) % peers) for i in range(peers)])  16.6 us
    pallas_call x7, Pallas kernels, fold(): pl.pallas_call(functools.partial(fold_kernel, block, first, last), out_sh...  15.6 us
    all_to_all x1, starting transfers between devices, per_row(): return lax.all_to_all(value, 'row', 0, 0, tiled=True)  8.61 us
    ppermute x16, waiting for transfers between devices, other_core(): return lax.ppermute(value, 'col', [(i, i ^ 1) for i in range(peers)])  8.14 us
    all_to_all x1, waiting for transfers between devices, per_row(): return lax.all_to_all(value, 'row', 0, 0, tiled=True)  7.53 us
  transfers between devices with their start and end apart: 41, of which 34 were waited for; matrix products, arithmetic and copies ran while one was open for 0% of the time, Pallas kernels for 5%

profile of v3, /device:TPU:1, one launch (start us, length us, event | category | flops | bytes accessed | tf_op | source)
XLA Modules:
  0.0 301.9 jit_solution(1180142018622120883)
XLA Ops:
  0.7 4.9 %pick.1 = (f32[16,32,128]{2,1,0:T(8,128)}, s32[1,512]{1,0:T(1,128)}) custom-call(s32[1]{0:T(128)S(6)} %copy.10.stride_hbm, s32[1,16]{1,0:T(1,128)} %counts_hbm.1, s32[1,16,32]{2,1,0:T(8,128)} %source_hbm.1, s32[16,32]{1,0:T(8,128)} %bitcast.65, f32[2048,128]{1,0:T(8,128)} %field_hbm.1, f32[2,2048,128]{2,1,0:T(8,128)} %nu_hbm.1), custom_call_target="tpu_custom_call" | custom-call | tf_op jit(solution)/shard_map/pick/pallas_call | solution.py:80
  5.5 8.6 %all-to-all-start = ((f32[16,32,128]{2,1,0:T(8,128)}), f32[16,32,128]{2,1,0:T(8,128)S(1)}, u32[]{:S(2)}, u32[]{:S(2)}) async-start(f32[16,32,128]{2,1,0:T(8,128)} %get-tuple-element.75), calls=%async_computation | async-start | bytes 524288 | tf_op jit(solution)/shard_map/all_to_all | solution.py:297
  14.2 7.5 %all-to-all-done = f32[16,32,128]{2,1,0:T(8,128)S(1)} async-done(((f32[16,32,128]{2,1,0:T(8,128)}), f32[16,32,128]{2,1,0:T(8,128)S(1)}, u32[]{:S(2)}, u32[]{:S(2)}) %all-to-all-start) | async-done | bytes 262176 | tf_op jit(solution)/shard_map/all_to_all | solution.py:297
  29.7 3.3 %collective-permute-done.2 = f32[128,128]{1,0:T(8,128)S(1)} collective-permute-done((f32[128,128]{1,0:T(8,128)S(1)}, f32[128,128]{1,0:T(8,128)S(1)}, u32[]{:S(2)}, u32[]{:S(2)}) %collective-permute-start.2) | collective-permute-done | bytes 65568 | tf_op jit(solution)/shard_map/ppermute | solution.py:288
  38.3 11.2 %all_to_all.80.parts_ref = f32[16,32,128]{2,1,0:T(8,128)S(1)} all-to-all(f32[16,32,128]{2,1,0:T(8,128)S(1)} %bitcast.58), channel_id=1, replica_groups=mesh['row'=16,'col'=8] {'row'}, dimensions={0} | all-to-all | bytes 524288 | tf_op jit(solution)/shard_map/all_to_all | solution.py:297
  49.5 10.2 %all_to_all.81 = f32[16,32,128]{2,1,0:T(8,128)S(1)} all-to-all(f32[16,32,128]{2,1,0:T(8,128)S(1)} %get-tuple-element.80), channel_id=1, replica_groups=mesh['row'=16,'col'=8] {'row'}, dimensions={0} | all-to-all | bytes 524288 | tf_op jit(solution)/shard_map/all_to_all | solution.py:297
  73.3 11.1 %all_to_all.82.parts_ref = f32[16,32,128]{2,1,0:T(8,128)S(1)} all-to-all(f32[16,32,128]{2,1,0:T(8,128)S(1)} %bitcast.59), channel_id=1, replica_groups=mesh['row'=16,'col'=8] {'row'}, dimensions={0} | all-to-all | bytes 524288 | tf_op jit(solution)/shard_map/all_to_all | solution.py:297
  84.4 10.2 %all_to_all.83 = f32[16,32,128]{2,1,0:T(8,128)S(1)} all-to-all(f32[16,32,128]{2,1,0:T(8,128)S(1)} %get-tuple-element.88), channel_id=1, replica_groups=mesh['row'=16,'col'=8] {'row'}, dimensions={0} | all-to-all | bytes 524288 | tf_op jit(solution)/shard_map/all_to_all | solution.py:297
  101.6 2.9 collective-permute-done.12
  109.6 11.1 %all_to_all.84.parts_ref = f32[16,32,128]{2,1,0:T(8,128)S(1)} all-to-all(f32[16,32,128]{2,1,0:T(8,128)S(1)} %bitcast.60), channel_id=1, replica_groups=mesh['row'=16,'col'=8] {'row'}, dimensions={0} | all-to-all | bytes 524288 | tf_op jit(solution)/shard_map/all_to_all | solution.py:297
  120.8 10.2 %all_to_all.85 = f32[16,32,128]{2,1,0:T(8,128)S(1)} all-to-all(f32[16,32,128]{2,1,0:T(8,128)S(1)} %get-tuple-element.96), channel_id=1, replica_groups=mesh['row'=16,'col'=8] {'row'}, dimensions={0} | all-to-all | bytes 524288 | tf_op jit(solution)/shard_map/all_to_all | solution.py:297
  145.2 11.1 %all_to_all.86.parts_ref = f32[16,32,128]{2,1,0:T(8,128)S(1)} all-to-all(f32[16,32,128]{2,1,0:T(8,128)S(1)} %bitcast.61), channel_id=1, replica_groups=mesh['row'=16,'col'=8] {'row'}, dimensions={0} | all-to-all | bytes 524288 | tf_op jit(solution)/shard_map/all_to_all | solution.py:297
  156.4 10.2 %all_to_all.87 = f32[16,32,128]{2,1,0:T(8,128)S(1)} all-to-all(f32[16,32,128]{2,1,0:T(8,128)S(1)} %get-tuple-element.104), channel_id=1, replica_groups=mesh['row'=16,'col'=8] {'row'}, dimensions={0} | all-to-all | bytes 524288 | tf_op jit(solution)/shard_map/all_to_all | solution.py:297
  173.6 2.9 collective-permute-done.22
  182.2 11.1 %all_to_all.88.parts_ref = f32[16,32,128]{2,1,0:T(8,128)S(1)} all-to-all(f32[16,32,128]{2,1,0:T(8,128)S(1)} %bitcast.62), channel_id=1, replica_groups=mesh['row'=16,'col'=8] {'row'}, dimensions={0} | all-to-all | bytes 524288 | tf_op jit(solution)/shard_map/all_to_all | solution.py:297
  193.4 10.2 %all_to_all.89 = f32[16,32,128]{2,1,0:T(8,128)S(1)} all-to-all(f32[16,32,128]{2,1,0:T(8,128)S(1)} %get-tuple-element.112), channel_id=1, replica_groups=mesh['row'=16,'col'=8] {'row'}, dimensions={0} | all-to-all | bytes 524288 | tf_op jit(solution)/shard_map/all_to_all | solution.py:297
  215.3 2.8 fold.12
  218.5 11.1 %all_to_all.90.parts_ref = f32[16,32,128]{2,1,0:T(8,128)S(1)} all-to-all(f32[16,32,128]{2,1,0:T(8,128)S(1)} %bitcast.63), channel_id=1, replica_groups=mesh['row'=16,'col'=8] {'row'}, dimensions={0} | all-to-all | bytes 524288 | tf_op jit(solution)/shard_map/all_to_all | solution.py:297
  229.6 10.2 %all_to_all.91 = f32[16,32,128]{2,1,0:T(8,128)S(1)} all-to-all(f32[16,32,128]{2,1,0:T(8,128)S(1)} %get-tuple-element.120), channel_id=1, replica_groups=mesh['row'=16,'col'=8] {'row'}, dimensions={0} | all-to-all | bytes 524288 | tf_op jit(solution)/shard_map/all_to_all | solution.py:297
  246.8 2.8 collective-permute-done.32
  252.5 3.2 %fold.13 = (f32[256,128]{1,0:T(8,128)S(1)}, bf16[256,512]{1,0:T(8,128)(2,1)S(1)}, bf16[256,512]{1,0:T(8,128)(2,1)S(1)}, bf16[512,256]{1,0:T(8,128)(2,1)S(1)}, bf...) custom-call(s32[1,512]{1,0:T(1,128)S(1)} %copy-done.1, ...), custom_call_target="tpu_custom_call" | custom-call | flops 704643072 | bytes 4718592 | tf_op jit(solution)/shard_map/fold/pallas_call | solution.py:182
  256.1 11.1 %all_to_all.92.parts_ref = f32[16,32,128]{2,1,0:T(8,128)S(1)} all-to-all(f32[16,32,128]{2,1,0:T(8,128)S(1)} %bitcast.64), channel_id=1, replica_groups=mesh['row'=16,'col'=8] {'row'}, dimensions={0} | all-to-all | bytes 524288 | tf_op jit(solution)/shard_map/all_to_all | solution.py:297
  267.3 10.2 %all_to_all.93 = f32[16,32,128]{2,1,0:T(8,128)S(1)} all-to-all(f32[16,32,128]{2,1,0:T(8,128)S(1)} %get-tuple-element.128), channel_id=1, replica_groups=mesh['row'=16,'col'=8] {'row'}, dimensions={0} | all-to-all | bytes 524288 | tf_op jit(solution)/shard_map/all_to_all | solution.py:297
  290.5 10.8 %all_to_all.94.parts_ref = f32[16,32,128]{2,1,0:T(8,128)S(1)} all-to-all(f32[16,32,128]{2,1,0:T(8,128)S(1)} %bitcast.57), channel_id=1, replica_groups=mesh['row'=16,'col'=8] {'row'}, dimensions={0} | all-to-all | bytes 524288 | tf_op jit(solution)/shard_map/all_to_all | solution.py:297
  (125 shorter events, 101.9 us)
Async XLA Ops:
  5.5 16.2 %all-to-all-start = ((f32[16,32,128]{2,1,0:T(8,128)}), f32[16,32,128]{2,1,0:T(8,128)S(1)}, u32[]{:S(2)}, u32[]{:S(2)}) async-start(f32[16,32,128]{2,1,0:T(8,128)} %get-tuple-element.75), calls=%async_computation | async-start | bytes 524288 | tf_op jit(solution)/shard_map/all_to_all | solution.py:297
  25.8 3.9 %collective-permute-start.3 = (f32[128,128]{1,0:T(8,128)S(1)}, f32[128,128]{1,0:T(8,128)S(1)}, u32[]{:S(2)}, u32[]{:S(2)}) collective-permute-start(f32[128,128]{1,0:T(8,128)S(1)} %add.101), channel_id=1, source_target_pairs={{0,6},{1,7},{2,0},{3,1},{4,2},{5,3},{6,4},{7,5},{8,14},{9,15},{10,... | collective-permute-start | bytes 196616 | tf_op jit(solution)/shard_map/ppermute | solution.py:288
  28.4 4.7 %collective-permute-start.2 = (f32[128,128]{1,0:T(8,128)S(1)}, f32[128,128]{1,0:T(8,128)S(1)}, u32[]{:S(2)}, u32[]{:S(2)}) collective-permute-start(f32[128,128]{1,0:T(8,128)S(1)} %add.101), channel_id=1, source_target_pairs={{0,4},{1,5},{2,6},{3,7},{4,0},{5,1},{6,2},{7,3},{8,12},{9,13},{10,... | collective-permute-start | bytes 196616 | tf_op jit(solution)/shard_map/ppermute | solution.py:288
  28.9 5.4 %collective-permute-start.1 = (f32[128,128]{1,0:T(8,128)S(1)}, f32[128,128]{1,0:T(8,128)S(1)}, u32[]{:S(2)}, u32[]{:S(2)}) collective-permute-start(f32[128,128]{1,0:T(8,128)S(1)} %add.101), channel_id=1, source_target_pairs={{0,2},{1,3},{2,4},{3,5},{4,6},{5,7},{6,0},{7,1},{8,10},{9,11},{10,... | collective-permute-start | bytes 196616 | tf_op jit(solution)/shard_map/ppermute | solution.py:288
  34.3 3.7 %collective-permute-start.4 = (f32[128,128]{1,0:T(8,128)S(1)}, f32[128,128]{1,0:T(8,128)S(1)}, u32[]{:S(2)}, u32[]{:S(2)}) collective-permute-start(f32[128,128]{1,0:T(8,128)S(1)} %add_add_fusion.7.mine_ref), channel_id=1, source_target_pairs={{0,1},{1,0},{2,3},{3,2},{4,5},{5,4},{6,7},{7,6},{8,9},{9,8},{10,11... | collective-permute-start | bytes 196616 | tf_op jit(solution)/shard_map/ppermute | solution.py:282
  63.8 4.6 %collective-permute-start.7 = (f32[128,128]{1,0:T(8,128)S(1)}, f32[128,128]{1,0:T(8,128)S(1)}, u32[]{:S(2)}, u32[]{:S(2)}) collective-permute-start(f32[128,128]{1,0:T(8,128)S(1)} %add.105), channel_id=1, source_target_pairs={{0,4},{1,5},{2,6},{3,7},{4,0},{5,1},{6,2},{7,3},{8,12},{9,13},{10,... | collective-permute-start | bytes 196616 | tf_op jit(solution)/shard_map/ppermute | solution.py:288
  64.4 6.0 %collective-permute-start.6 = (f32[128,128]{1,0:T(8,128)S(1)}, f32[128,128]{1,0:T(8,128)S(1)}, u32[]{:S(2)}, u32[]{:S(2)}) collective-permute-start(f32[128,128]{1,0:T(8,128)S(1)} %add.105), channel_id=1, source_target_pairs={{0,2},{1,3},{2,4},{3,5},{4,6},{5,7},{6,0},{7,1},{8,10},{9,11},{10,... | collective-permute-start | bytes 196616 | tf_op jit(solution)/shard_map/ppermute | solution.py:288
  99.9 4.7 %collective-permute-start.12 = (f32[128,128]{1,0:T(8,128)S(1)}, f32[128,128]{1,0:T(8,128)S(1)}, u32[]{:S(2)}, u32[]{:S(2)}) collective-permute-start(f32[128,128]{1,0:T(8,128)S(1)} %add.109), channel_id=1, source_target_pairs={{0,4},{1,5},{2,6},{3,7},{4,0},{5,1},{6,2},{7,3},{8,12},{9,13},{10,... | collective-permute-start | bytes 196616 | tf_op jit(solution)/shard_map/ppermute | solution.py:288
  100.5 5.4 %collective-permute-start.11 = (f32[128,128]{1,0:T(8,128)S(1)}, f32[128,128]{1,0:T(8,128)S(1)}, u32[]{:S(2)}, u32[]{:S(2)}) collective-permute-start(f32[128,128]{1,0:T(8,128)S(1)} %add.109), channel_id=1, source_target_pairs={{0,2},{1,3},{2,4},{3,5},{4,6},{5,7},{6,0},{7,1},{8,10},{9,11},{10,... | collective-permute-start | bytes 196616 | tf_op jit(solution)/shard_map/ppermute | solution.py:288
  135.2 4.6 %collective-permute-start.17 = (f32[128,128]{1,0:T(8,128)S(1)}, f32[128,128]{1,0:T(8,128)S(1)}, u32[]{:S(2)}, u32[]{:S(2)}) collective-permute-start(f32[128,128]{1,0:T(8,128)S(1)} %add.113), channel_id=1, source_target_pairs={{0,4},{1,5},{2,6},{3,7},{4,0},{5,1},{6,2},{7,3},{8,12},{9,13},{10,... | collective-permute-start | bytes 196616 | tf_op jit(solution)/shard_map/ppermute | solution.py:288
  135.8 6.0 %collective-permute-start.16 = (f32[128,128]{1,0:T(8,128)S(1)}, f32[128,128]{1,0:T(8,128)S(1)}, u32[]{:S(2)}, u32[]{:S(2)}) collective-permute-start(f32[128,128]{1,0:T(8,128)S(1)} %add.113), channel_id=1, source_target_pairs={{0,2},{1,3},{2,4},{3,5},{4,6},{5,7},{6,0},{7,1},{8,10},{9,11},{10,... | collective-permute-start | bytes 196616 | tf_op jit(solution)/shard_map/ppermute | solution.py:288
  166.9 3.5 %collective-permute-start.20 = (f32[128,128]{1,0:T(8,128)S(1)}, f32[128,128]{1,0:T(8,128)S(1)}, u32[]{:S(2)}, u32[]{:S(2)}) collective-permute-start(f32[128,128]{1,0:T(8,128)S(1)} %get-tuple-element.109), channel_id=1, source_target_pairs={{0,1},{1,0},{2,3},{3,2},{4,5},{5,4},{6,7},{7,6},{8,9},{9,8},{10,11... | collective-permute-start | bytes 196616 | tf_op jit(solution)/shard_map/ppermute | solution.py:282
  171.8 4.7 %collective-permute-start.22 = (f32[128,128]{1,0:T(8,128)S(1)}, f32[128,128]{1,0:T(8,128)S(1)}, u32[]{:S(2)}, u32[]{:S(2)}) collective-permute-start(f32[128,128]{1,0:T(8,128)S(1)} %add.117), channel_id=1, source_target_pairs={{0,4},{1,5},{2,6},{3,7},{4,0},{5,1},{6,2},{7,3},{8,12},{9,13},{10,... | collective-permute-start | bytes 196616 | tf_op jit(solution)/shard_map/ppermute | solution.py:288
  172.4 5.3 %collective-permute-start.21 = (f32[128,128]{1,0:T(8,128)S(1)}, f32[128,128]{1,0:T(8,128)S(1)}, u32[]{:S(2)}, u32[]{:S(2)}) collective-permute-start(f32[128,128]{1,0:T(8,128)S(1)} %add.117), channel_id=1, source_target_pairs={{0,2},{1,3},{2,4},{3,5},{4,6},{5,7},{6,0},{7,1},{8,10},{9,11},{10,... | collective-permute-start | bytes 196616 | tf_op jit(solution)/shard_map/ppermute | solution.py:288
  177.8 4.1 %collective-permute-start.24 = (f32[128,128]{1,0:T(8,128)S(1)}, f32[128,128]{1,0:T(8,128)S(1)}, u32[]{:S(2)}, u32[]{:S(2)}) collective-permute-start(f32[128,128]{1,0:T(8,128)S(1)} %add_add_fusion.3.mine_ref), channel_id=1, source_target_pairs={{0,1},{1,0},{2,3},{3,2},{4,5},{5,4},{6,7},{7,6},{8,9},{9,8},{10,11... | collective-permute-start | bytes 196616 | tf_op jit(solution)/shard_map/ppermute | solution.py:282
  207.8 4.6 %collective-permute-start.27 = (f32[128,128]{1,0:T(8,128)S(1)}, f32[128,128]{1,0:T(8,128)S(1)}, u32[]{:S(2)}, u32[]{:S(2)}) collective-permute-start(f32[128,128]{1,0:T(8,128)S(1)} %add.121), channel_id=1, source_target_pairs={{0,4},{1,5},{2,6},{3,7},{4,0},{5,1},{6,2},{7,3},{8,12},{9,13},{10,... | collective-permute-start | bytes 196616 | tf_op jit(solution)/shard_map/ppermute | solution.py:288
  208.4 6.0 %collective-permute-start.26 = (f32[128,128]{1,0:T(8,128)S(1)}, f32[128,128]{1,0:T(8,128)S(1)}, u32[]{:S(2)}, u32[]{:S(2)}) collective-permute-start(f32[128,128]{1,0:T(8,128)S(1)} %add.121), channel_id=1, source_target_pairs={{0,2},{1,3},{2,4},{3,5},{4,6},{5,7},{6,0},{7,1},{8,10},{9,11},{10,... | collective-permute-start | bytes 196616 | tf_op jit(solution)/shard_map/ppermute | solution.py:288
  214.4 3.8 %collective-permute-start.29 = (f32[128,128]{1,0:T(8,128)S(1)}, f32[128,128]{1,0:T(8,128)S(1)}, u32[]{:S(2)}, u32[]{:S(2)}) collective-permute-start(f32[128,128]{1,0:T(8,128)S(1)} %add_add_fusion.2.mine_ref), channel_id=1, source_target_pairs={{0,1},{1,0},{2,3},{3,2},{4,5},{5,4},{6,7},{7,6},{8,9},{9,8},{10,11... | collective-permute-start | bytes 196616 | tf_op jit(solution)/shard_map/ppermute | solution.py:282
  245.0 4.7 %collective-permute-start.32 = (f32[128,128]{1,0:T(8,128)S(1)}, f32[128,128]{1,0:T(8,128)S(1)}, u32[]{:S(2)}, u32[]{:S(2)}) collective-permute-start(f32[128,128]{1,0:T(8,128)S(1)} %add.125), channel_id=1, source_target_pairs={{0,4},{1,5},{2,6},{3,7},{4,0},{5,1},{6,2},{7,3},{8,12},{9,13},{10,... | collective-permute-start | bytes 196616 | tf_op jit(solution)/shard_map/ppermute | solution.py:288
  245.6 5.3 %collective-permute-start.31 = (f32[128,128]{1,0:T(8,128)S(1)}, f32[128,128]{1,0:T(8,128)S(1)}, u32[]{:S(2)}, u32[]{:S(2)}) collective-permute-start(f32[128,128]{1,0:T(8,128)S(1)} %add.125), channel_id=1, source_target_pairs={{0,2},{1,3},{2,4},{3,5},{4,6},{5,7},{6,0},{7,1},{8,10},{9,11},{10,... | collective-permute-start | bytes 196616 | tf_op jit(solution)/shard_map/ppermute | solution.py:288
  251.0 4.8 %collective-permute-start.34 = (f32[128,128]{1,0:T(8,128)S(1)}, f32[128,128]{1,0:T(8,128)S(1)}, u32[]{:S(2)}, u32[]{:S(2)}) collective-permute-start(f32[128,128]{1,0:T(8,128)S(1)} %add_add_fusion.1.mine_ref), channel_id=1, source_target_pairs={{0,1},{1,0},{2,3},{3,2},{4,5},{5,4},{6,7},{7,6},{8,9},{9,8},{10,11... | collective-permute-start | bytes 196616 | tf_op jit(solution)/shard_map/ppermute | solution.py:282
  277.8 3.5 %collective-permute-start.35 = (f32[128,128]{1,0:T(8,128)S(1)}, f32[128,128]{1,0:T(8,128)S(1)}, u32[]{:S(2)}, u32[]{:S(2)}) collective-permute-start(f32[128,128]{1,0:T(8,128)S(1)} %get-tuple-element.133), channel_id=1, source_target_pairs={{0,1},{1,0},{2,3},{3,2},{4,5},{5,4},{6,7},{7,6},{8,9},{9,8},{10,11... | collective-permute-start | bytes 196616 | tf_op jit(solution)/shard_map/ppermute | solution.py:282
  281.7 4.6 %collective-permute-start.37 = (f32[128,128]{1,0:T(8,128)S(1)}, f32[128,128]{1,0:T(8,128)S(1)}, u32[]{:S(2)}, u32[]{:S(2)}) collective-permute-start(f32[128,128]{1,0:T(8,128)S(1)} %add.129), channel_id=1, source_target_pairs={{0,4},{1,5},{2,6},{3,7},{4,0},{5,1},{6,2},{7,3},{8,12},{9,13},{10,... | collective-permute-start | bytes 196616 | tf_op jit(solution)/shard_map/ppermute | solution.py:288
  282.3 6.0 %collective-permute-start.36 = (f32[128,128]{1,0:T(8,128)S(1)}, f32[128,128]{1,0:T(8,128)S(1)}, u32[]{:S(2)}, u32[]{:S(2)}) collective-permute-start(f32[128,128]{1,0:T(8,128)S(1)} %add.129), channel_id=1, source_target_pairs={{0,2},{1,3},{2,4},{3,5},{4,6},{5,7},{6,0},{7,1},{8,10},{9,11},{10,... | collective-permute-start | bytes 196616 | tf_op jit(solution)/shard_map/ppermute | solution.py:288
  (19 other events, 55.1 us)

commit v4 on v3

--- a/solution.py
+++ b/solution.py
@@ -38,7 +38,7 @@
 
 
 def pick_kernel(
-    stride_hbm, counts_hbm, source_hbm, target_ref, field_hbm, nu_hbm,
+    core_ref, stride_hbm, counts_hbm, source_hbm, target_ref, field_hbm, nu_hbm,
     out_ref, targets_ref, stride_ref, counts_ref, source_ref, field, nu, sems,
 ):
     cells = nu.shape[1]
@@ -73,7 +73,7 @@
             out_ref[grid_row, pl.ds(slot, 1), :] = jnp.where(slot < live, swept, 0.0)
 
 
-def pick(sub_field, reluctivity, stride, counts, source_cell, target_row):
+def pick(core, sub_field, reluctivity, stride, counts, source_cell, target_row):
     cells, rotor = sub_field.shape
     _, grid_rows, slots = source_cell.shape
     pad = 512
@@ -83,7 +83,7 @@
             jax.ShapeDtypeStruct((grid_rows, slots, rotor), F32),
             jax.ShapeDtypeStruct((1, target_row.size), jnp.int32),
         ],
-        in_specs=[HBM, HBM, HBM, VMEM, HBM, HBM],
+        in_specs=[SMEM, HBM, HBM, HBM, VMEM, HBM, HBM],
         out_specs=[VMEM, VMEM],
         scratch_shapes=[
             pltpu.SMEM(stride.shape, jnp.int32),
@@ -95,7 +95,7 @@
         ],
         compiler_params=kernel_params(PICK_LIMIT),
         name="pick",
-    )(stride, counts, source_cell, target_row, sub_field, reluctivity)
+    )(core, stride, counts, source_cell, target_row, sub_field, reluctivity)
 
 
 def interface_rows(block, rows, targets_ref, received_ref):
@@ -306,7 +306,7 @@
     peers = lax.axis_size("row")
     core = (lax.axis_index("col") % 2).astype(jnp.int32).reshape(1)
     picked, targets = pick(
-        sub_field, reluctivity, stride, counts, source_cell, target_row[0, 0]
+        core, sub_field, reluctivity, stride, counts, source_cell, target_row[0, 0]
     )
     received = per_row(picked).reshape(-1, rotor)
 
@@ -317,8 +317,11 @@
         mine = total_along_x(mine + other_core(theirs))
         if block + 1 < blocks:
             last = block if block + 2 < blocks else block + 1
-            started, lower_high, lower_low, *diags = fold(
+            folded = fold(
                 block + 1, block, last, targets, received, lower_tiles, diag_inverse, shares
+            )
+            mine, (started, lower_high, lower_low, *diags) = lax.optimization_barrier(
+                (mine, folded)
             )
         diag_high, diag_low, *diags = diags
         partial = diag_product(core, mine, other_core(mine), diag_high, diag_low)

time: 303 us -> 293 us (0.967)
  waiting for transfers between devices: 57.4 us -> 39.1 us
  blocking collectives: 160 us -> 175 us
  starting transfers between devices: 55.6 us -> 49.1 us
    ppermute x24, waiting for transfers between devices: 41.7 us -> 24.7 us  [total_along_x(): lax.ppermute(value, 'col', [(i, (i + hop) % peers) for i in range(peers)])]
    all_to_all x15 -> x16, blocking collectives: 160 us -> 175 us  [per_row(): return lax.all_to_all(value, 'row', 0, 0, tiled=True)]
    all_to_all x1 -> x0, starting transfers between devices: 8.61 us -> none  [per_row(): return lax.all_to_all(value, 'row', 0, 0, tiled=True)]
    all_to_all x1 -> x0, waiting for transfers between devices: 7.53 us -> none  [per_row(): return lax.all_to_all(value, 'row', 0, 0, tiled=True)]
    ppermute x16, waiting for transfers between devices: 8.14 us -> 14.4 us  [other_core(): return lax.ppermute(value, 'col', [(i, i ^ 1) for i in range(peers)])]
  transfers between devices with their start and end apart: 41 -> 40, of which waited for: 34 -> 33; matrix products, arithmetic and copies ran while one was open for 0% -> 0% of each run, Pallas kernels for 5% -> 5%
where the time goes in v4:
time: 293 us; the launch traced here: 292 us
  blocking collectives  175 us (60%)
  starting transfers between devices  49.1 us (17%)
  waiting for transfers between devices  39.1 us (13%)
  Pallas kernels  26.3 us (9%)
    all_to_all x16, blocking collectives, per_row(): return lax.all_to_all(value, 'row', 0, 0, tiled=True)  175 us
    ppermute x16, starting transfers between devices, other_core(): return lax.ppermute(value, 'col', [(i, i ^ 1) for i in range(peers)])  32.2 us
    ppermute x24, waiting for transfers between devices, total_along_x(): lax.ppermute(value, 'col', [(i, (i + hop) % peers) for i in range(peers)])  24.7 us
    ppermute x24, starting transfers between devices, total_along_x(): lax.ppermute(value, 'col', [(i, (i + hop) % peers) for i in range(peers)])  16.9 us
    pallas_call x7, Pallas kernels, fold(): pl.pallas_call(functools.partial(fold_kernel, block, first, last), out_sh...  15.6 us
    ppermute x16, waiting for transfers between devices, other_core(): return lax.ppermute(value, 'col', [(i, i ^ 1) for i in range(peers)])  14.4 us
  transfers between devices with their start and end apart: 40, of which 33 were waited for; matrix products, arithmetic and copies ran while one was open for 0% of the time, Pallas kernels for 5%

profile of v4, /device:TPU:1, one launch (start us, length us, event | category | flops | bytes accessed | tf_op | source)
XLA Modules:
  0.0 291.9 jit_solution(3758702924418872664)
XLA Ops:
  0.7 4.9 %pick.1 = (f32[16,32,128]{2,1,0:T(8,128)}, s32[1,512]{1,0:T(1,128)}) custom-call(s32[1]{0:T(128)} %bitcast.core_ref, s32[1]{0:T(128)S(6)} %copy.10.stride_hbm, s32[1,16]{1,0:T(1,128)} %counts_hbm.1, s32[1,16,32]{2,1,0:T(8,128)} %source_hbm.1, s32[16,32]{1,0:T(8,128)} %bitcast.65, f32[2048,128]{1,0:T(8,128)} %field_hbm.1, f32[2,2048,128]{2,1,0:T(8,128)} %nu_hbm.1), custom_call_target="tpu_custom_call" | custom-call | tf_op jit(solution)/shard_map/pick/pallas_call | solution.py:80
  5.5 16.2 %all_to_all.80 = f32[16,32,128]{2,1,0:T(8,128)S(1)} all-to-all(f32[16,32,128]{2,1,0:T(8,128)} %get-tuple-element.119), channel_id=1, replica_groups=mesh['row'=16,'col'=8] {'row'}, dimensions={0} | all-to-all | bytes 524288 | tf_op jit(solution)/shard_map/all_to_all | solution.py:297
  37.1 10.8 %all_to_all.81.parts_ref = f32[16,32,128]{2,1,0:T(8,128)S(1)} all-to-all(f32[16,32,128]{2,1,0:T(8,128)S(1)} %bitcast.58), channel_id=1, replica_groups=mesh['row'=16,'col'=8] {'row'}, dimensions={0} | all-to-all | bytes 524288 | tf_op jit(solution)/shard_map/all_to_all | solution.py:297
  47.9 10.4 %all_to_all.82 = f32[16,32,128]{2,1,0:T(8,128)S(1)} all-to-all(f32[16,32,128]{2,1,0:T(8,128)S(1)} %get-tuple-element.130), channel_id=1, replica_groups=mesh['row'=16,'col'=8] {'row'}, dimensions={0} | all-to-all | bytes 524288 | tf_op jit(solution)/shard_map/all_to_all | solution.py:297
  58.6 2.8 collective-permute-start.5
  71.4 10.8 %all_to_all.83.parts_ref = f32[16,32,128]{2,1,0:T(8,128)S(1)} all-to-all(f32[16,32,128]{2,1,0:T(8,128)S(1)} %bitcast.59), channel_id=1, replica_groups=mesh['row'=16,'col'=8] {'row'}, dimensions={0} | all-to-all | bytes 524288 | tf_op jit(solution)/shard_map/all_to_all | solution.py:297
  82.2 10.4 %all_to_all.84 = f32[16,32,128]{2,1,0:T(8,128)S(1)} all-to-all(f32[16,32,128]{2,1,0:T(8,128)S(1)} %get-tuple-element.144), channel_id=1, replica_groups=mesh['row'=16,'col'=8] {'row'}, dimensions={0} | all-to-all | bytes 524288 | tf_op jit(solution)/shard_map/all_to_all | solution.py:297
  92.9 2.8 collective-permute-start.10
  106.7 10.8 %all_to_all.85.parts_ref = f32[16,32,128]{2,1,0:T(8,128)S(1)} all-to-all(f32[16,32,128]{2,1,0:T(8,128)S(1)} %bitcast.60), channel_id=1, replica_groups=mesh['row'=16,'col'=8] {'row'}, dimensions={0} | all-to-all | bytes 524288 | tf_op jit(solution)/shard_map/all_to_all | solution.py:297
  117.5 10.4 %all_to_all.86 = f32[16,32,128]{2,1,0:T(8,128)S(1)} all-to-all(f32[16,32,128]{2,1,0:T(8,128)S(1)} %get-tuple-element.158), channel_id=1, replica_groups=mesh['row'=16,'col'=8] {'row'}, dimensions={0} | all-to-all | bytes 524288 | tf_op jit(solution)/shard_map/all_to_all | solution.py:297
  128.2 2.8 collective-permute-start.15
  141.0 10.8 %all_to_all.87.parts_ref = f32[16,32,128]{2,1,0:T(8,128)S(1)} all-to-all(f32[16,32,128]{2,1,0:T(8,128)S(1)} %bitcast.61), channel_id=1, replica_groups=mesh['row'=16,'col'=8] {'row'}, dimensions={0} | all-to-all | bytes 524288 | tf_op jit(solution)/shard_map/all_to_all | solution.py:297
  151.8 10.4 %all_to_all.88 = f32[16,32,128]{2,1,0:T(8,128)S(1)} all-to-all(f32[16,32,128]{2,1,0:T(8,128)S(1)} %get-tuple-element.172), channel_id=1, replica_groups=mesh['row'=16,'col'=8] {'row'}, dimensions={0} | all-to-all | bytes 524288 | tf_op jit(solution)/shard_map/all_to_all | solution.py:297
  162.5 2.8 collective-permute-start.20
  176.3 10.8 %all_to_all.89.parts_ref = f32[16,32,128]{2,1,0:T(8,128)S(1)} all-to-all(f32[16,32,128]{2,1,0:T(8,128)S(1)} %bitcast.62), channel_id=1, replica_groups=mesh['row'=16,'col'=8] {'row'}, dimensions={0} | all-to-all | bytes 524288 | tf_op jit(solution)/shard_map/all_to_all | solution.py:297
  187.1 10.4 %all_to_all.90 = f32[16,32,128]{2,1,0:T(8,128)S(1)} all-to-all(f32[16,32,128]{2,1,0:T(8,128)S(1)} %get-tuple-element.186), channel_id=1, replica_groups=mesh['row'=16,'col'=8] {'row'}, dimensions={0} | all-to-all | bytes 524288 | tf_op jit(solution)/shard_map/all_to_all | solution.py:297
  197.8 2.8 collective-permute-start.25
  203.2 2.8 fold.12
  210.7 10.8 %all_to_all.91.parts_ref = f32[16,32,128]{2,1,0:T(8,128)S(1)} all-to-all(f32[16,32,128]{2,1,0:T(8,128)S(1)} %bitcast.63), channel_id=1, replica_groups=mesh['row'=16,'col'=8] {'row'}, dimensions={0} | all-to-all | bytes 524288 | tf_op jit(solution)/shard_map/all_to_all | solution.py:297
  221.5 10.4 %all_to_all.92 = f32[16,32,128]{2,1,0:T(8,128)S(1)} all-to-all(f32[16,32,128]{2,1,0:T(8,128)S(1)} %get-tuple-element.200), channel_id=1, replica_groups=mesh['row'=16,'col'=8] {'row'}, dimensions={0} | all-to-all | bytes 524288 | tf_op jit(solution)/shard_map/all_to_all | solution.py:297
  238.2 3.2 %fold.13 = (f32[256,128]{1,0:T(8,128)S(1)}, bf16[256,512]{1,0:T(8,128)(2,1)S(1)}, bf16[256,512]{1,0:T(8,128)(2,1)S(1)}, bf16[512,256]{1,0:T(8,128)(2,1)S(1)}, bf...) custom-call(s32[1,512]{1,0:T(1,128)S(1)} %copy-done.1, ...), custom_call_target="tpu_custom_call" | custom-call | flops 704643072 | bytes 4718592 | tf_op jit(solution)/shard_map/fold/pallas_call | solution.py:182
  246.0 10.8 %all_to_all.93.parts_ref = f32[16,32,128]{2,1,0:T(8,128)S(1)} all-to-all(f32[16,32,128]{2,1,0:T(8,128)S(1)} %bitcast.64), channel_id=1, replica_groups=mesh['row'=16,'col'=8] {'row'}, dimensions={0} | all-to-all | bytes 524288 | tf_op jit(solution)/shard_map/all_to_all | solution.py:297
  256.8 10.4 %all_to_all.94 = f32[16,32,128]{2,1,0:T(8,128)S(1)} all-to-all(f32[16,32,128]{2,1,0:T(8,128)S(1)} %get-tuple-element.216), channel_id=1, replica_groups=mesh['row'=16,'col'=8] {'row'}, dimensions={0} | all-to-all | bytes 524288 | tf_op jit(solution)/shard_map/all_to_all | solution.py:297
  280.5 10.8 %all_to_all.95.parts_ref = f32[16,32,128]{2,1,0:T(8,128)S(1)} all-to-all(f32[16,32,128]{2,1,0:T(8,128)S(1)} %bitcast.57), channel_id=1, replica_groups=mesh['row'=16,'col'=8] {'row'}, dimensions={0} | all-to-all | bytes 524288 | tf_op jit(solution)/shard_map/all_to_all | solution.py:297
  (124 shorter events, 91.2 us)
Async XLA Ops:
  25.8 5.8 %collective-permute-start.3 = (f32[128,128]{1,0:T(8,128)S(1)}, f32[128,128]{1,0:T(8,128)S(1)}, u32[]{:S(2)}, u32[]{:S(2)}) collective-permute-start(f32[128,128]{1,0:T(8,128)S(1)} %add.101), channel_id=1, source_target_pairs={{0,6},{1,7},{2,0},{3,1},{4,2},{5,3},{6,4},{7,5},{8,14},{9,15},{10,... | collective-permute-start | bytes 196616 | tf_op jit(solution)/shard_map/ppermute | solution.py:288
  28.4 4.7 %collective-permute-start.2 = (f32[128,128]{1,0:T(8,128)S(1)}, f32[128,128]{1,0:T(8,128)S(1)}, u32[]{:S(2)}, u32[]{:S(2)}) collective-permute-start(f32[128,128]{1,0:T(8,128)S(1)} %add.101), channel_id=1, source_target_pairs={{0,4},{1,5},{2,6},{3,7},{4,0},{5,1},{6,2},{7,3},{8,12},{9,13},{10,... | collective-permute-start | bytes 196616 | tf_op jit(solution)/shard_map/ppermute | solution.py:288
  28.9 5.5 %collective-permute-start.1 = (f32[128,128]{1,0:T(8,128)S(1)}, f32[128,128]{1,0:T(8,128)S(1)}, u32[]{:S(2)}, u32[]{:S(2)}) collective-permute-start(f32[128,128]{1,0:T(8,128)S(1)} %add.101), channel_id=1, source_target_pairs={{0,2},{1,3},{2,4},{3,5},{4,6},{5,7},{6,0},{7,1},{8,10},{9,11},{10,... | collective-permute-start | bytes 196616 | tf_op jit(solution)/shard_map/ppermute | solution.py:288
  58.6 3.7 %collective-permute-start.5 = (f32[128,128]{1,0:T(8,128)S(1)}, f32[128,128]{1,0:T(8,128)S(1)}, u32[]{:S(2)}, u32[]{:S(2)}) collective-permute-start(f32[128,128]{1,0:T(8,128)S(1)} %get-tuple-element.135), channel_id=1, source_target_pairs={{0,1},{1,0},{2,3},{3,2},{4,5},{5,4},{6,7},{7,6},{8,9},{9,8},{10,11... | collective-permute-start | bytes 196616 | tf_op jit(solution)/shard_map/ppermute | solution.py:282
  62.6 4.6 %collective-permute-start.7 = (f32[128,128]{1,0:T(8,128)S(1)}, f32[128,128]{1,0:T(8,128)S(1)}, u32[]{:S(2)}, u32[]{:S(2)}) collective-permute-start(f32[128,128]{1,0:T(8,128)S(1)} %add.105), channel_id=1, source_target_pairs={{0,4},{1,5},{2,6},{3,7},{4,0},{5,1},{6,2},{7,3},{8,12},{9,13},{10,... | collective-permute-start | bytes 196616 | tf_op jit(solution)/shard_map/ppermute | solution.py:288
  63.2 6.0 %collective-permute-start.6 = (f32[128,128]{1,0:T(8,128)S(1)}, f32[128,128]{1,0:T(8,128)S(1)}, u32[]{:S(2)}, u32[]{:S(2)}) collective-permute-start(f32[128,128]{1,0:T(8,128)S(1)} %add.105), channel_id=1, source_target_pairs={{0,2},{1,3},{2,4},{3,5},{4,6},{5,7},{6,0},{7,1},{8,10},{9,11},{10,... | collective-permute-start | bytes 196616 | tf_op jit(solution)/shard_map/ppermute | solution.py:288
  92.9 3.7 %collective-permute-start.10 = (f32[128,128]{1,0:T(8,128)S(1)}, f32[128,128]{1,0:T(8,128)S(1)}, u32[]{:S(2)}, u32[]{:S(2)}) collective-permute-start(f32[128,128]{1,0:T(8,128)S(1)} %get-tuple-element.149), channel_id=1, source_target_pairs={{0,1},{1,0},{2,3},{3,2},{4,5},{5,4},{6,7},{7,6},{8,9},{9,8},{10,11... | collective-permute-start | bytes 196616 | tf_op jit(solution)/shard_map/ppermute | solution.py:282
  96.6 4.0 %collective-permute-start.13 = (f32[128,128]{1,0:T(8,128)S(1)}, f32[128,128]{1,0:T(8,128)S(1)}, u32[]{:S(2)}, u32[]{:S(2)}) collective-permute-start(f32[128,128]{1,0:T(8,128)S(1)} %add.109), channel_id=1, source_target_pairs={{0,6},{1,7},{2,0},{3,1},{4,2},{5,3},{6,4},{7,5},{8,14},{9,15},{10,... | collective-permute-start | bytes 196616 | tf_op jit(solution)/shard_map/ppermute | solution.py:288
  98.0 4.7 %collective-permute-start.12 = (f32[128,128]{1,0:T(8,128)S(1)}, f32[128,128]{1,0:T(8,128)S(1)}, u32[]{:S(2)}, u32[]{:S(2)}) collective-permute-start(f32[128,128]{1,0:T(8,128)S(1)} %add.109), channel_id=1, source_target_pairs={{0,4},{1,5},{2,6},{3,7},{4,0},{5,1},{6,2},{7,3},{8,12},{9,13},{10,... | collective-permute-start | bytes 196616 | tf_op jit(solution)/shard_map/ppermute | solution.py:288
  98.6 5.4 %collective-permute-start.11 = (f32[128,128]{1,0:T(8,128)S(1)}, f32[128,128]{1,0:T(8,128)S(1)}, u32[]{:S(2)}, u32[]{:S(2)}) collective-permute-start(f32[128,128]{1,0:T(8,128)S(1)} %add.109), channel_id=1, source_target_pairs={{0,2},{1,3},{2,4},{3,5},{4,6},{5,7},{6,0},{7,1},{8,10},{9,11},{10,... | collective-permute-start | bytes 196616 | tf_op jit(solution)/shard_map/ppermute | solution.py:288
  131.9 3.9 %collective-permute-start.18 = (f32[128,128]{1,0:T(8,128)S(1)}, f32[128,128]{1,0:T(8,128)S(1)}, u32[]{:S(2)}, u32[]{:S(2)}) collective-permute-start(f32[128,128]{1,0:T(8,128)S(1)} %add.113), channel_id=1, source_target_pairs={{0,6},{1,7},{2,0},{3,1},{4,2},{5,3},{6,4},{7,5},{8,14},{9,15},{10,... | collective-permute-start | bytes 196616 | tf_op jit(solution)/shard_map/ppermute | solution.py:288
  132.3 4.6 %collective-permute-start.17 = (f32[128,128]{1,0:T(8,128)S(1)}, f32[128,128]{1,0:T(8,128)S(1)}, u32[]{:S(2)}, u32[]{:S(2)}) collective-permute-start(f32[128,128]{1,0:T(8,128)S(1)} %add.113), channel_id=1, source_target_pairs={{0,4},{1,5},{2,6},{3,7},{4,0},{5,1},{6,2},{7,3},{8,12},{9,13},{10,... | collective-permute-start | bytes 196616 | tf_op jit(solution)/shard_map/ppermute | solution.py:288
  132.9 6.0 %collective-permute-start.16 = (f32[128,128]{1,0:T(8,128)S(1)}, f32[128,128]{1,0:T(8,128)S(1)}, u32[]{:S(2)}, u32[]{:S(2)}) collective-permute-start(f32[128,128]{1,0:T(8,128)S(1)} %add.113), channel_id=1, source_target_pairs={{0,2},{1,3},{2,4},{3,5},{4,6},{5,7},{6,0},{7,1},{8,10},{9,11},{10,... | collective-permute-start | bytes 196616 | tf_op jit(solution)/shard_map/ppermute | solution.py:288
  166.2 4.6 %collective-permute-start.23 = (f32[128,128]{1,0:T(8,128)S(1)}, f32[128,128]{1,0:T(8,128)S(1)}, u32[]{:S(2)}, u32[]{:S(2)}) collective-permute-start(f32[128,128]{1,0:T(8,128)S(1)} %add.117), channel_id=1, source_target_pairs={{0,6},{1,7},{2,0},{3,1},{4,2},{5,3},{6,4},{7,5},{8,14},{9,15},{10,... | collective-permute-start | bytes 196616 | tf_op jit(solution)/shard_map/ppermute | solution.py:288
  167.6 4.7 %collective-permute-start.22 = (f32[128,128]{1,0:T(8,128)S(1)}, f32[128,128]{1,0:T(8,128)S(1)}, u32[]{:S(2)}, u32[]{:S(2)}) collective-permute-start(f32[128,128]{1,0:T(8,128)S(1)} %add.117), channel_id=1, source_target_pairs={{0,4},{1,5},{2,6},{3,7},{4,0},{5,1},{6,2},{7,3},{8,12},{9,13},{10,... | collective-permute-start | bytes 196616 | tf_op jit(solution)/shard_map/ppermute | solution.py:288
  168.2 5.3 %collective-permute-start.21 = (f32[128,128]{1,0:T(8,128)S(1)}, f32[128,128]{1,0:T(8,128)S(1)}, u32[]{:S(2)}, u32[]{:S(2)}) collective-permute-start(f32[128,128]{1,0:T(8,128)S(1)} %add.117), channel_id=1, source_target_pairs={{0,2},{1,3},{2,4},{3,5},{4,6},{5,7},{6,0},{7,1},{8,10},{9,11},{10,... | collective-permute-start | bytes 196616 | tf_op jit(solution)/shard_map/ppermute | solution.py:288
  201.5 4.5 %collective-permute-start.28 = (f32[128,128]{1,0:T(8,128)S(1)}, f32[128,128]{1,0:T(8,128)S(1)}, u32[]{:S(2)}, u32[]{:S(2)}) collective-permute-start(f32[128,128]{1,0:T(8,128)S(1)} %add.121), channel_id=1, source_target_pairs={{0,6},{1,7},{2,0},{3,1},{4,2},{5,3},{6,4},{7,5},{8,14},{9,15},{10,... | collective-permute-start | bytes 196616 | tf_op jit(solution)/shard_map/ppermute | solution.py:288
  202.0 4.6 %collective-permute-start.27 = (f32[128,128]{1,0:T(8,128)S(1)}, f32[128,128]{1,0:T(8,128)S(1)}, u32[]{:S(2)}, u32[]{:S(2)}) collective-permute-start(f32[128,128]{1,0:T(8,128)S(1)} %add.121), channel_id=1, source_target_pairs={{0,4},{1,5},{2,6},{3,7},{4,0},{5,1},{6,2},{7,3},{8,12},{9,13},{10,... | collective-permute-start | bytes 196616 | tf_op jit(solution)/shard_map/ppermute | solution.py:288
  202.5 6.0 %collective-permute-start.26 = (f32[128,128]{1,0:T(8,128)S(1)}, f32[128,128]{1,0:T(8,128)S(1)}, u32[]{:S(2)}, u32[]{:S(2)}) collective-permute-start(f32[128,128]{1,0:T(8,128)S(1)} %add.121), channel_id=1, source_target_pairs={{0,2},{1,3},{2,4},{3,5},{4,6},{5,7},{6,0},{7,1},{8,10},{9,11},{10,... | collective-permute-start | bytes 196616 | tf_op jit(solution)/shard_map/ppermute | solution.py:288
  235.9 5.5 %collective-permute-start.33 = (f32[128,128]{1,0:T(8,128)S(1)}, f32[128,128]{1,0:T(8,128)S(1)}, u32[]{:S(2)}, u32[]{:S(2)}) collective-permute-start(f32[128,128]{1,0:T(8,128)S(1)} %add.125), channel_id=1, source_target_pairs={{0,6},{1,7},{2,0},{3,1},{4,2},{5,3},{6,4},{7,5},{8,14},{9,15},{10,... | collective-permute-start | bytes 196616 | tf_op jit(solution)/shard_map/ppermute | solution.py:288
  237.2 4.7 %collective-permute-start.32 = (f32[128,128]{1,0:T(8,128)S(1)}, f32[128,128]{1,0:T(8,128)S(1)}, u32[]{:S(2)}, u32[]{:S(2)}) collective-permute-start(f32[128,128]{1,0:T(8,128)S(1)} %add.125), channel_id=1, source_target_pairs={{0,4},{1,5},{2,6},{3,7},{4,0},{5,1},{6,2},{7,3},{8,12},{9,13},{10,... | collective-permute-start | bytes 196616 | tf_op jit(solution)/shard_map/ppermute | solution.py:288
  237.9 5.3 %collective-permute-start.31 = (f32[128,128]{1,0:T(8,128)S(1)}, f32[128,128]{1,0:T(8,128)S(1)}, u32[]{:S(2)}, u32[]{:S(2)}) collective-permute-start(f32[128,128]{1,0:T(8,128)S(1)} %add.125), channel_id=1, source_target_pairs={{0,2},{1,3},{2,4},{3,5},{4,6},{5,7},{6,0},{7,1},{8,10},{9,11},{10,... | collective-permute-start | bytes 196616 | tf_op jit(solution)/shard_map/ppermute | solution.py:288
  271.6 4.6 %collective-permute-start.37 = (f32[128,128]{1,0:T(8,128)S(1)}, f32[128,128]{1,0:T(8,128)S(1)}, u32[]{:S(2)}, u32[]{:S(2)}) collective-permute-start(f32[128,128]{1,0:T(8,128)S(1)} %add.129), channel_id=1, source_target_pairs={{0,4},{1,5},{2,6},{3,7},{4,0},{5,1},{6,2},{7,3},{8,12},{9,13},{10,... | collective-permute-start | bytes 196616 | tf_op jit(solution)/shard_map/ppermute | solution.py:288
  272.7 5.1 %collective-permute-start.36 = (f32[128,128]{1,0:T(8,128)S(1)}, f32[128,128]{1,0:T(8,128)S(1)}, u32[]{:S(2)}, u32[]{:S(2)}) collective-permute-start(f32[128,128]{1,0:T(8,128)S(1)} %add.129), channel_id=1, source_target_pairs={{0,2},{1,3},{2,4},{3,5},{4,6},{5,7},{6,0},{7,1},{8,10},{9,11},{10,... | collective-permute-start | bytes 196616 | tf_op jit(solution)/shard_map/ppermute | solution.py:288
  (18 other events, 47.0 us)

commit v5 on v4

v5 whole, which is shorter than its diff:
```python
import functools

import jax
import jax.numpy as jnp
from jax import lax
from jax.experimental import pallas as pl
from jax.experimental.pallas import tpu as pltpu
from jax.sharding import PartitionSpec as P

F32 = jnp.float32
BF16 = jnp.bfloat16
VMEM_LIMIT = 32 * 1024 * 1024
WIDE_LIMIT = 50 * 1024 * 1024
PICK_LIMIT = 54 * 1024 * 1024
VMEM = pl.BlockSpec(memory_space=pltpu.VMEM)
SMEM = pl.BlockSpec(memory_space=pltpu.SMEM)
HBM = pl.BlockSpec(memory_space=pltpu.HBM)


def kernel_params(limit=VMEM_LIMIT):
    return pltpu.CompilerParams(vmem_limit_bytes=limit)


def dot(left, right):
    return jnp.dot(left, right, preferred_element_type=F32)


def split(value):
    high = value.astype(BF16)
    return high, (value - high.astype(F32)).astype(BF16)


def split_product(left_high, left_low, right):
    width = right.shape[1]
    high, low = split(right)
    both = dot(left_high, jnp.concatenate([high, low], axis=1))
    return both[:, :width] + both[:, width:] + dot(left_low, high)


def pick_kernel(
    core_ref, stride_hbm, counts_hbm, source_hbm, target_ref, field_hbm, nu_hbm,
    out_ref, targets_ref, stride_ref, counts_ref, source_ref, field, nu, sems,
):
    cells = nu.shape[1]
    pad = field.shape[0] - cells
    loads = [
        pltpu.make_async_copy(stride_hbm, stride_ref, sems.at[2]),
        pltpu.make_async_copy(counts_hbm, counts_ref, sems.at[3]),
        pltpu.make_async_copy(source_hbm, source_ref, sems.at[4]),
        pltpu.make_async_copy(field_hbm, field.at[pl.ds(pad, cells)], sems.at[0]),
        pltpu.make_async_copy(nu_hbm, nu, sems.at[1]),
    ]
    for load in loads:
        load.start()
    field[0:pad, :] = jnp.zeros((pad, field.shape[1]), F32)
    width = target_ref.shape[1]
    for sender in range(target_ref.shape[0]):
        targets_ref[0:1, sender * width : (sender + 1) * width] = target_ref[sender : sender + 1, :]
    for load in loads:
        load.wait()
    stride = stride_ref[0]
    slots = source_ref.shape[2]

    @pl.loop(0, source_ref.shape[1])
    def _(grid_row):
        live = counts_ref[0, grid_row]
        for slot in range(slots):
            cell = source_ref[0, grid_row, slot]
            here = field[pl.ds(pad + cell, 1), :]
            radial = here - field[pl.ds(pad + cell - stride, 1), :]
            tangent = here - field[pl.ds(pad - 1 + cell, 1), :]
            swept = nu[0, pl.ds(cell, 1), :] * radial + nu[1, pl.ds(cell, 1), :] * tangent
            out_ref[grid_row, pl.ds(slot, 1), :] = jnp.where(slot < live, swept, 0.0)


def pick(core, sub_field, reluctivity, stride, counts, source_cell, target_row):
    cells, rotor = sub_field.shape
    _, grid_rows, slots = source_cell.shape
    pad = 512
    return pl.pallas_call(
        pick_kernel,
        out_shape=[
            jax.ShapeDtypeStruct((grid_rows, slots, rotor), F32),
            jax.ShapeDtypeStruct((1, target_row.size), jnp.int32),
        ],
        in_specs=[SMEM, HBM, HBM, HBM, VMEM, HBM, HBM],
        out_specs=[VMEM, VMEM],
        scratch_shapes=[
            pltpu.SMEM(stride.shape, jnp.int32),
            pltpu.SMEM(counts.shape, jnp.int32),
            pltpu.SMEM(source_cell.shape, jnp.int32),
            pltpu.VMEM((pad + cells, rotor), F32),
            pltpu.VMEM((2, cells, rotor), F32),
            pltpu.SemaphoreType.DMA((5,)),
        ],
        compiler_params=kernel_params(PICK_LIMIT),
        name="pick",
    )(core, stride, counts, source_cell, target_row, sub_field, reluctivity)


def left_lanes(shape):
    return lax.broadcasted_iota(jnp.int32, shape, 1) < shape[1] // 2


def swap_lanes(value):
    return pltpu.roll(value, value.shape[1] // 2, 1)


def packed(own, other):
    half = own.shape[0] // 2
    return jnp.where(
        left_lanes((half, own.shape[1])),
        own[:half] + swap_lanes(other[:half]),
        swap_lanes(own[half:]) + other[half:],
    )


def three_parts(value):
    high, low = split(value)
    rest = (value - high.astype(F32) - low.astype(F32)).astype(BF16)
    return jnp.concatenate([high, low], axis=1), rest


def interface_rows(block, rows, targets_ref, parts):
    pair, rest = parts
    width = rest.shape[1]
    row = block * rows + lax.broadcasted_iota(jnp.int32, (rows, rest.shape[0]), 0)
    chosen = jnp.where(row == targets_ref[...], 1.0, 0.0).astype(BF16)
    both = dot(chosen, pair)
    return both[:, :width] + both[:, width:] + dot(chosen, rest)


def first_kernel(rows, core_ref, own_ref, other_ref, received_ref, swapped_ref, out_ref, slots_ref):
    received, swapped = received_ref[...], swapped_ref[...]
    left = left_lanes(received.shape)
    low = jnp.where(left, received, swap_lanes(swapped))
    high = jnp.where(left, swap_lanes(received), swapped)
    slots = jnp.where(core_ref[0] == 0, low, high)
    slots_ref[...] = slots
    parts = three_parts(slots)
    out_ref[...] = packed(
        interface_rows(0, rows, own_ref, parts), interface_rows(0, rows, other_ref, parts)
    )


def first_residual(core, own_targets, other_targets, received, swapped, rows):
    rotor = received.shape[1]
    return pl.pallas_call(
        functools.partial(first_kernel, rows),
        out_shape=[
            jax.ShapeDtypeStruct((rows // 2, rotor), F32),
            jax.ShapeDtypeStruct(received.shape, F32),
        ],
        in_specs=[SMEM] + [VMEM] * 4,
        out_specs=[VMEM, VMEM],
        compiler_params=kernel_params(),
        name="first",
    )(core, own_targets, other_targets, received, swapped)


def fold_kernel(block, *refs):
    earlier = block - 1
    own_targets, other_targets, slots_ref, *hbm = refs[:7]
    shares = refs[7 : 7 + earlier]
    started_ref, *outs = refs[7 + earlier : -3]
    tiles, diags, sems = refs[-3:]
    base = block * (block - 1) // 2
    loads = []
    for j in range(block):
        for side in range(2):
            at = 2 * j + side
            loads.append(pltpu.make_async_copy(hbm[side].at[base + j], tiles.at[at], sems.at[at]))
    for side in range(2):
        loads.append(
            pltpu.make_async_copy(
                hbm[2 + side].at[earlier], diags.at[side], sems.at[2 * block + side]
            )
        )
    for load in loads:
        load.start()
    parts = three_parts(slots_ref[...])
    rows = tiles.shape[1]
    totals = [
        interface_rows(block, rows, targets, parts) for targets in (own_targets, other_targets)
    ]
    for j in range(earlier):
        share = shares[j][...]
        for side in range(2):
            loads[2 * j + side].wait()
            high, low = split(tiles[2 * j + side])
            totals[side] = totals[side] - split_product(high, low, share)
    started_ref[...] = packed(*totals)
    for side in range(2):
        loads[2 * earlier + side].wait()
        outs[2 * side][...], outs[2 * side + 1][...] = split(tiles[2 * earlier + side])
    for side in range(2):
        loads[2 * block + side].wait()
        outs[4 + 2 * side][...], outs[5 + 2 * side][...] = split(diags[side])


def fold(block, own_targets, other_targets, slots, lowers, diags, shares):
    _, rows, columns = lowers[0].shape
    _, out_rows, depth = diags[0].shape
    rotor = slots.shape[1]
    shapes = [jax.ShapeDtypeStruct((rows // 2, rotor), F32)]
    shapes += [jax.ShapeDtypeStruct((rows, columns), BF16)] * 4
    shapes += [jax.ShapeDtypeStruct((out_rows, depth), BF16)] * 4
    return pl.pallas_call(
        functools.partial(fold_kernel, block),
        out_shape=shapes,
        in_specs=[VMEM] * 3 + [HBM] * 4 + [VMEM] * len(shares),
        out_specs=[VMEM] * len(shapes),
        scratch_shapes=[
            pltpu.VMEM((2 * block, rows, columns), F32),
            pltpu.VMEM((2, out_rows, depth), F32),
            pltpu.SemaphoreType.DMA((2 * block + 2,)),
        ],
        compiler_params=kernel_params(WIDE_LIMIT),
        cost_estimate=pl.CostEstimate(
            flops=12 * block * rows * columns * rotor,
            bytes_accessed=8 * (block + 1) * rows * columns,
            transcendentals=0,
        ),
        name="fold",
    )(own_targets, other_targets, slots, *lowers, *diags, *shares)


def prepare_kernel(block, own_hbm, other_hbm, *refs):
    *outs, diags, sems = refs
    loads = [
        pltpu.make_async_copy(hbm.at[block], diags.at[side], sems.at[side])
        for side, hbm in enumerate((own_hbm, other_hbm))
    ]
    for load in loads:
        load.start()
    for side in range(2):
        loads[side].wait()
        outs[2 * side][...], outs[2 * side + 1][...] = split(diags[side])


def prepare(block, diags):
    _, out_rows, depth = diags[0].shape
    return pl.pallas_call(
        functools.partial(prepare_kernel, block),
        out_shape=[jax.ShapeDtypeStruct((out_rows, depth), BF16)] * 4,
        in_specs=[HBM] * 2,
        out_specs=[VMEM] * 4,
        scratch_shapes=[
            pltpu.VMEM((2, out_rows, depth), F32),
            pltpu.SemaphoreType.DMA((2,)),
        ],
        compiler_params=kernel_params(WIDE_LIMIT),
        cost_estimate=pl.CostEstimate(
            flops=8 * out_rows * depth,
            bytes_accessed=16 * out_rows * depth,
            transcendentals=0,
        ),
        name="prepare",
    )(*diags)


def lower_kernel(share_ref, own_high, own_low, other_high, other_low, started_ref, out_ref):
    share = share_ref[...]
    out_ref[...] = started_ref[...] - packed(
        split_product(own_high[...], own_low[...], share),
        split_product(other_high[...], other_low[...], share),
    )


def lower_product(share, tiles, started):
    return pl.pallas_call(
        lower_kernel,
        out_shape=jax.ShapeDtypeStruct(started.shape, F32),
        in_specs=[VMEM] * 6,
        out_specs=VMEM,
        compiler_params=kernel_params(),
        name="lower",
    )(share, *tiles, started)


def diag_kernel(*refs):
    *residual_refs, own_high, own_low, other_high, other_low, out_ref = refs
    residual = residual_refs[0][...]
    for ref in residual_refs[1:]:
        residual = residual + ref[...]
    turned = swap_lanes(residual)
    left = left_lanes(residual.shape)
    on_left = jnp.concatenate(
        [jnp.where(left, residual, 0.0), jnp.where(left, turned, 0.0)], axis=0
    )
    on_right = jnp.concatenate(
        [jnp.where(left, 0.0, turned), jnp.where(left, 0.0, residual)], axis=0
    )
    out_ref[...] = split_product(own_high[...], own_low[...], on_left) + split_product(
        other_high[...], other_low[...], on_right
    )


def diag_product(residuals, tiles):
    return pl.pallas_call(
        diag_kernel,
        out_shape=jax.ShapeDtypeStruct((tiles[0].shape[0], residuals[0].shape[1]), F32),
        in_specs=[VMEM] * (len(residuals) + 4),
        out_specs=VMEM,
        compiler_params=kernel_params(),
        name="diag",
    )(*residuals, *tiles)


def piece_kernel(parts_ref, piece_ref, copies_ref):
    piece = jnp.sum(parts_ref[...], axis=0)
    piece_ref[...] = piece
    for peer in range(copies_ref.shape[0]):
        copies_ref[peer] = piece


def piece_and_copies(parts):
    return pl.pallas_call(
        piece_kernel,
        out_shape=[
            jax.ShapeDtypeStruct(parts.shape[1:], F32),
            jax.ShapeDtypeStruct(parts.shape, F32),
        ],
        in_specs=[VMEM],
        out_specs=[VMEM, VMEM],
        compiler_params=kernel_params(),
        name="piece",
    )(parts)


def join_kernel(*refs):
    *piece_refs, out_ref = refs
    for block, piece_ref in enumerate(piece_refs):
        out_ref[block] = piece_ref[...]


def joined(pieces):
    return pl.pallas_call(
        join_kernel,
        out_shape=jax.ShapeDtypeStruct((len(pieces), *pieces[0].shape), F32),
        in_specs=[VMEM] * len(pieces),
        out_specs=VMEM,
        compiler_params=kernel_params(),
        name="join",
    )(*pieces)


def stacked_kernel(core_ref, early_ref, early_other_ref, last_ref, last_other_ref, out_ref):
    left = left_lanes(last_ref.shape)
    first_core = core_ref[0] == 0
    early = early_ref.shape[0]
    for block in range(early + 1):
        own = early_ref[block] if block < early else last_ref[...]
        other = early_other_ref[block] if block < early else last_other_ref[...]
        rows = jnp.where(left, own, other)
        out_ref[block] = jnp.where(first_core, rows, swap_lanes(rows))


def stacked(core, early, early_other, last, last_other):
    return pl.pallas_call(
        stacked_kernel,
        out_shape=jax.ShapeDtypeStruct((early.shape[0] + 1, *last.shape), F32),
        in_specs=[SMEM] + [VMEM] * 4,
        out_specs=VMEM,
        compiler_params=kernel_params(),
        name="stacked",
    )(core, early, early_other, last, last_other)


def other_core(value):
    peers = lax.axis_size("col")
    return lax.ppermute(value, "col", [(i, i ^ 1) for i in range(peers)])


def along_x(value):
    peers = lax.axis_size("col")
    return [value] + [
        lax.ppermute(value, "col", [(i, i ^ apart) for i in range(peers)])
        for apart in (2, 6, 4)
    ]


def per_row(value):
    return lax.all_to_all(value, "row", 0, 0, tiled=True)


def per_device(
    sub_field, reluctivity, stride, counts, source_cell, target_row, lower_tiles, diag_inverse
):
    blocks = diag_inverse.shape[0]
    tile_rows = lower_tiles.shape[1]
    rotor = sub_field.shape[1]
    peers = lax.axis_size("row")
    core = (lax.axis_index("col") % 2).astype(jnp.int32).reshape(1)
    diags = (diag_inverse, other_core(diag_inverse))
    lowers = (lower_tiles, other_core(lower_tiles))
    picked, targets = pick(
        core, sub_field, reluctivity, stride, counts, source_cell, target_row[0, 0]
    )
    other_targets = other_core(targets)
    received = per_row(picked).reshape(-1, rotor)

    shares = []
    pieces = []
    residual, slots = first_residual(
        core, targets, other_targets, received, other_core(received), tile_rows
    )
    for block in range(blocks):
        residuals = along_x(residual)
        if block + 1 < blocks:
            started, *tiles = fold(
                block + 1, targets, other_targets, slots, lowers, diags, shares
            )
            tiles, diag_tiles = tiles[:4], tiles[4:]
        else:
            diag_tiles = prepare(block, diags)
            early = joined(pieces)
            early_other = other_core(early)
        parts = per_row(diag_product(residuals, diag_tiles).reshape(peers, -1, rotor))
        if block + 1 < blocks:
            piece, copies = piece_and_copies(parts)
            pieces.append(piece)
            share = per_row(copies).reshape(-1, rotor)
            shares.append(share)
            residual = lower_product(share, tiles, started)
    last = jnp.sum(parts, axis=0)
    return stacked(core, early, early_other, last, other_core(last))[:, None]


def solution(mesh):
    placed = (
        P(("row", "col"), None),
        P(None, ("row", "col"), None),
        P(("row", "col")),
        P(("row", "col"), None),
        P(("row", "col"), None, None),
        P("row", "col", None, None),
        P(None, "row", "col"),
        P(None, "col", "row"),
    )
    return jax.shard_map(
        per_device,
        mesh=mesh,
        in_specs=placed,
        out_specs=P(None, "col", "row", None),
        check_vma=False,
    )
```

time: 293 us -> 300 us (1.024); the launches traced: 292 us -> 295 us
  starting transfers between devices: 49.1 us -> 80.9 us
  waiting for transfers between devices: 39.1 us -> 10.9 us
  blocking collectives: 175 us -> 160 us
  Pallas kernels: 26.3 us -> 40 us
    ppermute x24, waiting for transfers between devices: 24.7 us -> 4.94 us  [along_x(): lax.ppermute(value, 'col', [(i, i ^ apart) for i in range(peers)])]
    ppermute x24, starting transfers between devices: 16.9 us -> 36.3 us  [along_x(): lax.ppermute(value, 'col', [(i, i ^ apart) for i in range(peers)])]
    all_to_all x16 -> x15, blocking collectives: 175 us -> 160 us  [per_row(): return lax.all_to_all(value, 'row', 0, 0, tiled=True)]
    pallas_call x24 -> x26, Pallas kernels: 21.2 us -> 34.9 us  [the longest x7 24.2 us: fold(): pl.pallas_call(functools.partial(fold_kernel, block), out_shape=shapes, i...]
    ppermute x16 -> x6, starting transfers between devices: 32.2 us -> 41.1 us  [other_core(): return lax.ppermute(value, 'col', [(i, i ^ 1) for i in range(peers)])]
    ppermute x16 -> x6, waiting for transfers between devices: 14.4 us -> 5.94 us  [other_core(): return lax.ppermute(value, 'col', [(i, i ^ 1) for i in range(peers)])]
    all_to_all x0 -> x1, starting transfers between devices: none -> 3.53 us  [per_row(): return lax.all_to_all(value, 'row', 0, 0, tiled=True)]
  transfers between devices with their start and end apart: 40 -> 31, of which waited for: 33 -> 8; matrix products, arithmetic and copies ran while one was open for 0% -> 0% of each run, Pallas kernels for 5% -> 11%
where the time goes in v5:
time: 300 us; the launch traced here: 295 us
  blocking collectives  160 us (53%)
  starting transfers between devices  80.9 us (27%)
  Pallas kernels  40 us (13%)
  waiting for transfers between devices  10.9 us (4%)
    all_to_all x15, blocking collectives, per_row(): return lax.all_to_all(value, 'row', 0, 0, tiled=True)  160 us
    ppermute x6, starting transfers between devices, other_core(): return lax.ppermute(value, 'col', [(i, i ^ 1) for i in range(peers)])  41.1 us
    ppermute x24, starting transfers between devices, along_x(): lax.ppermute(value, 'col', [(i, i ^ apart) for i in range(peers)])  36.3 us
    pallas_call x7, Pallas kernels, fold(): pl.pallas_call(functools.partial(fold_kernel, block), out_shape=shapes, i...  24.2 us
  transfers between devices with their start and end apart: 31, of which 8 were waited for; matrix products, arithmetic and copies ran while one was open for 0% of the time, Pallas kernels for 11%

profile of v5, /device:TPU:1, one launch (start us, length us, event | category | flops | bytes accessed | tf_op | source)
XLA Modules:
  0.0 294.5 jit_solution(6709632765064992080)
XLA Ops:
  2.1 4.9 %pick.1 = (f32[16,32,128]{2,1,0:T(8,128)}, s32[1,512]{1,0:T(1,128)}) custom-call(s32[1]{0:T(128)} %bitcast.core_ref, s32[1]{0:T(128)S(6)} %copy.10.stride_hbm, s32[1,16]{1,0:T(1,128)} %counts_hbm.1, s32[1,16,32]{2,1,0:T(8,128)} %source_hbm.1, s32[16,32]{1,0:T(8,128)} %bitcast.58, f32[2048,128]{1,0:T(8,128)} %field_hbm.1, f32[2,2048,128]{2,1,0:T(8,128)} %nu_hbm.1), custom_call_target="tpu_custom_call" | custom-call | tf_op jit(solution)/shard_map/pick/pallas_call | solution.py:80
  7.0 15.8 %all_to_all.80 = f32[16,32,128]{2,1,0:T(8,128)S(1)} all-to-all(f32[16,32,128]{2,1,0:T(8,128)} %get-tuple-element.91), channel_id=1, replica_groups=mesh['row'=16,'col'=8] {'row'}, dimensions={0} | all-to-all | bytes 524288 | tf_op jit(solution)/shard_map/all_to_all | solution.py:384
  24.5 4.9 %collective-permute-done.other_ref.refs_1_ = s32[1,512]{1,0:T(1,128)S(1)} collective-permute-done((s32[1,512]{1,0:T(1,128)}, s32[1,512]{1,0:T(1,128)S(1)}, u32[]{:S(2)}, u32[]{:S(2)}) %collective-permute-start) | collective-permute-done | bytes 2080 | tf_op jit(solution)/shard_map/ppermute | solution.py:372
  39.2 10.4 %all_to_all.81.parts_ref = f32[16,32,128]{2,1,0:T(8,128)S(1)} all-to-all(f32[16,32,128]{2,1,0:T(8,128)S(1)} %bitcast.50), channel_id=1, replica_groups=mesh['row'=16,'col'=8] {'row'}, dimensions={0} | all-to-all | bytes 524288 | tf_op jit(solution)/shard_map/all_to_all | solution.py:384
  49.6 10.5 %all_to_all.82 = f32[16,32,128]{2,1,0:T(8,128)S(1)} all-to-all(f32[16,32,128]{2,1,0:T(8,128)S(1)} %get-tuple-element.99), channel_id=1, replica_groups=mesh['row'=16,'col'=8] {'row'}, dimensions={0} | all-to-all | bytes 524288 | tf_op jit(solution)/shard_map/all_to_all | solution.py:384
  67.3 10.4 %all_to_all.83.parts_ref = f32[16,32,128]{2,1,0:T(8,128)S(1)} all-to-all(f32[16,32,128]{2,1,0:T(8,128)S(1)} %bitcast.51), channel_id=1, replica_groups=mesh['row'=16,'col'=8] {'row'}, dimensions={0} | all-to-all | bytes 524288 | tf_op jit(solution)/shard_map/all_to_all | solution.py:384
  77.7 10.2 %all_to_all.84 = f32[16,32,128]{2,1,0:T(8,128)S(1)} all-to-all(f32[16,32,128]{2,1,0:T(8,128)S(1)} %get-tuple-element.110), channel_id=1, replica_groups=mesh['row'=16,'col'=8] {'row'}, dimensions={0} | all-to-all | bytes 524288 | tf_op jit(solution)/shard_map/all_to_all | solution.py:384
  95.6 10.4 %all_to_all.85.parts_ref = f32[16,32,128]{2,1,0:T(8,128)S(1)} all-to-all(f32[16,32,128]{2,1,0:T(8,128)S(1)} %bitcast.52), channel_id=1, replica_groups=mesh['row'=16,'col'=8] {'row'}, dimensions={0} | all-to-all | bytes 524288 | tf_op jit(solution)/shard_map/all_to_all | solution.py:384
  106.0 11.0 %all_to_all.86 = f32[16,32,128]{2,1,0:T(8,128)S(1)} all-to-all(f32[16,32,128]{2,1,0:T(8,128)S(1)} %get-tuple-element.121), channel_id=1, replica_groups=mesh['row'=16,'col'=8] {'row'}, dimensions={0} | all-to-all | bytes 524288 | tf_op jit(solution)/shard_map/all_to_all | solution.py:384
  125.2 10.1 %all_to_all.87.parts_ref = f32[16,32,128]{2,1,0:T(8,128)S(1)} all-to-all(f32[16,32,128]{2,1,0:T(8,128)S(1)} %bitcast.53), channel_id=1, replica_groups=mesh['row'=16,'col'=8] {'row'}, dimensions={0} | all-to-all | bytes 524288 | tf_op jit(solution)/shard_map/all_to_all | solution.py:384
  135.4 10.5 %all_to_all.88 = f32[16,32,128]{2,1,0:T(8,128)S(1)} all-to-all(f32[16,32,128]{2,1,0:T(8,128)S(1)} %get-tuple-element.132), channel_id=1, replica_groups=mesh['row'=16,'col'=8] {'row'}, dimensions={0} | all-to-all | bytes 524288 | tf_op jit(solution)/shard_map/all_to_all | solution.py:384
  149.7 4.0 %fold.11 = (f32[128,128]{1,0:T(8,128)S(1)}, bf16[256,512]{1,0:T(8,128)(2,1)S(1)}, bf16[256,512]{1,0:T(8,128)(2,1)S(1)}, bf16[256,512]{1,0:T(8,128)(2,1)S(1)}, bf...) custom-call(s32[1,512]{1,0:T(1,128)S(1)} %copy-done.1, ...), custom_call_target="tpu_custom_call" | custom-call | flops 1006632960 | bytes 6291456 | tf_op jit(solution)/shard_map/fold/pallas_call | solution.py:208
  154.3 10.2 %all_to_all.89.parts_ref = f32[16,32,128]{2,1,0:T(8,128)S(1)} all-to-all(f32[16,32,128]{2,1,0:T(8,128)S(1)} %bitcast.54), channel_id=1, replica_groups=mesh['row'=16,'col'=8] {'row'}, dimensions={0} | all-to-all | bytes 524288 | tf_op jit(solution)/shard_map/all_to_all | solution.py:384
  164.5 10.2 %all_to_all.90 = f32[16,32,128]{2,1,0:T(8,128)S(1)} all-to-all(f32[16,32,128]{2,1,0:T(8,128)S(1)} %get-tuple-element.143), channel_id=1, replica_groups=mesh['row'=16,'col'=8] {'row'}, dimensions={0} | all-to-all | bytes 524288 | tf_op jit(solution)/shard_map/all_to_all | solution.py:384
  177.0 10.6 %collective-permute-start.21 = (f32[128,128]{1,0:T(8,128)S(1)}, f32[128,128]{1,0:T(8,128)S(1)}, u32[]{:S(2)}, u32[]{:S(2)}) collective-permute-start(f32[128,128]{1,0:T(8,128)S(1)} %lower.11.refs_0_), channel_id=1, source_target_pairs={{0,4},{1,5},{2,6},{3,7},{4,0},{5,1},{6,2},{7,3},{8,12},{9,13},{10,... | collective-permute-start | bytes 196616 | tf_op jit(solution)/shard_map/ppermute | solution.py:378
  187.6 4.6 %fold.12 = (f32[128,128]{1,0:T(8,128)S(1)}, bf16[256,512]{1,0:T(8,128)(2,1)S(1)}, bf16[256,512]{1,0:T(8,128)(2,1)S(1)}, bf16[256,512]{1,0:T(8,128)(2,1)S(1)}, bf...) custom-call(s32[1,512]{1,0:T(1,128)S(1)} %copy-done.1, ...), custom_call_target="tpu_custom_call" | custom-call | flops 1207959552 | bytes 7340032 | tf_op jit(solution)/shard_map/fold/pallas_call | solution.py:208
  192.7 10.2 %all_to_all.91.parts_ref = f32[16,32,128]{2,1,0:T(8,128)S(1)} all-to-all(f32[16,32,128]{2,1,0:T(8,128)S(1)} %bitcast.55), channel_id=1, replica_groups=mesh['row'=16,'col'=8] {'row'}, dimensions={0} | all-to-all | bytes 524288 | tf_op jit(solution)/shard_map/all_to_all | solution.py:384
  202.9 10.2 %all_to_all.92 = f32[16,32,128]{2,1,0:T(8,128)S(1)} all-to-all(f32[16,32,128]{2,1,0:T(8,128)S(1)} %get-tuple-element.154), channel_id=1, replica_groups=mesh['row'=16,'col'=8] {'row'}, dimensions={0} | all-to-all | bytes 524288 | tf_op jit(solution)/shard_map/all_to_all | solution.py:384
  216.9 5.2 %fold.13 = (f32[128,128]{1,0:T(8,128)S(1)}, bf16[256,512]{1,0:T(8,128)(2,1)S(1)}, bf16[256,512]{1,0:T(8,128)(2,1)S(1)}, bf16[256,512]{1,0:T(8,128)(2,1)S(1)}, bf...) custom-call(s32[1,512]{1,0:T(1,128)S(1)} %copy-done.1, ...), custom_call_target="tpu_custom_call" | custom-call | flops 1409286144 | bytes 8388608 | tf_op jit(solution)/shard_map/fold/pallas_call | solution.py:208
  222.7 10.2 %all_to_all.93.parts_ref = f32[16,32,128]{2,1,0:T(8,128)S(1)} all-to-all(f32[16,32,128]{2,1,0:T(8,128)S(1)} %bitcast.56), channel_id=1, replica_groups=mesh['row'=16,'col'=8] {'row'}, dimensions={0} | all-to-all | bytes 524288 | tf_op jit(solution)/shard_map/all_to_all | solution.py:384
  232.9 10.2 %all_to_all.94 = f32[16,32,128]{2,1,0:T(8,128)S(1)} all-to-all(f32[16,32,128]{2,1,0:T(8,128)S(1)} %get-tuple-element.165), channel_id=1, replica_groups=mesh['row'=16,'col'=8] {'row'}, dimensions={0} | all-to-all | bytes 524288 | tf_op jit(solution)/shard_map/all_to_all | solution.py:384
  251.2 3.5 %all-to-all-start.15 = ((f32[16,32,128]{2,1,0:T(8,128)}), f32[16,32,128]{2,1,0:T(8,128)S(1)}, u32[]{:S(2)}, u32[]{:S(2)}) async-start(f32[16,32,128]{2,1,0:T(8,128)} %bitcast.17), calls=%async_computation.15 | async-start | bytes 524288 | tf_op jit(solution)/shard_map/all_to_all | solution.py:384
  254.8 29.3 %collective-permute-start.25 = (f32[7,32,128]{2,1,0:T(8,128)S(1)}, f32[7,32,128]{2,1,0:T(8,128)S(1)}, u32[]{:S(2)}, u32[]{:S(2)}) collective-permute-start(f32[7,32,128]{2,1,0:T(8,128)S(1)} %join.1.early_ref), channel_id=1, source_target_pairs={{0,1},{1,0},{2,3},{3,2},{4,5},{5,4},{6,7},{7,6},{8,9},{9,8},{10,11... | collective-permute-start | bytes 344072 | tf_op jit(solution)/shard_map/ppermute | solution.py:372
  284.1 8.6 %collective-permute-start.29 = (f32[32,128]{1,0:T(8,128)S(1)}, f32[32,128]{1,0:T(8,128)S(1)}, u32[]{:S(2)}, u32[]{:S(2)}) collective-permute-start(f32[32,128]{1,0:T(8,128)S(1)} %reduce_sum.9.last_ref), channel_id=1, source_target_pairs={{0,1},{1,0},{2,3},{3,2},{4,5},{5,4},{6,7},{7,6},{8,9},{9,8},{10,11... | collective-permute-start | bytes 49160 | tf_op jit(solution)/shard_map/ppermute | solution.py:372
  (92 shorter events, 57.4 us)
Async XLA Ops:
  0.0 34.7 %collective-permute-start.5 = (f32[28,256,512]{2,1,0:T(8,128)}, f32[28,256,512]{2,1,0:T(8,128)}, u32[]{:S(2)}, u32[]{:S(2)}) collective-permute-start(f32[28,256,512]{2,1,0:T(8,128)} %refs_3_.13), channel_id=1, source_target_pairs={{0,1},{1,0},{2,3},{3,2},{4,5},{5,4},{6,7},{7,6},{8,9},{9,8},{10,11... | collective-permute-start | bytes 44040200 | tf_op jit(solution)/shard_map/ppermute | solution.py:372
  1.4 33.3 %collective-permute-start.6 = (f32[8,512,256]{2,1,0:T(8,128)}, f32[8,512,256]{2,1,0:T(8,128)}, u32[]{:S(2)}, u32[]{:S(2)}) collective-permute-start(f32[8,512,256]{2,1,0:T(8,128)} %own_hbm.1), channel_id=1, source_target_pairs={{0,1},{1,0},{2,3},{3,2},{4,5},{5,4},{6,7},{7,6},{8,9},{9,8},{10,11... | collective-permute-start | bytes 12582920 | tf_op jit(solution)/shard_map/ppermute | solution.py:372
  22.8 6.8 %collective-permute-start.1 = (f32[512,128]{1,0:T(8,128)S(1)}, f32[512,128]{1,0:T(8,128)S(1)}, u32[]{:S(2)}, u32[]{:S(2)}) collective-permute-start(f32[512,128]{1,0:T(8,128)S(1)} %bitcast.48), channel_id=1, source_target_pairs={{0,1},{1,0},{2,3},{3,2},{4,5},{5,4},{6,7},{7,6},{8,9},{9,8},{10,11... | collective-permute-start | bytes 786440 | tf_op jit(solution)/shard_map/ppermute | solution.py:372
  24.5 4.9 %collective-permute-start = (s32[1,512]{1,0:T(1,128)}, s32[1,512]{1,0:T(1,128)S(1)}, u32[]{:S(2)}, u32[]{:S(2)}) collective-permute-start(s32[1,512]{1,0:T(1,128)} %get-tuple-element.90.own_ref.refs_0_), channel_id=1, source_target_pairs={{0,1},{1,0},{2,3},{3,2},{4,5},{5,4},{6,7},{7,6},{8,9},{9,8},{10,11... | collective-permute-start | bytes 6152 | tf_op jit(solution)/shard_map/ppermute | solution.py:372
  30.9 6.2 %collective-permute-start.2 = (f32[128,128]{1,0:T(8,128)S(1)}, f32[128,128]{1,0:T(8,128)S(1)}, u32[]{:S(2)}, u32[]{:S(2)}) collective-permute-start(f32[128,128]{1,0:T(8,128)S(1)} %get-tuple-element.92.refs_0_), channel_id=1, source_target_pairs={{0,2},{1,3},{2,0},{3,1},{4,6},{5,7},{6,4},{7,5},{8,10},{9,11},{10,... | collective-permute-start | bytes 196616 | tf_op jit(solution)/shard_map/ppermute | solution.py:378
  60.5 5.7 %collective-permute-start.7 = (f32[128,128]{1,0:T(8,128)S(1)}, f32[128,128]{1,0:T(8,128)S(1)}, u32[]{:S(2)}, u32[]{:S(2)}) collective-permute-start(f32[128,128]{1,0:T(8,128)S(1)} %lower.7.refs_0_), channel_id=1, source_target_pairs={{0,2},{1,3},{2,0},{3,1},{4,6},{5,7},{6,4},{7,5},{8,10},{9,11},{10,... | collective-permute-start | bytes 196616 | tf_op jit(solution)/shard_map/ppermute | solution.py:378
  60.9 5.3 %collective-permute-start.8 = (f32[128,128]{1,0:T(8,128)S(1)}, f32[128,128]{1,0:T(8,128)S(1)}, u32[]{:S(2)}, u32[]{:S(2)}) collective-permute-start(f32[128,128]{1,0:T(8,128)S(1)} %lower.7.refs_0_), channel_id=1, source_target_pairs={{0,6},{1,7},{2,4},{3,5},{4,2},{5,3},{6,0},{7,1},{8,14},{9,15},{10,... | collective-permute-start | bytes 196616 | tf_op jit(solution)/shard_map/ppermute | solution.py:378
  88.4 6.3 %collective-permute-start.10 = (f32[128,128]{1,0:T(8,128)S(1)}, f32[128,128]{1,0:T(8,128)S(1)}, u32[]{:S(2)}, u32[]{:S(2)}) collective-permute-start(f32[128,128]{1,0:T(8,128)S(1)} %lower.8.refs_0_), channel_id=1, source_target_pairs={{0,2},{1,3},{2,0},{3,1},{4,6},{5,7},{6,4},{7,5},{8,10},{9,11},{10,... | collective-permute-start | bytes 196616 | tf_op jit(solution)/shard_map/ppermute | solution.py:378
  88.5 6.2 %collective-permute-start.11 = (f32[128,128]{1,0:T(8,128)S(1)}, f32[128,128]{1,0:T(8,128)S(1)}, u32[]{:S(2)}, u32[]{:S(2)}) collective-permute-start(f32[128,128]{1,0:T(8,128)S(1)} %lower.8.refs_0_), channel_id=1, source_target_pairs={{0,6},{1,7},{2,4},{3,5},{4,2},{5,3},{6,0},{7,1},{8,14},{9,15},{10,... | collective-permute-start | bytes 196616 | tf_op jit(solution)/shard_map/ppermute | solution.py:378
  90.2 4.9 %collective-permute-start.12 = (f32[128,128]{1,0:T(8,128)S(1)}, f32[128,128]{1,0:T(8,128)S(1)}, u32[]{:S(2)}, u32[]{:S(2)}) collective-permute-start(f32[128,128]{1,0:T(8,128)S(1)} %lower.8.refs_0_), channel_id=1, source_target_pairs={{0,4},{1,5},{2,6},{3,7},{4,0},{5,1},{6,2},{7,3},{8,12},{9,13},{10,... | collective-permute-start | bytes 196616 | tf_op jit(solution)/shard_map/ppermute | solution.py:378
  117.5 6.8 %collective-permute-start.13 = (f32[128,128]{1,0:T(8,128)S(1)}, f32[128,128]{1,0:T(8,128)S(1)}, u32[]{:S(2)}, u32[]{:S(2)}) collective-permute-start(f32[128,128]{1,0:T(8,128)S(1)} %lower.9.refs_0_), channel_id=1, source_target_pairs={{0,2},{1,3},{2,0},{3,1},{4,6},{5,7},{6,4},{7,5},{8,10},{9,11},{10,... | collective-permute-start | bytes 196616 | tf_op jit(solution)/shard_map/ppermute | solution.py:378
  117.8 6.4 %collective-permute-start.14 = (f32[128,128]{1,0:T(8,128)S(1)}, f32[128,128]{1,0:T(8,128)S(1)}, u32[]{:S(2)}, u32[]{:S(2)}) collective-permute-start(f32[128,128]{1,0:T(8,128)S(1)} %lower.9.refs_0_), channel_id=1, source_target_pairs={{0,6},{1,7},{2,4},{3,5},{4,2},{5,3},{6,0},{7,1},{8,14},{9,15},{10,... | collective-permute-start | bytes 196616 | tf_op jit(solution)/shard_map/ppermute | solution.py:378
  146.3 7.4 %collective-permute-start.16 = (f32[128,128]{1,0:T(8,128)S(1)}, f32[128,128]{1,0:T(8,128)S(1)}, u32[]{:S(2)}, u32[]{:S(2)}) collective-permute-start(f32[128,128]{1,0:T(8,128)S(1)} %lower.10.refs_0_), channel_id=1, source_target_pairs={{0,2},{1,3},{2,0},{3,1},{4,6},{5,7},{6,4},{7,5},{8,10},{9,11},{10,... | collective-permute-start | bytes 196616 | tf_op jit(solution)/shard_map/ppermute | solution.py:378
  146.4 7.3 %collective-permute-start.17 = (f32[128,128]{1,0:T(8,128)S(1)}, f32[128,128]{1,0:T(8,128)S(1)}, u32[]{:S(2)}, u32[]{:S(2)}) collective-permute-start(f32[128,128]{1,0:T(8,128)S(1)} %lower.10.refs_0_), channel_id=1, source_target_pairs={{0,6},{1,7},{2,4},{3,5},{4,2},{5,3},{6,0},{7,1},{8,14},{9,15},{10,... | collective-permute-start | bytes 196616 | tf_op jit(solution)/shard_map/ppermute | solution.py:378
  148.2 5.5 %collective-permute-start.18 = (f32[128,128]{1,0:T(8,128)S(1)}, f32[128,128]{1,0:T(8,128)S(1)}, u32[]{:S(2)}, u32[]{:S(2)}) collective-permute-start(f32[128,128]{1,0:T(8,128)S(1)} %lower.10.refs_0_), channel_id=1, source_target_pairs={{0,4},{1,5},{2,6},{3,7},{4,0},{5,1},{6,2},{7,3},{8,12},{9,13},{10,... | collective-permute-start | bytes 196616 | tf_op jit(solution)/shard_map/ppermute | solution.py:378
  175.1 17.1 %collective-permute-start.19 = (f32[128,128]{1,0:T(8,128)S(1)}, f32[128,128]{1,0:T(8,128)S(1)}, u32[]{:S(2)}, u32[]{:S(2)}) collective-permute-start(f32[128,128]{1,0:T(8,128)S(1)} %lower.11.refs_0_), channel_id=1, source_target_pairs={{0,2},{1,3},{2,0},{3,1},{4,6},{5,7},{6,4},{7,5},{8,10},{9,11},{10,... | collective-permute-start | bytes 196616 | tf_op jit(solution)/shard_map/ppermute | solution.py:378
  175.3 16.9 %collective-permute-start.20 = (f32[128,128]{1,0:T(8,128)S(1)}, f32[128,128]{1,0:T(8,128)S(1)}, u32[]{:S(2)}, u32[]{:S(2)}) collective-permute-start(f32[128,128]{1,0:T(8,128)S(1)} %lower.11.refs_0_), channel_id=1, source_target_pairs={{0,6},{1,7},{2,4},{3,5},{4,2},{5,3},{6,0},{7,1},{8,14},{9,15},{10,... | collective-permute-start | bytes 196616 | tf_op jit(solution)/shard_map/ppermute | solution.py:378
  177.0 15.3 %collective-permute-start.21 = (f32[128,128]{1,0:T(8,128)S(1)}, f32[128,128]{1,0:T(8,128)S(1)}, u32[]{:S(2)}, u32[]{:S(2)}) collective-permute-start(f32[128,128]{1,0:T(8,128)S(1)} %lower.11.refs_0_), channel_id=1, source_target_pairs={{0,4},{1,5},{2,6},{3,7},{4,0},{5,1},{6,2},{7,3},{8,12},{9,13},{10,... | collective-permute-start | bytes 196616 | tf_op jit(solution)/shard_map/ppermute | solution.py:378
  213.6 8.6 %collective-permute-start.22 = (f32[128,128]{1,0:T(8,128)S(1)}, f32[128,128]{1,0:T(8,128)S(1)}, u32[]{:S(2)}, u32[]{:S(2)}) collective-permute-start(f32[128,128]{1,0:T(8,128)S(1)} %lower.12.refs_0_), channel_id=1, source_target_pairs={{0,2},{1,3},{2,0},{3,1},{4,6},{5,7},{6,4},{7,5},{8,10},{9,11},{10,... | collective-permute-start | bytes 196616 | tf_op jit(solution)/shard_map/ppermute | solution.py:378
  213.8 8.4 %collective-permute-start.23 = (f32[128,128]{1,0:T(8,128)S(1)}, f32[128,128]{1,0:T(8,128)S(1)}, u32[]{:S(2)}, u32[]{:S(2)}) collective-permute-start(f32[128,128]{1,0:T(8,128)S(1)} %lower.12.refs_0_), channel_id=1, source_target_pairs={{0,6},{1,7},{2,4},{3,5},{4,2},{5,3},{6,0},{7,1},{8,14},{9,15},{10,... | collective-permute-start | bytes 196616 | tf_op jit(solution)/shard_map/ppermute | solution.py:378
  215.5 6.7 %collective-permute-start.24 = (f32[128,128]{1,0:T(8,128)S(1)}, f32[128,128]{1,0:T(8,128)S(1)}, u32[]{:S(2)}, u32[]{:S(2)}) collective-permute-start(f32[128,128]{1,0:T(8,128)S(1)} %lower.12.refs_0_), channel_id=1, source_target_pairs={{0,4},{1,5},{2,6},{3,7},{4,0},{5,1},{6,2},{7,3},{8,12},{9,13},{10,... | collective-permute-start | bytes 196616 | tf_op jit(solution)/shard_map/ppermute | solution.py:378
  251.2 32.9 %all-to-all-start.15 = ((f32[16,32,128]{2,1,0:T(8,128)}), f32[16,32,128]{2,1,0:T(8,128)S(1)}, u32[]{:S(2)}, u32[]{:S(2)}) async-start(f32[16,32,128]{2,1,0:T(8,128)} %bitcast.17), calls=%async_computation.15 | async-start | bytes 524288 | tf_op jit(solution)/shard_map/all_to_all | solution.py:384
  254.8 38.0 %collective-permute-start.25 = (f32[7,32,128]{2,1,0:T(8,128)S(1)}, f32[7,32,128]{2,1,0:T(8,128)S(1)}, u32[]{:S(2)}, u32[]{:S(2)}) collective-permute-start(f32[7,32,128]{2,1,0:T(8,128)S(1)} %join.1.early_ref), channel_id=1, source_target_pairs={{0,1},{1,0},{2,3},{3,2},{4,5},{5,4},{6,7},{7,6},{8,9},{9,8},{10,11... | collective-permute-start | bytes 344072 | tf_op jit(solution)/shard_map/ppermute | solution.py:372
  284.1 9.5 %collective-permute-start.29 = (f32[32,128]{1,0:T(8,128)S(1)}, f32[32,128]{1,0:T(8,128)S(1)}, u32[]{:S(2)}, u32[]{:S(2)}) collective-permute-start(f32[32,128]{1,0:T(8,128)S(1)} %reduce_sum.9.last_ref), channel_id=1, source_target_pairs={{0,1},{1,0},{2,3},{3,2},{4,5},{5,4},{6,7},{7,6},{8,9},{9,8},{10,11... | collective-permute-start | bytes 49160 | tf_op jit(solution)/shard_map/ppermute | solution.py:372
  (9 other events, 33.7 us)

commit v6 on v5

--- a/solution.py
+++ b/solution.py
@@ -121,100 +121,141 @@
     return jnp.concatenate([high, low], axis=1), rest
 
 
-def interface_rows(block, rows, targets_ref, parts):
+def interface_rows(block, rows, targets, parts):
     pair, rest = parts
     width = rest.shape[1]
     row = block * rows + lax.broadcasted_iota(jnp.int32, (rows, rest.shape[0]), 0)
-    chosen = jnp.where(row == targets_ref[...], 1.0, 0.0).astype(BF16)
+    chosen = jnp.where(row == targets, 1.0, 0.0).astype(BF16)
     both = dot(chosen, pair)
     return both[:, :width] + both[:, width:] + dot(chosen, rest)
 
 
-def first_kernel(rows, core_ref, own_ref, other_ref, received_ref, swapped_ref, out_ref, slots_ref):
+def fill_interface(block, targets_ref, slots, totals):
+    pair, rest = three_parts(slots)
+
+    @pl.loop(0, 2)
+    def _(side):
+        totals[side] = interface_rows(block, totals.shape[1], targets_ref[side], (pair, rest))
+
+
+def first_kernel(
+    core_ref, own_ref, other_ref, received_ref, swapped_ref, out_ref, slots_ref, targets_ref, totals
+):
+    targets_ref[0] = own_ref[...]
+    targets_ref[1] = other_ref[...]
     received, swapped = received_ref[...], swapped_ref[...]
     left = left_lanes(received.shape)
     low = jnp.where(left, received, swap_lanes(swapped))
     high = jnp.where(left, swap_lanes(received), swapped)
     slots = jnp.where(core_ref[0] == 0, low, high)
     slots_ref[...] = slots
-    parts = three_parts(slots)
-    out_ref[...] = packed(
-        interface_rows(0, rows, own_ref, parts), interface_rows(0, rows, other_ref, parts)
-    )
+    fill_interface(0, targets_ref, slots, totals)
+    out_ref[...] = packed(totals[0], totals[1])
 
 
 def first_residual(core, own_targets, other_targets, received, swapped, rows):
     rotor = received.shape[1]
     return pl.pallas_call(
-        functools.partial(first_kernel, rows),
+        first_kernel,
         out_shape=[
             jax.ShapeDtypeStruct((rows // 2, rotor), F32),
             jax.ShapeDtypeStruct(received.shape, F32),
+            jax.ShapeDtypeStruct((2, *own_targets.shape), jnp.int32),
         ],
         in_specs=[SMEM] + [VMEM] * 4,
-        out_specs=[VMEM, VMEM],
+        out_specs=[VMEM] * 3,
+        scratch_shapes=[pltpu.VMEM((2, rows, rotor), F32)],
         compiler_params=kernel_params(),
         name="first",
     )(core, own_targets, other_targets, received, swapped)
 
 
-def fold_kernel(block, *refs):
+def split_sides(load, tiles, first, high_ref, low_ref):
+    @pl.loop(0, 2)
+    def _(side):
+        load(first + side).wait()
+        high_ref[side], low_ref[side] = split(tiles[first + side])
+
+
+def fold_kernel(block, with_diag, *refs):
     earlier = block - 1
-    own_targets, other_targets, slots_ref, *hbm = refs[:7]
-    shares = refs[7 : 7 + earlier]
-    started_ref, *outs = refs[7 + earlier : -3]
-    tiles, diags, sems = refs[-3:]
+    refs = list(refs)
+    targets_ref, slots_ref = refs[:2]
+    lowers = refs[2:4]
+    diags = refs[4:6] if with_diag else []
+    at = 4 + len(diags)
+    shares = refs[at : at + earlier]
+    at += earlier
+    started_ref, lower_high, lower_low = refs[at : at + 3]
+    at += 3
+    diag_outs = refs[at : at + 2] if with_diag else []
+    at += len(diag_outs)
+    totals, tiles, held, sems, share_sems = refs[at : at + 5]
     base = block * (block - 1) // 2
-    loads = []
+
     for j in range(block):
         for side in range(2):
-            at = 2 * j + side
-            loads.append(pltpu.make_async_copy(hbm[side].at[base + j], tiles.at[at], sems.at[at]))
-    for side in range(2):
-        loads.append(
+            at_tile = 2 * j + side
             pltpu.make_async_copy(
-                hbm[2 + side].at[earlier], diags.at[side], sems.at[2 * block + side]
-            )
-        )
-    for load in loads:
-        load.start()
-    parts = three_parts(slots_ref[...])
-    rows = tiles.shape[1]
-    totals = [
-        interface_rows(block, rows, targets, parts) for targets in (own_targets, other_targets)
-    ]
+                lowers[side].at[base + j], tiles.at[at_tile], sems.at[at_tile]
+            ).start()
     for j in range(earlier):
-        share = shares[j][...]
+        pltpu.make_async_copy(shares[j], held.at[j], share_sems.at[j]).start()
+
+    def loaded(at_tile):
+        return pltpu.make_async_copy(lowers[0].at[0], tiles.at[at_tile], sems.at[at_tile])
+
+    if with_diag:
+        diag_tiles, diag_sems = refs[-2:]
+
+        def diag_loaded(side):
+            return pltpu.make_async_copy(diags[0].at[0], diag_tiles.at[side], diag_sems.at[side])
+
         for side in range(2):
-            loads[2 * j + side].wait()
-            high, low = split(tiles[2 * j + side])
-            totals[side] = totals[side] - split_product(high, low, share)
-    started_ref[...] = packed(*totals)
-    for side in range(2):
-        loads[2 * earlier + side].wait()
-        outs[2 * side][...], outs[2 * side + 1][...] = split(tiles[2 * earlier + side])
-    for side in range(2):
-        loads[2 * block + side].wait()
-        outs[4 + 2 * side][...], outs[5 + 2 * side][...] = split(diags[side])
-
-
-def fold(block, own_targets, other_targets, slots, lowers, diags, shares):
+            pltpu.make_async_copy(
+                diags[side].at[earlier], diag_tiles.at[side], diag_sems.at[side]
+            ).start()
+
+    fill_interface(block, targets_ref, slots_ref[...], totals)
+    for j in range(earlier):
+        pltpu.make_async_copy(shares[j], held.at[j], share_sems.at[j]).wait()
+    if earlier:
+
+        @pl.loop(0, 2 * earlier)
+        def _(at_tile):
+            loaded(at_tile).wait()
+            high, low = split(tiles[at_tile])
+            side = lax.rem(at_tile, 2)
+            totals[side] = totals[side] - split_product(high, low, held[lax.div(at_tile, 2)])
+
+    started_ref[...] = packed(totals[0], totals[1])
+    split_sides(loaded, tiles, 2 * earlier, lower_high, lower_low)
+    if with_diag:
+        split_sides(diag_loaded, diag_tiles, 0, *diag_outs)
+
+
+def fold(block, targets, slots, lowers, diags, shares):
     _, rows, columns = lowers[0].shape
-    _, out_rows, depth = diags[0].shape
     rotor = slots.shape[1]
     shapes = [jax.ShapeDtypeStruct((rows // 2, rotor), F32)]
-    shapes += [jax.ShapeDtypeStruct((rows, columns), BF16)] * 4
-    shapes += [jax.ShapeDtypeStruct((out_rows, depth), BF16)] * 4
-    return pl.pallas_call(
-        functools.partial(fold_kernel, block),
+    shapes += [jax.ShapeDtypeStruct((2, rows, columns), BF16)] * 2
+    scratch = [
+        pltpu.VMEM((2, rows, rotor), F32),
+        pltpu.VMEM((2 * block, rows, columns), F32),
+        pltpu.VMEM((max(block - 1, 1), columns, rotor), F32),
+        pltpu.SemaphoreType.DMA((2 * block,)),
+        pltpu.SemaphoreType.DMA((block,)),
+    ]
+    if diags:
+        _, out_rows, depth = diags[0].shape
+        shapes += [jax.ShapeDtypeStruct((2, out_rows, depth), BF16)] * 2
+        scratch += [pltpu.VMEM((2, out_rows, depth), F32), pltpu.SemaphoreType.DMA((2,))]
+    return pl.pallas_call(
+        functools.partial(fold_kernel, block, bool(diags)),
         out_shape=shapes,
-        in_specs=[VMEM] * 3 + [HBM] * 4 + [VMEM] * len(shares),
+        in_specs=[VMEM] * 2 + [HBM] * (2 + len(diags)) + [VMEM] * len(shares),
         out_specs=[VMEM] * len(shapes),
-        scratch_shapes=[
-            pltpu.VMEM((2 * block, rows, columns), F32),
-            pltpu.VMEM((2, out_rows, depth), F32),
-            pltpu.SemaphoreType.DMA((2 * block + 2,)),
-        ],
+        scratch_shapes=scratch,
         compiler_params=kernel_params(WIDE_LIMIT),
         cost_estimate=pl.CostEstimate(
             flops=12 * block * rows * columns * rotor,
@@ -222,29 +263,26 @@
             transcendentals=0,
         ),
         name="fold",
-    )(own_targets, other_targets, slots, *lowers, *diags, *shares)
-
-
-def prepare_kernel(block, own_hbm, other_hbm, *refs):
-    *outs, diags, sems = refs
-    loads = [
-        pltpu.make_async_copy(hbm.at[block], diags.at[side], sems.at[side])
-        for side, hbm in enumerate((own_hbm, other_hbm))
-    ]
-    for load in loads:
-        load.start()
-    for side in range(2):
-        loads[side].wait()
-        outs[2 * side][...], outs[2 * side + 1][...] = split(diags[side])
+    )(targets, slots, *lowers, *diags, *shares)
+
+
+def prepare_kernel(block, own_hbm, other_hbm, high_ref, low_ref, diags, sems):
+    for side, hbm in enumerate((own_hbm, other_hbm)):
+        pltpu.make_async_copy(hbm.at[block], diags.at[side], sems.at[side]).start()
+
+    def loaded(side):
+        return pltpu.make_async_copy(own_hbm.at[block], diags.at[side], sems.at[side])
+
+    split_sides(loaded, diags, 0, high_ref, low_ref)
 
 
 def prepare(block, diags):
     _, out_rows, depth = diags[0].shape
     return pl.pallas_call(
         functools.partial(prepare_kernel, block),
-        out_shape=[jax.ShapeDtypeStruct((out_rows, depth), BF16)] * 4,
+        out_shape=[jax.ShapeDtypeStruct((2, out_rows, depth), BF16)] * 2,
         in_specs=[HBM] * 2,
-        out_specs=[VMEM] * 4,
+        out_specs=[VMEM] * 2,
         scratch_shapes=[
             pltpu.VMEM((2, out_rows, depth), F32),
             pltpu.SemaphoreType.DMA((2,)),
@@ -259,11 +297,10 @@
     )(*diags)
 
 
-def lower_kernel(share_ref, own_high, own_low, other_high, other_low, started_ref, out_ref):
+def lower_kernel(share_ref, high_ref, low_ref, started_ref, out_ref):
     share = share_ref[...]
     out_ref[...] = started_ref[...] - packed(
-        split_product(own_high[...], own_low[...], share),
-        split_product(other_high[...], other_low[...], share),
+        split_product(high_ref[0], low_ref[0], share), split_product(high_ref[1], low_ref[1], share)
     )
 
 
@@ -271,7 +308,7 @@
     return pl.pallas_call(
         lower_kernel,
         out_shape=jax.ShapeDtypeStruct(started.shape, F32),
-        in_specs=[VMEM] * 6,
+        in_specs=[VMEM] * 4,
         out_specs=VMEM,
         compiler_params=kernel_params(),
         name="lower",
@@ -279,7 +316,7 @@
 
 
 def diag_kernel(*refs):
-    *residual_refs, own_high, own_low, other_high, other_low, out_ref = refs
+    *residual_refs, high_ref, low_ref, out_ref = refs
     residual = residual_refs[0][...]
     for ref in residual_refs[1:]:
         residual = residual + ref[...]
@@ -291,16 +328,16 @@
     on_right = jnp.concatenate(
         [jnp.where(left, 0.0, turned), jnp.where(left, 0.0, residual)], axis=0
     )
-    out_ref[...] = split_product(own_high[...], own_low[...], on_left) + split_product(
-        other_high[...], other_low[...], on_right
+    out_ref[...] = split_product(high_ref[0], low_ref[0], on_left) + split_product(
+        high_ref[1], low_ref[1], on_right
     )
 
 
 def diag_product(residuals, tiles):
     return pl.pallas_call(
         diag_kernel,
-        out_shape=jax.ShapeDtypeStruct((tiles[0].shape[0], residuals[0].shape[1]), F32),
-        in_specs=[VMEM] * (len(residuals) + 4),
+        out_shape=jax.ShapeDtypeStruct((tiles[0].shape[1], residuals[0].shape[1]), F32),
+        in_specs=[VMEM] * (len(residuals) + 2),
         out_specs=VMEM,
         compiler_params=kernel_params(),
         name="diag",
@@ -393,7 +430,6 @@
     peers = lax.axis_size("row")
     core = (lax.axis_index("col") % 2).astype(jnp.int32).reshape(1)
     diags = (diag_inverse, other_core(diag_inverse))
-    lowers = (lower_tiles, other_core(lower_tiles))
     picked, targets = pick(
         core, sub_field, reluctivity, stride, counts, source_cell, target_row[0, 0]
     )
@@ -402,27 +438,34 @@
 
     shares = []
     pieces = []
-    residual, slots = first_residual(
+    residual, slots, targets = first_residual(
         core, targets, other_targets, received, other_core(received), tile_rows
     )
+    own_lower, slots = lax.optimization_barrier((lower_tiles, slots))
+    lowers = (lower_tiles, other_core(own_lower))
     for block in range(blocks):
+        later = block + 1
+        if later == blocks:
+            residual, pieces = lax.optimization_barrier((residual, pieces))
         residuals = along_x(residual)
-        if block + 1 < blocks:
-            started, *tiles = fold(
-                block + 1, targets, other_targets, slots, lowers, diags, shares
+        if later < blocks:
+            started, lower_high, lower_low, *diag_tiles = fold(
+                later, targets, slots, lowers, diags if block else (), shares
             )
-            tiles, diag_tiles = tiles[:4], tiles[4:]
-        else:
+        if block == 0 or later == blocks:
             diag_tiles = prepare(block, diags)
+        if later == blocks:
             early = joined(pieces)
-            early_other = other_core(early)
+            diag_tiles, early, early_other = lax.optimization_barrier(
+                (diag_tiles, early, other_core(early))
+            )
         parts = per_row(diag_product(residuals, diag_tiles).reshape(peers, -1, rotor))
-        if block + 1 < blocks:
+        if later < blocks:
             piece, copies = piece_and_copies(parts)
             pieces.append(piece)
             share = per_row(copies).reshape(-1, rotor)
             shares.append(share)
-            residual = lower_product(share, tiles, started)
+            residual = lower_product(share, (lower_high, lower_low), started)
     last = jnp.sum(parts, axis=0)
     return stacked(core, early, early_other, last, other_core(last))[:, None]
 

time: 300 us -> 294 us (0.980); the launches traced: 295 us -> 293 us
  starting transfers between devices: 80.9 us -> 63.2 us
  waiting for transfers between devices: 10.9 us -> 24.1 us
    ppermute x24, starting transfers between devices: 36.3 us -> 27.3 us  [along_x(): lax.ppermute(value, 'col', [(i, i ^ apart) for i in range(peers)])]
    ppermute x6, starting transfers between devices: 41.1 us -> 32.3 us  [other_core(): return lax.ppermute(value, 'col', [(i, i ^ 1) for i in range(peers)])]
    ppermute x6, waiting for transfers between devices: 5.94 us -> 14.6 us  [other_core(): return lax.ppermute(value, 'col', [(i, i ^ 1) for i in range(peers)])]
    all_to_all x1, waiting for transfers between devices: 0.01 us -> 6.17 us  [per_row(): return lax.all_to_all(value, 'row', 0, 0, tiled=True)]
  transfers between devices with their start and end apart: 31 -> 31, of which waited for: 8 -> 8; matrix products, arithmetic and copies ran while one was open for 0% -> 0% of each run, Pallas kernels for 11% -> 10%
where the time goes in v6:
time: 294 us; the launch traced here: 293 us
  blocking collectives  161 us (55%)
  starting transfers between devices  63.2 us (21%)
  Pallas kernels  41.7 us (14%)
  waiting for transfers between devices  24.1 us (8%)
    all_to_all x15, blocking collectives, per_row(): return lax.all_to_all(value, 'row', 0, 0, tiled=True)  161 us
    ppermute x6, starting transfers between devices, other_core(): return lax.ppermute(value, 'col', [(i, i ^ 1) for i in range(peers)])  32.3 us
    ppermute x24, starting transfers between devices, along_x(): lax.ppermute(value, 'col', [(i, i ^ apart) for i in range(peers)])  27.3 us
    pallas_call x7, Pallas kernels, fold(): pl.pallas_call(functools.partial(fold_kernel, block, bool(diags)), out_sh...  24.3 us
    ppermute x6, waiting for transfers between devices, other_core(): return lax.ppermute(value, 'col', [(i, i ^ 1) for i in range(peers)])  14.6 us
    all_to_all x1, waiting for transfers between devices, per_row(): return lax.all_to_all(value, 'row', 0, 0, tiled=True)  6.17 us
  transfers between devices with their start and end apart: 31, of which 8 were waited for; matrix products, arithmetic and copies ran while one was open for 0% of the time, Pallas kernels for 10%

profile of v6, /device:TPU:1, one launch (start us, length us, event | category | flops | bytes accessed | tf_op | source)
XLA Modules:
  0.0 293.4 jit_solution(17855448378278998900)
XLA Ops:
  0.7 4.9 %pick.1 = (f32[16,32,128]{2,1,0:T(8,128)}, s32[1,512]{1,0:T(1,128)}) custom-call(s32[1]{0:T(128)} %bitcast.core_ref, s32[1]{0:T(128)S(6)} %copy.10.stride_hbm, s32[1,16]{1,0:T(1,128)} %counts_hbm.1, s32[1,16,32]{2,1,0:T(8,128)} %source_hbm.1, s32[16,32]{1,0:T(8,128)} %bitcast.59, f32[2048,128]{1,0:T(8,128)} %field_hbm.1, f32[2,2048,128]{2,1,0:T(8,128)} %nu_hbm.1), custom_call_target="tpu_custom_call" | custom-call | tf_op jit(solution)/shard_map/pick/pallas_call | solution.py:80
  5.5 16.2 %all_to_all.80 = f32[16,32,128]{2,1,0:T(8,128)S(1)} all-to-all(f32[16,32,128]{2,1,0:T(8,128)} %get-tuple-element.78), channel_id=1, replica_groups=mesh['row'=16,'col'=8] {'row'}, dimensions={0} | all-to-all | bytes 524288 | tf_op jit(solution)/shard_map/all_to_all | solution.py:421
  31.0 12.4 %collective-permute-done.other_hbm.refs_5_ = f32[8,512,256]{2,1,0:T(8,128)S(1)} collective-permute-done((f32[8,512,256]{2,1,0:T(8,128)}, f32[8,512,256]{2,1,0:T(8,128)S(1)}, u32[]{:S(2)}, u32[]{:S(2)}) %collective-permute-start) | collective-permute-done | bytes 4194336 | tf_op jit(solution)/shard_map/ppermute | solution.py:409
  47.2 10.7 %all_to_all.81.parts_ref = f32[16,32,128]{2,1,0:T(8,128)S(1)} all-to-all(f32[16,32,128]{2,1,0:T(8,128)S(1)} %bitcast.50), channel_id=1, replica_groups=mesh['row'=16,'col'=8] {'row'}, dimensions={0} | all-to-all | bytes 524288 | tf_op jit(solution)/shard_map/all_to_all | solution.py:421
  58.7 3.5 %all-to-all-start.2 = ((f32[16,32,128]{2,1,0:T(8,128)}), f32[16,32,128]{2,1,0:T(8,128)S(1)}, u32[]{:S(2)}, u32[]{:S(2)}) async-start(f32[16,32,128]{2,1,0:T(8,128)} %get-tuple-element.82), calls=%async_computation.2 | async-start | bytes 524288 | tf_op jit(solution)/shard_map/all_to_all | solution.py:421
  63.6 6.2 %all-to-all-done.2 = f32[16,32,128]{2,1,0:T(8,128)S(1)} async-done(((f32[16,32,128]{2,1,0:T(8,128)}), f32[16,32,128]{2,1,0:T(8,128)S(1)}, u32[]{:S(2)}, u32[]{:S(2)}) %all-to-all-start.2) | async-done | bytes 262176 | tf_op jit(solution)/shard_map/all_to_all | solution.py:421
  78.5 10.7 %all_to_all.82.parts_ref = f32[16,32,128]{2,1,0:T(8,128)S(1)} all-to-all(f32[16,32,128]{2,1,0:T(8,128)S(1)} %bitcast.51), channel_id=1, replica_groups=mesh['row'=16,'col'=8] {'row'}, dimensions={0} | all-to-all | bytes 524288 | tf_op jit(solution)/shard_map/all_to_all | solution.py:421
  89.2 10.2 %all_to_all.83 = f32[16,32,128]{2,1,0:T(8,128)S(1)} all-to-all(f32[16,32,128]{2,1,0:T(8,128)S(1)} %get-tuple-element.92), channel_id=1, replica_groups=mesh['row'=16,'col'=8] {'row'}, dimensions={0} | all-to-all | bytes 524288 | tf_op jit(solution)/shard_map/all_to_all | solution.py:421
  106.6 10.2 %all_to_all.84.parts_ref = f32[16,32,128]{2,1,0:T(8,128)S(1)} all-to-all(f32[16,32,128]{2,1,0:T(8,128)S(1)} %bitcast.52), channel_id=1, replica_groups=mesh['row'=16,'col'=8] {'row'}, dimensions={0} | all-to-all | bytes 524288 | tf_op jit(solution)/shard_map/all_to_all | solution.py:421
  116.8 10.2 %all_to_all.85 = f32[16,32,128]{2,1,0:T(8,128)S(1)} all-to-all(f32[16,32,128]{2,1,0:T(8,128)S(1)} %get-tuple-element.98), channel_id=1, replica_groups=mesh['row'=16,'col'=8] {'row'}, dimensions={0} | all-to-all | bytes 524288 | tf_op jit(solution)/shard_map/all_to_all | solution.py:421
  130.8 3.5 %fold.10 = (f32[128,128]{1,0:T(8,128)S(1)}, bf16[2,256,512]{2,1,0:T(8,128)(2,1)S(1)}, bf16[2,256,512]{2,1,0:T(8,128)(2,1)S(1)}, bf16[2,512,256]{2,1,0:T(8,128)(2,1)S(1)}, bf16[2,512,256]{2,1,0:T(8,128)(2,1)S(1)}) custom-call(s32[2,1,512]{2,1,0:T(1,128)S(1)} %get-tuple-element.83.refs_0_, f32[512,128]{1,0:T(8,128)S(1)} %get-tuple-element.85.refs_1_, ...), custom_call_target="tpu_custom_call" | custom-call | flops 805306368 | bytes 5242880 | tf_op jit(solution)/shard_map/fold/pallas_call | solution.py:253
  135.3 10.1 %all_to_all.86.parts_ref = f32[16,32,128]{2,1,0:T(8,128)S(1)} all-to-all(f32[16,32,128]{2,1,0:T(8,128)S(1)} %bitcast.53), channel_id=1, replica_groups=mesh['row'=16,'col'=8] {'row'}, dimensions={0} | all-to-all | bytes 524288 | tf_op jit(solution)/shard_map/all_to_all | solution.py:421
  145.5 10.2 %all_to_all.87 = f32[16,32,128]{2,1,0:T(8,128)S(1)} all-to-all(f32[16,32,128]{2,1,0:T(8,128)S(1)} %get-tuple-element.104), channel_id=1, replica_groups=mesh['row'=16,'col'=8] {'row'}, dimensions={0} | all-to-all | bytes 524288 | tf_op jit(solution)/shard_map/all_to_all | solution.py:421
  159.4 4.2 %fold.11 = (f32[128,128]{1,0:T(8,128)S(1)}, bf16[2,256,512]{2,1,0:T(8,128)(2,1)S(1)}, bf16[2,256,512]{2,1,0:T(8,128)(2,1)S(1)}, bf16[2,512,256]{2,1,0:T(8,128)(2,1)S(1)}, bf16[2,512,256]{2,1,0:T(8,128)(2,1)S(1)}) custom-call(s32[2,1,512]{2,1,0:T(1,128)S(1)} %get-tuple-element.83.refs_0_, f32[512,128]{1,0:T(8,128)S(1)} %get-tuple-element.85.refs_1_, ...), custom_call_target="tpu_custom_call" | custom-call | flops 1006632960 | bytes 6291456 | tf_op jit(solution)/shard_map/fold/pallas_call | solution.py:253
  164.1 10.4 %all_to_all.88.parts_ref = f32[16,32,128]{2,1,0:T(8,128)S(1)} all-to-all(f32[16,32,128]{2,1,0:T(8,128)S(1)} %bitcast.54), channel_id=1, replica_groups=mesh['row'=16,'col'=8] {'row'}, dimensions={0} | all-to-all | bytes 524288 | tf_op jit(solution)/shard_map/all_to_all | solution.py:421
  174.6 10.2 %all_to_all.89 = f32[16,32,128]{2,1,0:T(8,128)S(1)} all-to-all(f32[16,32,128]{2,1,0:T(8,128)S(1)} %get-tuple-element.110), channel_id=1, replica_groups=mesh['row'=16,'col'=8] {'row'}, dimensions={0} | all-to-all | bytes 524288 | tf_op jit(solution)/shard_map/all_to_all | solution.py:421
  188.6 4.8 %fold.12 = (f32[128,128]{1,0:T(8,128)S(1)}, bf16[2,256,512]{2,1,0:T(8,128)(2,1)S(1)}, bf16[2,256,512]{2,1,0:T(8,128)(2,1)S(1)}, bf16[2,512,256]{2,1,0:T(8,128)(2,1)S(1)}, bf16[2,512,256]{2,1,0:T(8,128)(2,1)S(1)}) custom-call(s32[2,1,512]{2,1,0:T(1,128)S(1)} %get-tuple-element.83.refs_0_, f32[512,128]{1,0:T(8,128)S(1)} %get-tuple-element.85.refs_1_, ...), custom_call_target="tpu_custom_call" | custom-call | flops 1207959552 | bytes 7340032 | tf_op jit(solution)/shard_map/fold/pallas_call | solution.py:253
  193.9 10.6 %all_to_all.90.parts_ref = f32[16,32,128]{2,1,0:T(8,128)S(1)} all-to-all(f32[16,32,128]{2,1,0:T(8,128)S(1)} %bitcast.55), channel_id=1, replica_groups=mesh['row'=16,'col'=8] {'row'}, dimensions={0} | all-to-all | bytes 524288 | tf_op jit(solution)/shard_map/all_to_all | solution.py:421
  204.6 10.2 %all_to_all.91 = f32[16,32,128]{2,1,0:T(8,128)S(1)} all-to-all(f32[16,32,128]{2,1,0:T(8,128)S(1)} %get-tuple-element.116), channel_id=1, replica_groups=mesh['row'=16,'col'=8] {'row'}, dimensions={0} | all-to-all | bytes 524288 | tf_op jit(solution)/shard_map/all_to_all | solution.py:421
  218.6 5.5 %fold.13 = (f32[128,128]{1,0:T(8,128)S(1)}, bf16[2,256,512]{2,1,0:T(8,128)(2,1)S(1)}, bf16[2,256,512]{2,1,0:T(8,128)(2,1)S(1)}, bf16[2,512,256]{2,1,0:T(8,128)(2,1)S(1)}, bf16[2,512,256]{2,1,0:T(8,128)(2,1)S(1)}) custom-call(s32[2,1,512]{2,1,0:T(1,128)S(1)} %get-tuple-element.83.refs_0_, f32[512,128]{1,0:T(8,128)S(1)} %get-tuple-element.85.refs_1_, ...), custom_call_target="tpu_custom_call" | custom-call | flops 1409286144 | bytes 8388608 | tf_op jit(solution)/shard_map/fold/pallas_call | solution.py:253
  224.6 10.3 %all_to_all.92.parts_ref = f32[16,32,128]{2,1,0:T(8,128)S(1)} all-to-all(f32[16,32,128]{2,1,0:T(8,128)S(1)} %bitcast.56), channel_id=1, replica_groups=mesh['row'=16,'col'=8] {'row'}, dimensions={0} | all-to-all | bytes 524288 | tf_op jit(solution)/shard_map/all_to_all | solution.py:421
  234.9 10.3 %all_to_all.93 = f32[16,32,128]{2,1,0:T(8,128)S(1)} all-to-all(f32[16,32,128]{2,1,0:T(8,128)S(1)} %get-tuple-element.122), channel_id=1, replica_groups=mesh['row'=16,'col'=8] {'row'}, dimensions={0} | all-to-all | bytes 524288 | tf_op jit(solution)/shard_map/all_to_all | solution.py:421
  245.7 26.3 %collective-permute-start.25 = (f32[7,32,128]{2,1,0:T(8,128)S(1)}, f32[7,32,128]{2,1,0:T(8,128)S(1)}, u32[]{:S(2)}, u32[]{:S(2)}) collective-permute-start(f32[7,32,128]{2,1,0:T(8,128)S(1)} %join.1.early_ref), channel_id=1, source_target_pairs={{0,1},{1,0},{2,3},{3,2},{4,5},{5,4},{6,7},{7,6},{8,9},{9,8},{10,11... | collective-permute-start | bytes 344072 | tf_op jit(solution)/shard_map/ppermute | solution.py:409
  278.3 10.2 %all_to_all.94 = f32[16,32,128]{2,1,0:T(8,128)S(1)} all-to-all(f32[16,32,128]{2,1,0:T(8,128)S(1)} %bitcast.57), channel_id=1, replica_groups=mesh['row'=16,'col'=8] {'row'}, dimensions={0} | all-to-all | bytes 524288 | tf_op jit(solution)/shard_map/all_to_all | solution.py:421
  (93 shorter events, 60.5 us)
Async XLA Ops:
  26.7 35.5 %collective-permute-start.6 = (f32[28,256,512]{2,1,0:T(8,128)}, f32[28,256,512]{2,1,0:T(8,128)}, u32[]{:S(2)}, u32[]{:S(2)}) collective-permute-start(f32[28,256,512]{2,1,0:T(8,128)} %refs_2_.13), channel_id=1, source_target_pairs={{0,1},{1,0},{2,3},{3,2},{4,5},{5,4},{6,7},{7,6},{8,9},{9,8},{10,11... | collective-permute-start | bytes 44040200 | tf_op jit(solution)/shard_map/ppermute | solution.py:409
  27.0 16.4 %collective-permute-start = (f32[8,512,256]{2,1,0:T(8,128)}, f32[8,512,256]{2,1,0:T(8,128)S(1)}, u32[]{:S(2)}, u32[]{:S(2)}) collective-permute-start(f32[8,512,256]{2,1,0:T(8,128)} %refs_4_.11), channel_id=1, source_target_pairs={{0,1},{1,0},{2,3},{3,2},{4,5},{5,4},{6,7},{7,6},{8,9},{9,8},{10,11... | collective-permute-start | bytes 12582920 | tf_op jit(solution)/shard_map/ppermute | solution.py:409
  27.3 19.3 %collective-permute-start.3 = (f32[128,128]{1,0:T(8,128)S(1)}, f32[128,128]{1,0:T(8,128)S(1)}, u32[]{:S(2)}, u32[]{:S(2)}) collective-permute-start(f32[128,128]{1,0:T(8,128)S(1)} %get-tuple-element.79.refs_0_), channel_id=1, source_target_pairs={{0,2},{1,3},{2,0},{3,1},{4,6},{5,7},{6,4},{7,5},{8,10},{9,11},{10,... | collective-permute-start | bytes 196616 | tf_op jit(solution)/shard_map/ppermute | solution.py:415
  28.5 18.1 %collective-permute-start.4 = (f32[128,128]{1,0:T(8,128)S(1)}, f32[128,128]{1,0:T(8,128)S(1)}, u32[]{:S(2)}, u32[]{:S(2)}) collective-permute-start(f32[128,128]{1,0:T(8,128)S(1)} %get-tuple-element.79.refs_0_), channel_id=1, source_target_pairs={{0,6},{1,7},{2,4},{3,5},{4,2},{5,3},{6,0},{7,1},{8,14},{9,15},{10,... | collective-permute-start | bytes 196616 | tf_op jit(solution)/shard_map/ppermute | solution.py:415
  30.4 16.3 %collective-permute-start.5 = (f32[128,128]{1,0:T(8,128)S(1)}, f32[128,128]{1,0:T(8,128)S(1)}, u32[]{:S(2)}, u32[]{:S(2)}) collective-permute-start(f32[128,128]{1,0:T(8,128)S(1)} %get-tuple-element.79.refs_0_), channel_id=1, source_target_pairs={{0,4},{1,5},{2,6},{3,7},{4,0},{5,1},{6,2},{7,3},{8,12},{9,13},{10,... | collective-permute-start | bytes 196616 | tf_op jit(solution)/shard_map/ppermute | solution.py:415
  58.7 11.0 %all-to-all-start.2 = ((f32[16,32,128]{2,1,0:T(8,128)}), f32[16,32,128]{2,1,0:T(8,128)S(1)}, u32[]{:S(2)}, u32[]{:S(2)}) async-start(f32[16,32,128]{2,1,0:T(8,128)} %get-tuple-element.82), calls=%async_computation.2 | async-start | bytes 524288 | tf_op jit(solution)/shard_map/all_to_all | solution.py:421
  70.2 6.0 %collective-permute-start.7 = (f32[128,128]{1,0:T(8,128)S(1)}, f32[128,128]{1,0:T(8,128)S(1)}, u32[]{:S(2)}, u32[]{:S(2)}) collective-permute-start(f32[128,128]{1,0:T(8,128)S(1)} %lower.7.refs_0_), channel_id=1, source_target_pairs={{0,2},{1,3},{2,0},{3,1},{4,6},{5,7},{6,4},{7,5},{8,10},{9,11},{10,... | collective-permute-start | bytes 196616 | tf_op jit(solution)/shard_map/ppermute | solution.py:415
  99.9 6.2 %collective-permute-start.10 = (f32[128,128]{1,0:T(8,128)S(1)}, f32[128,128]{1,0:T(8,128)S(1)}, u32[]{:S(2)}, u32[]{:S(2)}) collective-permute-start(f32[128,128]{1,0:T(8,128)S(1)} %lower.8.refs_0_), channel_id=1, source_target_pairs={{0,2},{1,3},{2,0},{3,1},{4,6},{5,7},{6,4},{7,5},{8,10},{9,11},{10,... | collective-permute-start | bytes 196616 | tf_op jit(solution)/shard_map/ppermute | solution.py:415
  100.6 5.5 %collective-permute-start.11 = (f32[128,128]{1,0:T(8,128)S(1)}, f32[128,128]{1,0:T(8,128)S(1)}, u32[]{:S(2)}, u32[]{:S(2)}) collective-permute-start(f32[128,128]{1,0:T(8,128)S(1)} %lower.8.refs_0_), channel_id=1, source_target_pairs={{0,6},{1,7},{2,4},{3,5},{4,2},{5,3},{6,0},{7,1},{8,14},{9,15},{10,... | collective-permute-start | bytes 196616 | tf_op jit(solution)/shard_map/ppermute | solution.py:415
  101.2 4.9 %collective-permute-start.12 = (f32[128,128]{1,0:T(8,128)S(1)}, f32[128,128]{1,0:T(8,128)S(1)}, u32[]{:S(2)}, u32[]{:S(2)}) collective-permute-start(f32[128,128]{1,0:T(8,128)S(1)} %lower.8.refs_0_), channel_id=1, source_target_pairs={{0,4},{1,5},{2,6},{3,7},{4,0},{5,1},{6,2},{7,3},{8,12},{9,13},{10,... | collective-permute-start | bytes 196616 | tf_op jit(solution)/shard_map/ppermute | solution.py:415
  127.4 6.8 %collective-permute-start.13 = (f32[128,128]{1,0:T(8,128)S(1)}, f32[128,128]{1,0:T(8,128)S(1)}, u32[]{:S(2)}, u32[]{:S(2)}) collective-permute-start(f32[128,128]{1,0:T(8,128)S(1)} %lower.9.refs_0_), channel_id=1, source_target_pairs={{0,2},{1,3},{2,0},{3,1},{4,6},{5,7},{6,4},{7,5},{8,10},{9,11},{10,... | collective-permute-start | bytes 196616 | tf_op jit(solution)/shard_map/ppermute | solution.py:415
  128.2 6.1 %collective-permute-start.14 = (f32[128,128]{1,0:T(8,128)S(1)}, f32[128,128]{1,0:T(8,128)S(1)}, u32[]{:S(2)}, u32[]{:S(2)}) collective-permute-start(f32[128,128]{1,0:T(8,128)S(1)} %lower.9.refs_0_), channel_id=1, source_target_pairs={{0,6},{1,7},{2,4},{3,5},{4,2},{5,3},{6,0},{7,1},{8,14},{9,15},{10,... | collective-permute-start | bytes 196616 | tf_op jit(solution)/shard_map/ppermute | solution.py:415
  129.8 4.9 %collective-permute-start.15 = (f32[128,128]{1,0:T(8,128)S(1)}, f32[128,128]{1,0:T(8,128)S(1)}, u32[]{:S(2)}, u32[]{:S(2)}) collective-permute-start(f32[128,128]{1,0:T(8,128)S(1)} %lower.9.refs_0_), channel_id=1, source_target_pairs={{0,4},{1,5},{2,6},{3,7},{4,0},{5,1},{6,2},{7,3},{8,12},{9,13},{10,... | collective-permute-start | bytes 196616 | tf_op jit(solution)/shard_map/ppermute | solution.py:415
  156.1 7.5 %collective-permute-start.16 = (f32[128,128]{1,0:T(8,128)S(1)}, f32[128,128]{1,0:T(8,128)S(1)}, u32[]{:S(2)}, u32[]{:S(2)}) collective-permute-start(f32[128,128]{1,0:T(8,128)S(1)} %lower.10.refs_0_), channel_id=1, source_target_pairs={{0,2},{1,3},{2,0},{3,1},{4,6},{5,7},{6,4},{7,5},{8,10},{9,11},{10,... | collective-permute-start | bytes 196616 | tf_op jit(solution)/shard_map/ppermute | solution.py:415
  156.5 7.1 %collective-permute-start.17 = (f32[128,128]{1,0:T(8,128)S(1)}, f32[128,128]{1,0:T(8,128)S(1)}, u32[]{:S(2)}, u32[]{:S(2)}) collective-permute-start(f32[128,128]{1,0:T(8,128)S(1)} %lower.10.refs_0_), channel_id=1, source_target_pairs={{0,6},{1,7},{2,4},{3,5},{4,2},{5,3},{6,0},{7,1},{8,14},{9,15},{10,... | collective-permute-start | bytes 196616 | tf_op jit(solution)/shard_map/ppermute | solution.py:415
  158.2 5.4 %collective-permute-start.18 = (f32[128,128]{1,0:T(8,128)S(1)}, f32[128,128]{1,0:T(8,128)S(1)}, u32[]{:S(2)}, u32[]{:S(2)}) collective-permute-start(f32[128,128]{1,0:T(8,128)S(1)} %lower.10.refs_0_), channel_id=1, source_target_pairs={{0,4},{1,5},{2,6},{3,7},{4,0},{5,1},{6,2},{7,3},{8,12},{9,13},{10,... | collective-permute-start | bytes 196616 | tf_op jit(solution)/shard_map/ppermute | solution.py:415
  185.3 8.1 %collective-permute-start.19 = (f32[128,128]{1,0:T(8,128)S(1)}, f32[128,128]{1,0:T(8,128)S(1)}, u32[]{:S(2)}, u32[]{:S(2)}) collective-permute-start(f32[128,128]{1,0:T(8,128)S(1)} %lower.11.refs_0_), channel_id=1, source_target_pairs={{0,2},{1,3},{2,0},{3,1},{4,6},{5,7},{6,4},{7,5},{8,10},{9,11},{10,... | collective-permute-start | bytes 196616 | tf_op jit(solution)/shard_map/ppermute | solution.py:415
  185.7 7.7 %collective-permute-start.20 = (f32[128,128]{1,0:T(8,128)S(1)}, f32[128,128]{1,0:T(8,128)S(1)}, u32[]{:S(2)}, u32[]{:S(2)}) collective-permute-start(f32[128,128]{1,0:T(8,128)S(1)} %lower.11.refs_0_), channel_id=1, source_target_pairs={{0,6},{1,7},{2,4},{3,5},{4,2},{5,3},{6,0},{7,1},{8,14},{9,15},{10,... | collective-permute-start | bytes 196616 | tf_op jit(solution)/shard_map/ppermute | solution.py:415
  187.3 6.1 %collective-permute-start.21 = (f32[128,128]{1,0:T(8,128)S(1)}, f32[128,128]{1,0:T(8,128)S(1)}, u32[]{:S(2)}, u32[]{:S(2)}) collective-permute-start(f32[128,128]{1,0:T(8,128)S(1)} %lower.11.refs_0_), channel_id=1, source_target_pairs={{0,4},{1,5},{2,6},{3,7},{4,0},{5,1},{6,2},{7,3},{8,12},{9,13},{10,... | collective-permute-start | bytes 196616 | tf_op jit(solution)/shard_map/ppermute | solution.py:415
  215.2 8.8 %collective-permute-start.22 = (f32[128,128]{1,0:T(8,128)S(1)}, f32[128,128]{1,0:T(8,128)S(1)}, u32[]{:S(2)}, u32[]{:S(2)}) collective-permute-start(f32[128,128]{1,0:T(8,128)S(1)} %lower.12.refs_0_), channel_id=1, source_target_pairs={{0,2},{1,3},{2,0},{3,1},{4,6},{5,7},{6,4},{7,5},{8,10},{9,11},{10,... | collective-permute-start | bytes 196616 | tf_op jit(solution)/shard_map/ppermute | solution.py:415
  215.3 8.7 %collective-permute-start.23 = (f32[128,128]{1,0:T(8,128)S(1)}, f32[128,128]{1,0:T(8,128)S(1)}, u32[]{:S(2)}, u32[]{:S(2)}) collective-permute-start(f32[128,128]{1,0:T(8,128)S(1)} %lower.12.refs_0_), channel_id=1, source_target_pairs={{0,6},{1,7},{2,4},{3,5},{4,2},{5,3},{6,0},{7,1},{8,14},{9,15},{10,... | collective-permute-start | bytes 196616 | tf_op jit(solution)/shard_map/ppermute | solution.py:415
  216.9 7.2 %collective-permute-start.24 = (f32[128,128]{1,0:T(8,128)S(1)}, f32[128,128]{1,0:T(8,128)S(1)}, u32[]{:S(2)}, u32[]{:S(2)}) collective-permute-start(f32[128,128]{1,0:T(8,128)S(1)} %lower.12.refs_0_), channel_id=1, source_target_pairs={{0,4},{1,5},{2,6},{3,7},{4,0},{5,1},{6,2},{7,3},{8,12},{9,13},{10,... | collective-permute-start | bytes 196616 | tf_op jit(solution)/shard_map/ppermute | solution.py:415
  245.7 30.9 %collective-permute-start.25 = (f32[7,32,128]{2,1,0:T(8,128)S(1)}, f32[7,32,128]{2,1,0:T(8,128)S(1)}, u32[]{:S(2)}, u32[]{:S(2)}) collective-permute-start(f32[7,32,128]{2,1,0:T(8,128)S(1)} %join.1.early_ref), channel_id=1, source_target_pairs={{0,1},{1,0},{2,3},{3,2},{4,5},{5,4},{6,7},{7,6},{8,9},{9,8},{10,11... | collective-permute-start | bytes 344072 | tf_op jit(solution)/shard_map/ppermute | solution.py:409
  272.0 4.7 %collective-permute-start.27 = (f32[128,128]{1,0:T(8,128)S(1)}, f32[128,128]{1,0:T(8,128)S(1)}, u32[]{:S(2)}, u32[]{:S(2)}) collective-permute-start(f32[128,128]{1,0:T(8,128)S(1)} %lower.13.refs_0_), channel_id=1, source_target_pairs={{0,6},{1,7},{2,4},{3,5},{4,2},{5,3},{6,0},{7,1},{8,14},{9,15},{10,... | collective-permute-start | bytes 196616 | tf_op jit(solution)/shard_map/ppermute | solution.py:415
  (9 other events, 30.2 us)

commit v7 on v6

--- a/solution.py
+++ b/solution.py
@@ -429,12 +429,14 @@
     rotor = sub_field.shape[1]
     peers = lax.axis_size("row")
     core = (lax.axis_index("col") % 2).astype(jnp.int32).reshape(1)
-    diags = (diag_inverse, other_core(diag_inverse))
+    other_diag = other_core(diag_inverse)
     picked, targets = pick(
         core, sub_field, reluctivity, stride, counts, source_cell, target_row[0, 0]
     )
     other_targets = other_core(targets)
     received = per_row(picked).reshape(-1, rotor)
+    received, other_diag = lax.optimization_barrier((received, other_diag))
+    diags = (diag_inverse, other_diag)
 
     shares = []
     pieces = []

time: 294 us -> 283 us (0.963)
  waiting for transfers between devices: 24.1 us -> 14.5 us
    ppermute x6, waiting for transfers between devices: 14.6 us -> 2.21 us  [other_core(): return lax.ppermute(value, 'col', [(i, i ^ 1) for i in range(peers)])]
  transfers between devices with their start and end apart: 31 -> 31, of which waited for: 8 -> 9; matrix products, arithmetic and copies ran while one was open for 0% -> 0% of each run, Pallas kernels for 10% -> 12%
where the time goes in v7:
time: 283 us
  blocking collectives  160 us (57%)
  starting transfers between devices  64.6 us (23%)
  Pallas kernels  41.7 us (15%)
  waiting for transfers between devices  14.5 us (5%)
    all_to_all x15, blocking collectives, per_row(): return lax.all_to_all(value, 'row', 0, 0, tiled=True)  160 us
    ppermute x6, starting transfers between devices, other_core(): return lax.ppermute(value, 'col', [(i, i ^ 1) for i in range(peers)])  34.1 us
    ppermute x24, starting transfers between devices, along_x(): lax.ppermute(value, 'col', [(i, i ^ apart) for i in range(peers)])  26.9 us
    pallas_call x7, Pallas kernels, fold(): pl.pallas_call(functools.partial(fold_kernel, block, bool(diags)), out_sh...  24.3 us
    all_to_all x1, waiting for transfers between devices, per_row(): return lax.all_to_all(value, 'row', 0, 0, tiled=True)  6.17 us
    ppermute x24, waiting for transfers between devices, along_x(): lax.ppermute(value, 'col', [(i, i ^ apart) for i in range(peers)])  6.15 us
  transfers between devices with their start and end apart: 31, of which 9 were waited for; matrix products, arithmetic and copies ran while one was open for 0% of the time, Pallas kernels for 12%

profile of v7, /device:TPU:1, one launch (start us, length us, event | category | flops | bytes accessed | tf_op | source)
XLA Modules:
  0.0 282.5 jit_solution(7433661992130511855)
XLA Ops:
  2.1 4.9 %pick.1 = (f32[16,32,128]{2,1,0:T(8,128)}, s32[1,512]{1,0:T(1,128)}) custom-call(s32[1]{0:T(128)} %bitcast.core_ref, s32[1]{0:T(128)S(6)} %copy.10.stride_hbm, s32[1,16]{1,0:T(1,128)} %counts_hbm.1, s32[1,16,32]{2,1,0:T(8,128)} %source_hbm.1, s32[16,32]{1,0:T(8,128)} %bitcast.59, f32[2048,128]{1,0:T(8,128)} %field_hbm.1, f32[2,2048,128]{2,1,0:T(8,128)} %nu_hbm.1), custom_call_target="tpu_custom_call" | custom-call | tf_op jit(solution)/shard_map/pick/pallas_call | solution.py:80
  7.0 16.4 %all_to_all.80 = f32[16,32,128]{2,1,0:T(8,128)S(1)} all-to-all(f32[16,32,128]{2,1,0:T(8,128)} %get-tuple-element.77), channel_id=1, replica_groups=mesh['row'=16,'col'=8] {'row'}, dimensions={0} | all-to-all | bytes 524288 | tf_op jit(solution)/shard_map/all_to_all | solution.py:421
  35.8 10.2 %all_to_all.81.parts_ref = f32[16,32,128]{2,1,0:T(8,128)S(1)} all-to-all(f32[16,32,128]{2,1,0:T(8,128)S(1)} %bitcast.50), channel_id=1, replica_groups=mesh['row'=16,'col'=8] {'row'}, dimensions={0} | all-to-all | bytes 524288 | tf_op jit(solution)/shard_map/all_to_all | solution.py:421
  46.8 3.5 %all-to-all-start.2 = ((f32[16,32,128]{2,1,0:T(8,128)}), f32[16,32,128]{2,1,0:T(8,128)S(1)}, u32[]{:S(2)}, u32[]{:S(2)}) async-start(f32[16,32,128]{2,1,0:T(8,128)} %get-tuple-element.86), calls=%async_computation.2 | async-start | bytes 524288 | tf_op jit(solution)/shard_map/all_to_all | solution.py:421
  51.6 6.2 %all-to-all-done.2 = f32[16,32,128]{2,1,0:T(8,128)S(1)} async-done(((f32[16,32,128]{2,1,0:T(8,128)}), f32[16,32,128]{2,1,0:T(8,128)S(1)}, u32[]{:S(2)}, u32[]{:S(2)}) %all-to-all-start.2) | async-done | bytes 262176 | tf_op jit(solution)/shard_map/all_to_all | solution.py:421
  64.6 10.1 %all_to_all.82.parts_ref = f32[16,32,128]{2,1,0:T(8,128)S(1)} all-to-all(f32[16,32,128]{2,1,0:T(8,128)S(1)} %bitcast.51), channel_id=1, replica_groups=mesh['row'=16,'col'=8] {'row'}, dimensions={0} | all-to-all | bytes 524288 | tf_op jit(solution)/shard_map/all_to_all | solution.py:421
  74.8 10.2 %all_to_all.83 = f32[16,32,128]{2,1,0:T(8,128)S(1)} all-to-all(f32[16,32,128]{2,1,0:T(8,128)S(1)} %get-tuple-element.96), channel_id=1, replica_groups=mesh['row'=16,'col'=8] {'row'}, dimensions={0} | all-to-all | bytes 524288 | tf_op jit(solution)/shard_map/all_to_all | solution.py:421
  93.4 10.1 %all_to_all.84.parts_ref = f32[16,32,128]{2,1,0:T(8,128)S(1)} all-to-all(f32[16,32,128]{2,1,0:T(8,128)S(1)} %bitcast.52), channel_id=1, replica_groups=mesh['row'=16,'col'=8] {'row'}, dimensions={0} | all-to-all | bytes 524288 | tf_op jit(solution)/shard_map/all_to_all | solution.py:421
  103.6 10.7 %all_to_all.85 = f32[16,32,128]{2,1,0:T(8,128)S(1)} all-to-all(f32[16,32,128]{2,1,0:T(8,128)S(1)} %get-tuple-element.102), channel_id=1, replica_groups=mesh['row'=16,'col'=8] {'row'}, dimensions={0} | all-to-all | bytes 524288 | tf_op jit(solution)/shard_map/all_to_all | solution.py:421
  118.0 3.5 %fold.10 = (f32[128,128]{1,0:T(8,128)S(1)}, bf16[2,256,512]{2,1,0:T(8,128)(2,1)S(1)}, bf16[2,256,512]{2,1,0:T(8,128)(2,1)S(1)}, bf16[2,512,256]{2,1,0:T(8,128)(2,1)S(1)}, bf16[2,512,256]{2,1,0:T(8,128)(2,1)S(1)}) custom-call(s32[2,1,512]{2,1,0:T(1,128)S(1)} %get-tuple-element.87.refs_0_, f32[512,128]{1,0:T(8,128)S(1)} %get-tuple-element.89.refs_1_, ...), custom_call_target="tpu_custom_call" | custom-call | flops 805306368 | bytes 5242880 | tf_op jit(solution)/shard_map/fold/pallas_call | solution.py:253
  122.1 10.1 %all_to_all.86.parts_ref = f32[16,32,128]{2,1,0:T(8,128)S(1)} all-to-all(f32[16,32,128]{2,1,0:T(8,128)S(1)} %bitcast.53), channel_id=1, replica_groups=mesh['row'=16,'col'=8] {'row'}, dimensions={0} | all-to-all | bytes 524288 | tf_op jit(solution)/shard_map/all_to_all | solution.py:421
  132.3 10.2 %all_to_all.87 = f32[16,32,128]{2,1,0:T(8,128)S(1)} all-to-all(f32[16,32,128]{2,1,0:T(8,128)S(1)} %get-tuple-element.108), channel_id=1, replica_groups=mesh['row'=16,'col'=8] {'row'}, dimensions={0} | all-to-all | bytes 524288 | tf_op jit(solution)/shard_map/all_to_all | solution.py:421
  146.2 4.1 %fold.11 = (f32[128,128]{1,0:T(8,128)S(1)}, bf16[2,256,512]{2,1,0:T(8,128)(2,1)S(1)}, bf16[2,256,512]{2,1,0:T(8,128)(2,1)S(1)}, bf16[2,512,256]{2,1,0:T(8,128)(2,1)S(1)}, bf16[2,512,256]{2,1,0:T(8,128)(2,1)S(1)}) custom-call(s32[2,1,512]{2,1,0:T(1,128)S(1)} %get-tuple-element.87.refs_0_, f32[512,128]{1,0:T(8,128)S(1)} %get-tuple-element.89.refs_1_, ...), custom_call_target="tpu_custom_call" | custom-call | flops 1006632960 | bytes 6291456 | tf_op jit(solution)/shard_map/fold/pallas_call | solution.py:253
  150.9 10.2 %all_to_all.88.parts_ref = f32[16,32,128]{2,1,0:T(8,128)S(1)} all-to-all(f32[16,32,128]{2,1,0:T(8,128)S(1)} %bitcast.54), channel_id=1, replica_groups=mesh['row'=16,'col'=8] {'row'}, dimensions={0} | all-to-all | bytes 524288 | tf_op jit(solution)/shard_map/all_to_all | solution.py:421
  161.1 10.2 %all_to_all.89 = f32[16,32,128]{2,1,0:T(8,128)S(1)} all-to-all(f32[16,32,128]{2,1,0:T(8,128)S(1)} %get-tuple-element.114), channel_id=1, replica_groups=mesh['row'=16,'col'=8] {'row'}, dimensions={0} | all-to-all | bytes 524288 | tf_op jit(solution)/shard_map/all_to_all | solution.py:421
  175.1 4.8 %fold.12 = (f32[128,128]{1,0:T(8,128)S(1)}, bf16[2,256,512]{2,1,0:T(8,128)(2,1)S(1)}, bf16[2,256,512]{2,1,0:T(8,128)(2,1)S(1)}, bf16[2,512,256]{2,1,0:T(8,128)(2,1)S(1)}, bf16[2,512,256]{2,1,0:T(8,128)(2,1)S(1)}) custom-call(s32[2,1,512]{2,1,0:T(1,128)S(1)} %get-tuple-element.87.refs_0_, f32[512,128]{1,0:T(8,128)S(1)} %get-tuple-element.89.refs_1_, ...), custom_call_target="tpu_custom_call" | custom-call | flops 1207959552 | bytes 7340032 | tf_op jit(solution)/shard_map/fold/pallas_call | solution.py:253
  180.5 10.9 %all_to_all.90.parts_ref = f32[16,32,128]{2,1,0:T(8,128)S(1)} all-to-all(f32[16,32,128]{2,1,0:T(8,128)S(1)} %bitcast.55), channel_id=1, replica_groups=mesh['row'=16,'col'=8] {'row'}, dimensions={0} | all-to-all | bytes 524288 | tf_op jit(solution)/shard_map/all_to_all | solution.py:421
  191.4 10.3 %all_to_all.91 = f32[16,32,128]{2,1,0:T(8,128)S(1)} all-to-all(f32[16,32,128]{2,1,0:T(8,128)S(1)} %get-tuple-element.120), channel_id=1, replica_groups=mesh['row'=16,'col'=8] {'row'}, dimensions={0} | all-to-all | bytes 524288 | tf_op jit(solution)/shard_map/all_to_all | solution.py:421
  205.5 5.4 %fold.13 = (f32[128,128]{1,0:T(8,128)S(1)}, bf16[2,256,512]{2,1,0:T(8,128)(2,1)S(1)}, bf16[2,256,512]{2,1,0:T(8,128)(2,1)S(1)}, bf16[2,512,256]{2,1,0:T(8,128)(2,1)S(1)}, bf16[2,512,256]{2,1,0:T(8,128)(2,1)S(1)}) custom-call(s32[2,1,512]{2,1,0:T(1,128)S(1)} %get-tuple-element.87.refs_0_, f32[512,128]{1,0:T(8,128)S(1)} %get-tuple-element.89.refs_1_, ...), custom_call_target="tpu_custom_call" | custom-call | flops 1409286144 | bytes 8388608 | tf_op jit(solution)/shard_map/fold/pallas_call | solution.py:253
  211.4 10.2 %all_to_all.92.parts_ref = f32[16,32,128]{2,1,0:T(8,128)S(1)} all-to-all(f32[16,32,128]{2,1,0:T(8,128)S(1)} %bitcast.56), channel_id=1, replica_groups=mesh['row'=16,'col'=8] {'row'}, dimensions={0} | all-to-all | bytes 524288 | tf_op jit(solution)/shard_map/all_to_all | solution.py:421
  221.7 10.1 %all_to_all.93 = f32[16,32,128]{2,1,0:T(8,128)S(1)} all-to-all(f32[16,32,128]{2,1,0:T(8,128)S(1)} %get-tuple-element.126), channel_id=1, replica_groups=mesh['row'=16,'col'=8] {'row'}, dimensions={0} | all-to-all | bytes 524288 | tf_op jit(solution)/shard_map/all_to_all | solution.py:421
  232.3 28.1 %collective-permute-start.25 = (f32[7,32,128]{2,1,0:T(8,128)S(1)}, f32[7,32,128]{2,1,0:T(8,128)S(1)}, u32[]{:S(2)}, u32[]{:S(2)}) collective-permute-start(f32[7,32,128]{2,1,0:T(8,128)S(1)} %join.1.early_ref), channel_id=1, source_target_pairs={{0,1},{1,0},{2,3},{3,2},{4,5},{5,4},{6,7},{7,6},{8,9},{9,8},{10,11... | collective-permute-start | bytes 344072 | tf_op jit(solution)/shard_map/ppermute | solution.py:409
  267.4 10.2 %all_to_all.94 = f32[16,32,128]{2,1,0:T(8,128)S(1)} all-to-all(f32[16,32,128]{2,1,0:T(8,128)S(1)} %bitcast.57), channel_id=1, replica_groups=mesh['row'=16,'col'=8] {'row'}, dimensions={0} | all-to-all | bytes 524288 | tf_op jit(solution)/shard_map/all_to_all | solution.py:421
  277.6 3.3 %collective-permute-start.29 = (f32[32,128]{1,0:T(8,128)S(1)}, f32[32,128]{1,0:T(8,128)S(1)}, u32[]{:S(2)}, u32[]{:S(2)}) collective-permute-start(f32[32,128]{1,0:T(8,128)S(1)} %reduce_sum.9.last_ref), channel_id=1, source_target_pairs={{0,1},{1,0},{2,3},{3,2},{4,5},{5,4},{6,7},{7,6},{8,9},{9,8},{10,11... | collective-permute-start | bytes 49160 | tf_op jit(solution)/shard_map/ppermute | solution.py:409
  (91 shorter events, 57.7 us)
Async XLA Ops:
  0.0 23.4 %collective-permute-start = (f32[8,512,256]{2,1,0:T(8,128)}, f32[8,512,256]{2,1,0:T(8,128)}, u32[]{:S(2)}, u32[]{:S(2)}) collective-permute-start(f32[8,512,256]{2,1,0:T(8,128)} %refs_4_.11), channel_id=1, source_target_pairs={{0,1},{1,0},{2,3},{3,2},{4,5},{5,4},{6,7},{7,6},{8,9},{9,8},{10,11... | collective-permute-start | bytes 12582920 | tf_op jit(solution)/shard_map/ppermute | solution.py:409
  27.4 22.9 %collective-permute-start.6 = (f32[28,256,512]{2,1,0:T(8,128)}, f32[28,256,512]{2,1,0:T(8,128)}, u32[]{:S(2)}, u32[]{:S(2)}) collective-permute-start(f32[28,256,512]{2,1,0:T(8,128)} %refs_2_.13), channel_id=1, source_target_pairs={{0,1},{1,0},{2,3},{3,2},{4,5},{5,4},{6,7},{7,6},{8,9},{9,8},{10,11... | collective-permute-start | bytes 44040200 | tf_op jit(solution)/shard_map/ppermute | solution.py:409
  27.7 5.0 %collective-permute-start.3 = (f32[128,128]{1,0:T(8,128)S(1)}, f32[128,128]{1,0:T(8,128)S(1)}, u32[]{:S(2)}, u32[]{:S(2)}) collective-permute-start(f32[128,128]{1,0:T(8,128)S(1)} %get-tuple-element.83.refs_0_), channel_id=1, source_target_pairs={{0,2},{1,3},{2,0},{3,1},{4,6},{5,7},{6,4},{7,5},{8,10},{9,11},{10,... | collective-permute-start | bytes 196616 | tf_op jit(solution)/shard_map/ppermute | solution.py:415
  30.7 4.6 %collective-permute-start.5 = (f32[128,128]{1,0:T(8,128)S(1)}, f32[128,128]{1,0:T(8,128)S(1)}, u32[]{:S(2)}, u32[]{:S(2)}) collective-permute-start(f32[128,128]{1,0:T(8,128)S(1)} %get-tuple-element.83.refs_0_), channel_id=1, source_target_pairs={{0,4},{1,5},{2,6},{3,7},{4,0},{5,1},{6,2},{7,3},{8,12},{9,13},{10,... | collective-permute-start | bytes 196616 | tf_op jit(solution)/shard_map/ppermute | solution.py:415
  46.8 11.0 %all-to-all-start.2 = ((f32[16,32,128]{2,1,0:T(8,128)}), f32[16,32,128]{2,1,0:T(8,128)S(1)}, u32[]{:S(2)}, u32[]{:S(2)}) async-start(f32[16,32,128]{2,1,0:T(8,128)} %get-tuple-element.86), calls=%async_computation.2 | async-start | bytes 524288 | tf_op jit(solution)/shard_map/all_to_all | solution.py:421
  58.3 5.5 %collective-permute-start.7 = (f32[128,128]{1,0:T(8,128)S(1)}, f32[128,128]{1,0:T(8,128)S(1)}, u32[]{:S(2)}, u32[]{:S(2)}) collective-permute-start(f32[128,128]{1,0:T(8,128)S(1)} %lower.7.refs_0_), channel_id=1, source_target_pairs={{0,2},{1,3},{2,0},{3,1},{4,6},{5,7},{6,4},{7,5},{8,10},{9,11},{10,... | collective-permute-start | bytes 196616 | tf_op jit(solution)/shard_map/ppermute | solution.py:415
  58.7 5.2 %collective-permute-start.8 = (f32[128,128]{1,0:T(8,128)S(1)}, f32[128,128]{1,0:T(8,128)S(1)}, u32[]{:S(2)}, u32[]{:S(2)}) collective-permute-start(f32[128,128]{1,0:T(8,128)S(1)} %lower.7.refs_0_), channel_id=1, source_target_pairs={{0,6},{1,7},{2,4},{3,5},{4,2},{5,3},{6,0},{7,1},{8,14},{9,15},{10,... | collective-permute-start | bytes 196616 | tf_op jit(solution)/shard_map/ppermute | solution.py:415
  59.5 4.6 %collective-permute-start.9 = (f32[128,128]{1,0:T(8,128)S(1)}, f32[128,128]{1,0:T(8,128)S(1)}, u32[]{:S(2)}, u32[]{:S(2)}) collective-permute-start(f32[128,128]{1,0:T(8,128)S(1)} %lower.7.refs_0_), channel_id=1, source_target_pairs={{0,4},{1,5},{2,6},{3,7},{4,0},{5,1},{6,2},{7,3},{8,12},{9,13},{10,... | collective-permute-start | bytes 196616 | tf_op jit(solution)/shard_map/ppermute | solution.py:415
  85.4 6.2 %collective-permute-start.10 = (f32[128,128]{1,0:T(8,128)S(1)}, f32[128,128]{1,0:T(8,128)S(1)}, u32[]{:S(2)}, u32[]{:S(2)}) collective-permute-start(f32[128,128]{1,0:T(8,128)S(1)} %lower.8.refs_0_), channel_id=1, source_target_pairs={{0,2},{1,3},{2,0},{3,1},{4,6},{5,7},{6,4},{7,5},{8,10},{9,11},{10,... | collective-permute-start | bytes 196616 | tf_op jit(solution)/shard_map/ppermute | solution.py:415
  86.2 5.4 %collective-permute-start.11 = (f32[128,128]{1,0:T(8,128)S(1)}, f32[128,128]{1,0:T(8,128)S(1)}, u32[]{:S(2)}, u32[]{:S(2)}) collective-permute-start(f32[128,128]{1,0:T(8,128)S(1)} %lower.8.refs_0_), channel_id=1, source_target_pairs={{0,6},{1,7},{2,4},{3,5},{4,2},{5,3},{6,0},{7,1},{8,14},{9,15},{10,... | collective-permute-start | bytes 196616 | tf_op jit(solution)/shard_map/ppermute | solution.py:415
  88.0 4.9 %collective-permute-start.12 = (f32[128,128]{1,0:T(8,128)S(1)}, f32[128,128]{1,0:T(8,128)S(1)}, u32[]{:S(2)}, u32[]{:S(2)}) collective-permute-start(f32[128,128]{1,0:T(8,128)S(1)} %lower.8.refs_0_), channel_id=1, source_target_pairs={{0,4},{1,5},{2,6},{3,7},{4,0},{5,1},{6,2},{7,3},{8,12},{9,13},{10,... | collective-permute-start | bytes 196616 | tf_op jit(solution)/shard_map/ppermute | solution.py:415
  114.7 6.8 %collective-permute-start.13 = (f32[128,128]{1,0:T(8,128)S(1)}, f32[128,128]{1,0:T(8,128)S(1)}, u32[]{:S(2)}, u32[]{:S(2)}) collective-permute-start(f32[128,128]{1,0:T(8,128)S(1)} %lower.9.refs_0_), channel_id=1, source_target_pairs={{0,2},{1,3},{2,0},{3,1},{4,6},{5,7},{6,4},{7,5},{8,10},{9,11},{10,... | collective-permute-start | bytes 196616 | tf_op jit(solution)/shard_map/ppermute | solution.py:415
  115.1 6.4 %collective-permute-start.14 = (f32[128,128]{1,0:T(8,128)S(1)}, f32[128,128]{1,0:T(8,128)S(1)}, u32[]{:S(2)}, u32[]{:S(2)}) collective-permute-start(f32[128,128]{1,0:T(8,128)S(1)} %lower.9.refs_0_), channel_id=1, source_target_pairs={{0,6},{1,7},{2,4},{3,5},{4,2},{5,3},{6,0},{7,1},{8,14},{9,15},{10,... | collective-permute-start | bytes 196616 | tf_op jit(solution)/shard_map/ppermute | solution.py:415
  116.5 5.1 %collective-permute-start.15 = (f32[128,128]{1,0:T(8,128)S(1)}, f32[128,128]{1,0:T(8,128)S(1)}, u32[]{:S(2)}, u32[]{:S(2)}) collective-permute-start(f32[128,128]{1,0:T(8,128)S(1)} %lower.9.refs_0_), channel_id=1, source_target_pairs={{0,4},{1,5},{2,6},{3,7},{4,0},{5,1},{6,2},{7,3},{8,12},{9,13},{10,... | collective-permute-start | bytes 196616 | tf_op jit(solution)/shard_map/ppermute | solution.py:415
  142.9 7.5 %collective-permute-start.16 = (f32[128,128]{1,0:T(8,128)S(1)}, f32[128,128]{1,0:T(8,128)S(1)}, u32[]{:S(2)}, u32[]{:S(2)}) collective-permute-start(f32[128,128]{1,0:T(8,128)S(1)} %lower.10.refs_0_), channel_id=1, source_target_pairs={{0,2},{1,3},{2,0},{3,1},{4,6},{5,7},{6,4},{7,5},{8,10},{9,11},{10,... | collective-permute-start | bytes 196616 | tf_op jit(solution)/shard_map/ppermute | solution.py:415
  143.3 7.1 %collective-permute-start.17 = (f32[128,128]{1,0:T(8,128)S(1)}, f32[128,128]{1,0:T(8,128)S(1)}, u32[]{:S(2)}, u32[]{:S(2)}) collective-permute-start(f32[128,128]{1,0:T(8,128)S(1)} %lower.10.refs_0_), channel_id=1, source_target_pairs={{0,6},{1,7},{2,4},{3,5},{4,2},{5,3},{6,0},{7,1},{8,14},{9,15},{10,... | collective-permute-start | bytes 196616 | tf_op jit(solution)/shard_map/ppermute | solution.py:415
  144.9 5.5 %collective-permute-start.18 = (f32[128,128]{1,0:T(8,128)S(1)}, f32[128,128]{1,0:T(8,128)S(1)}, u32[]{:S(2)}, u32[]{:S(2)}) collective-permute-start(f32[128,128]{1,0:T(8,128)S(1)} %lower.10.refs_0_), channel_id=1, source_target_pairs={{0,4},{1,5},{2,6},{3,7},{4,0},{5,1},{6,2},{7,3},{8,12},{9,13},{10,... | collective-permute-start | bytes 196616 | tf_op jit(solution)/shard_map/ppermute | solution.py:415
  171.8 8.1 %collective-permute-start.19 = (f32[128,128]{1,0:T(8,128)S(1)}, f32[128,128]{1,0:T(8,128)S(1)}, u32[]{:S(2)}, u32[]{:S(2)}) collective-permute-start(f32[128,128]{1,0:T(8,128)S(1)} %lower.11.refs_0_), channel_id=1, source_target_pairs={{0,2},{1,3},{2,0},{3,1},{4,6},{5,7},{6,4},{7,5},{8,10},{9,11},{10,... | collective-permute-start | bytes 196616 | tf_op jit(solution)/shard_map/ppermute | solution.py:415
  172.2 7.7 %collective-permute-start.20 = (f32[128,128]{1,0:T(8,128)S(1)}, f32[128,128]{1,0:T(8,128)S(1)}, u32[]{:S(2)}, u32[]{:S(2)}) collective-permute-start(f32[128,128]{1,0:T(8,128)S(1)} %lower.11.refs_0_), channel_id=1, source_target_pairs={{0,6},{1,7},{2,4},{3,5},{4,2},{5,3},{6,0},{7,1},{8,14},{9,15},{10,... | collective-permute-start | bytes 196616 | tf_op jit(solution)/shard_map/ppermute | solution.py:415
  173.8 6.2 %collective-permute-start.21 = (f32[128,128]{1,0:T(8,128)S(1)}, f32[128,128]{1,0:T(8,128)S(1)}, u32[]{:S(2)}, u32[]{:S(2)}) collective-permute-start(f32[128,128]{1,0:T(8,128)S(1)} %lower.11.refs_0_), channel_id=1, source_target_pairs={{0,4},{1,5},{2,6},{3,7},{4,0},{5,1},{6,2},{7,3},{8,12},{9,13},{10,... | collective-permute-start | bytes 196616 | tf_op jit(solution)/shard_map/ppermute | solution.py:415
  202.1 8.8 %collective-permute-start.22 = (f32[128,128]{1,0:T(8,128)S(1)}, f32[128,128]{1,0:T(8,128)S(1)}, u32[]{:S(2)}, u32[]{:S(2)}) collective-permute-start(f32[128,128]{1,0:T(8,128)S(1)} %lower.12.refs_0_), channel_id=1, source_target_pairs={{0,2},{1,3},{2,0},{3,1},{4,6},{5,7},{6,4},{7,5},{8,10},{9,11},{10,... | collective-permute-start | bytes 196616 | tf_op jit(solution)/shard_map/ppermute | solution.py:415
  202.6 8.3 %collective-permute-start.23 = (f32[128,128]{1,0:T(8,128)S(1)}, f32[128,128]{1,0:T(8,128)S(1)}, u32[]{:S(2)}, u32[]{:S(2)}) collective-permute-start(f32[128,128]{1,0:T(8,128)S(1)} %lower.12.refs_0_), channel_id=1, source_target_pairs={{0,6},{1,7},{2,4},{3,5},{4,2},{5,3},{6,0},{7,1},{8,14},{9,15},{10,... | collective-permute-start | bytes 196616 | tf_op jit(solution)/shard_map/ppermute | solution.py:415
  204.1 6.8 %collective-permute-start.24 = (f32[128,128]{1,0:T(8,128)S(1)}, f32[128,128]{1,0:T(8,128)S(1)}, u32[]{:S(2)}, u32[]{:S(2)}) collective-permute-start(f32[128,128]{1,0:T(8,128)S(1)} %lower.12.refs_0_), channel_id=1, source_target_pairs={{0,4},{1,5},{2,6},{3,7},{4,0},{5,1},{6,2},{7,3},{8,12},{9,13},{10,... | collective-permute-start | bytes 196616 | tf_op jit(solution)/shard_map/ppermute | solution.py:415
  232.3 32.7 %collective-permute-start.25 = (f32[7,32,128]{2,1,0:T(8,128)S(1)}, f32[7,32,128]{2,1,0:T(8,128)S(1)}, u32[]{:S(2)}, u32[]{:S(2)}) collective-permute-start(f32[7,32,128]{2,1,0:T(8,128)S(1)} %join.1.early_ref), channel_id=1, source_target_pairs={{0,1},{1,0},{2,3},{3,2},{4,5},{5,4},{6,7},{7,6},{8,9},{9,8},{10,11... | collective-permute-start | bytes 344072 | tf_op jit(solution)/shard_map/ppermute | solution.py:409
  (8 other events, 26.5 us)

commit v8 on v7

--- a/solution.py
+++ b/solution.py
@@ -43,33 +43,58 @@
 ):
     cells = nu.shape[1]
     pad = field.shape[0] - cells
-    loads = [
-        pltpu.make_async_copy(stride_hbm, stride_ref, sems.at[2]),
-        pltpu.make_async_copy(counts_hbm, counts_ref, sems.at[3]),
-        pltpu.make_async_copy(source_hbm, source_ref, sems.at[4]),
-        pltpu.make_async_copy(field_hbm, field.at[pl.ds(pad, cells)], sems.at[0]),
-        pltpu.make_async_copy(nu_hbm, nu, sems.at[1]),
+    indices = [
+        pltpu.make_async_copy(stride_hbm, stride_ref, sems.at[0]),
+        pltpu.make_async_copy(counts_hbm, counts_ref, sems.at[1]),
+        pltpu.make_async_copy(source_hbm, source_ref, sems.at[2]),
     ]
-    for load in loads:
+    parts = 4
+    part = cells // parts
+    loads = []
+    for at in range(parts):
+        rows = pl.ds(at * part, part)
+        loads.append(
+            [
+                pltpu.make_async_copy(
+                    field_hbm.at[rows], field.at[pl.ds(pad + at * part, part)], sems.at[3 + 3 * at]
+                )
+            ]
+            + [
+                pltpu.make_async_copy(
+                    nu_hbm.at[side, rows], nu.at[side, rows], sems.at[4 + 3 * at + side]
+                )
+                for side in range(2)
+            ]
+        )
+    for load in indices + sum(loads, []):
         load.start()
     field[0:pad, :] = jnp.zeros((pad, field.shape[1]), F32)
     width = target_ref.shape[1]
     for sender in range(target_ref.shape[0]):
         targets_ref[0:1, sender * width : (sender + 1) * width] = target_ref[sender : sender + 1, :]
-    for load in loads:
+    for load in indices:
         load.wait()
     stride = stride_ref[0]
     slots = source_ref.shape[2]
+    chunk = 64
+    for at_part in range(parts):
+        for load in loads[at_part]:
+            load.wait()
+
+        @pl.loop(0, part // chunk)
+        def _(step):
+            at = pl.multiple_of(at_part * part + step * chunk, chunk)
+            here = field[pl.ds(pad + at, chunk), :]
+            radial = here - field[pl.ds(pad + at - stride, chunk), :]
+            tangent = here - field[pl.ds(pad - 1 + at, chunk), :]
+            rows = pl.ds(at, chunk)
+            nu[0, rows, :] = nu[0, rows, :] * radial + nu[1, rows, :] * tangent
 
     @pl.loop(0, source_ref.shape[1])
     def _(grid_row):
         live = counts_ref[0, grid_row]
         for slot in range(slots):
-            cell = source_ref[0, grid_row, slot]
-            here = field[pl.ds(pad + cell, 1), :]
-            radial = here - field[pl.ds(pad + cell - stride, 1), :]
-            tangent = here - field[pl.ds(pad - 1 + cell, 1), :]
-            swept = nu[0, pl.ds(cell, 1), :] * radial + nu[1, pl.ds(cell, 1), :] * tangent
+            swept = nu[0, pl.ds(source_ref[0, grid_row, slot], 1), :]
             out_ref[grid_row, pl.ds(slot, 1), :] = jnp.where(slot < live, swept, 0.0)
 
 
@@ -91,7 +116,7 @@
             pltpu.SMEM(source_cell.shape, jnp.int32),
             pltpu.VMEM((pad + cells, rotor), F32),
             pltpu.VMEM((2, cells, rotor), F32),
-            pltpu.SemaphoreType.DMA((5,)),
+            pltpu.SemaphoreType.DMA((15,)),
         ],
         compiler_params=kernel_params(PICK_LIMIT),
         name="pick",
@@ -121,21 +146,20 @@
     return jnp.concatenate([high, low], axis=1), rest
 
 
-def interface_rows(block, rows, targets, parts):
-    pair, rest = parts
-    width = rest.shape[1]
-    row = block * rows + lax.broadcasted_iota(jnp.int32, (rows, rest.shape[0]), 0)
-    chosen = jnp.where(row == targets, 1.0, 0.0).astype(BF16)
-    both = dot(chosen, pair)
-    return both[:, :width] + both[:, width:] + dot(chosen, rest)
+def both_sides(pair):
+    return pair.reshape(pair.shape[0] * pair.shape[1], pair.shape[2])
 
 
 def fill_interface(block, targets_ref, slots, totals):
     pair, rest = three_parts(slots)
-
-    @pl.loop(0, 2)
-    def _(side):
-        totals[side] = interface_rows(block, totals.shape[1], targets_ref[side], (pair, rest))
+    _, rows, width = totals.shape
+    row = block * rows + lax.broadcasted_iota(jnp.int32, (rows, slots.shape[0]), 0)
+    chosen = jnp.concatenate(
+        [jnp.where(row == targets_ref[side], 1.0, 0.0) for side in range(2)], axis=0
+    ).astype(BF16)
+    both = dot(chosen, pair)
+    total = both[:, :width] + both[:, width:] + dot(chosen, rest)
+    totals[...] = total.reshape(totals.shape)
 
 
 def first_kernel(
@@ -221,12 +245,12 @@
         pltpu.make_async_copy(shares[j], held.at[j], share_sems.at[j]).wait()
     if earlier:
 
-        @pl.loop(0, 2 * earlier)
-        def _(at_tile):
-            loaded(at_tile).wait()
-            high, low = split(tiles[at_tile])
-            side = lax.rem(at_tile, 2)
-            totals[side] = totals[side] - split_product(high, low, held[lax.div(at_tile, 2)])
+        @pl.loop(0, earlier)
+        def _(j):
+            loaded(2 * j).wait()
+            loaded(2 * j + 1).wait()
+            high, low = split(both_sides(tiles[pl.ds(2 * j, 2)]))
+            totals[...] = totals[...] - split_product(high, low, held[j]).reshape(totals.shape)
 
     started_ref[...] = packed(totals[0], totals[1])
     split_sides(loaded, tiles, 2 * earlier, lower_high, lower_low)
@@ -298,10 +322,9 @@
 
 
 def lower_kernel(share_ref, high_ref, low_ref, started_ref, out_ref):
-    share = share_ref[...]
-    out_ref[...] = started_ref[...] - packed(
-        split_product(high_ref[0], low_ref[0], share), split_product(high_ref[1], low_ref[1], share)
-    )
+    value = split_product(both_sides(high_ref[...]), both_sides(low_ref[...]), share_ref[...])
+    rows = high_ref.shape[1]
+    out_ref[...] = started_ref[...] - packed(value[:rows], value[rows:])
 
 
 def lower_product(share, tiles, started):

time: 283 us -> 281 us (level)
  Pallas kernels: 41.7 us -> 38.1 us
  transfers between devices with their start and end apart: 31 -> 31, of which waited for: 9 -> 8; matrix products, arithmetic and copies ran while one was open for 0% -> 0% of each run, Pallas kernels for 12% -> 11%
where the time goes in v8:
time: 281 us; the launch traced here: 280 us
  blocking collectives  160 us (57%)
  starting transfers between devices  66.1 us (24%)
  Pallas kernels  38.1 us (14%)
  waiting for transfers between devices  14.5 us (5%)
    all_to_all x15, blocking collectives, per_row(): return lax.all_to_all(value, 'row', 0, 0, tiled=True)  160 us
    ppermute x6, starting transfers between devices, other_core(): return lax.ppermute(value, 'col', [(i, i ^ 1) for i in range(peers)])  35.6 us
    ppermute x24, starting transfers between devices, along_x(): lax.ppermute(value, 'col', [(i, i ^ apart) for i in range(peers)])  26.9 us
    pallas_call x7, Pallas kernels, fold(): pl.pallas_call(functools.partial(fold_kernel, block, bool(diags)), out_sh...  21.4 us
    all_to_all x1, waiting for transfers between devices, per_row(): return lax.all_to_all(value, 'row', 0, 0, tiled=True)  6.17 us
    ppermute x24, waiting for transfers between devices, along_x(): lax.ppermute(value, 'col', [(i, i ^ apart) for i in range(peers)])  6.16 us
  transfers between devices with their start and end apart: 31, of which 8 were waited for; matrix products, arithmetic and copies ran while one was open for 0% of the time, Pallas kernels for 11%

profile of v8, /device:TPU:1, one launch (start us, length us, event | category | flops | bytes accessed | tf_op | source)
XLA Modules:
  0.0 280.1 jit_solution(13672046715628313724)
XLA Ops:
  2.1 4.4 %pick.1 = (f32[16,32,128]{2,1,0:T(8,128)}, s32[1,512]{1,0:T(1,128)}) custom-call(s32[1]{0:T(128)} %bitcast.core_ref, s32[1]{0:T(128)S(6)} %copy.10.stride_hbm, s32[1,16]{1,0:T(1,128)} %counts_hbm.1, s32[1,16,32]{2,1,0:T(8,128)} %source_hbm.1, s32[16,32]{1,0:T(8,128)} %bitcast.59, f32[2048,128]{1,0:T(8,128)} %field_hbm.1, f32[2,2048,128]{2,1,0:T(8,128)} %nu_hbm.1), custom_call_target="tpu_custom_call" | custom-call | tf_op jit(solution)/shard_map/pick/pallas_call | solution.py:105
  6.5 16.4 %all_to_all.80 = f32[16,32,128]{2,1,0:T(8,128)S(1)} all-to-all(f32[16,32,128]{2,1,0:T(8,128)} %get-tuple-element.77), channel_id=1, replica_groups=mesh['row'=16,'col'=8] {'row'}, dimensions={0} | all-to-all | bytes 524288 | tf_op jit(solution)/shard_map/all_to_all | solution.py:444
  35.0 10.2 %all_to_all.81.parts_ref = f32[16,32,128]{2,1,0:T(8,128)S(1)} all-to-all(f32[16,32,128]{2,1,0:T(8,128)S(1)} %bitcast.50), channel_id=1, replica_groups=mesh['row'=16,'col'=8] {'row'}, dimensions={0} | all-to-all | bytes 524288 | tf_op jit(solution)/shard_map/all_to_all | solution.py:444
  46.0 3.5 %all-to-all-start.2 = ((f32[16,32,128]{2,1,0:T(8,128)}), f32[16,32,128]{2,1,0:T(8,128)S(1)}, u32[]{:S(2)}, u32[]{:S(2)}) async-start(f32[16,32,128]{2,1,0:T(8,128)} %get-tuple-element.86), calls=%async_computation.2 | async-start | bytes 524288 | tf_op jit(solution)/shard_map/all_to_all | solution.py:444
  50.8 6.2 %all-to-all-done.2 = f32[16,32,128]{2,1,0:T(8,128)S(1)} async-done(((f32[16,32,128]{2,1,0:T(8,128)}), f32[16,32,128]{2,1,0:T(8,128)S(1)}, u32[]{:S(2)}, u32[]{:S(2)}) %all-to-all-start.2) | async-done | bytes 262176 | tf_op jit(solution)/shard_map/all_to_all | solution.py:444
  63.8 10.1 %all_to_all.82.parts_ref = f32[16,32,128]{2,1,0:T(8,128)S(1)} all-to-all(f32[16,32,128]{2,1,0:T(8,128)S(1)} %bitcast.51), channel_id=1, replica_groups=mesh['row'=16,'col'=8] {'row'}, dimensions={0} | all-to-all | bytes 524288 | tf_op jit(solution)/shard_map/all_to_all | solution.py:444
  74.0 10.2 %all_to_all.83 = f32[16,32,128]{2,1,0:T(8,128)S(1)} all-to-all(f32[16,32,128]{2,1,0:T(8,128)S(1)} %get-tuple-element.96), channel_id=1, replica_groups=mesh['row'=16,'col'=8] {'row'}, dimensions={0} | all-to-all | bytes 524288 | tf_op jit(solution)/shard_map/all_to_all | solution.py:444
  92.6 10.1 %all_to_all.84.parts_ref = f32[16,32,128]{2,1,0:T(8,128)S(1)} all-to-all(f32[16,32,128]{2,1,0:T(8,128)S(1)} %bitcast.52), channel_id=1, replica_groups=mesh['row'=16,'col'=8] {'row'}, dimensions={0} | all-to-all | bytes 524288 | tf_op jit(solution)/shard_map/all_to_all | solution.py:444
  102.8 10.7 %all_to_all.85 = f32[16,32,128]{2,1,0:T(8,128)S(1)} all-to-all(f32[16,32,128]{2,1,0:T(8,128)S(1)} %get-tuple-element.102), channel_id=1, replica_groups=mesh['row'=16,'col'=8] {'row'}, dimensions={0} | all-to-all | bytes 524288 | tf_op jit(solution)/shard_map/all_to_all | solution.py:444
  117.3 3.1 %fold.10 = (f32[128,128]{1,0:T(8,128)S(1)}, bf16[2,256,512]{2,1,0:T(8,128)(2,1)S(1)}, bf16[2,256,512]{2,1,0:T(8,128)(2,1)S(1)}, bf16[2,512,256]{2,1,0:T(8,128)(2,1)S(1)}, bf16[2,512,256]{2,1,0:T(8,128)(2,1)S(1)}) custom-call(s32[2,1,512]{2,1,0:T(1,128)S(1)} %get-tuple-element.87.refs_0_, f32[512,128]{1,0:T(8,128)S(1)} %get-tuple-element.89.refs_1_, ...), custom_call_target="tpu_custom_call" | custom-call | flops 805306368 | bytes 5242880 | tf_op jit(solution)/shard_map/fold/pallas_call | solution.py:277
  120.9 10.1 %all_to_all.86.parts_ref = f32[16,32,128]{2,1,0:T(8,128)S(1)} all-to-all(f32[16,32,128]{2,1,0:T(8,128)S(1)} %bitcast.53), channel_id=1, replica_groups=mesh['row'=16,'col'=8] {'row'}, dimensions={0} | all-to-all | bytes 524288 | tf_op jit(solution)/shard_map/all_to_all | solution.py:444
  131.1 10.2 %all_to_all.87 = f32[16,32,128]{2,1,0:T(8,128)S(1)} all-to-all(f32[16,32,128]{2,1,0:T(8,128)S(1)} %get-tuple-element.108), channel_id=1, replica_groups=mesh['row'=16,'col'=8] {'row'}, dimensions={0} | all-to-all | bytes 524288 | tf_op jit(solution)/shard_map/all_to_all | solution.py:444
  145.1 3.6 %fold.11 = (f32[128,128]{1,0:T(8,128)S(1)}, bf16[2,256,512]{2,1,0:T(8,128)(2,1)S(1)}, bf16[2,256,512]{2,1,0:T(8,128)(2,1)S(1)}, bf16[2,512,256]{2,1,0:T(8,128)(2,1)S(1)}, bf16[2,512,256]{2,1,0:T(8,128)(2,1)S(1)}) custom-call(s32[2,1,512]{2,1,0:T(1,128)S(1)} %get-tuple-element.87.refs_0_, f32[512,128]{1,0:T(8,128)S(1)} %get-tuple-element.89.refs_1_, ...), custom_call_target="tpu_custom_call" | custom-call | flops 1006632960 | bytes 6291456 | tf_op jit(solution)/shard_map/fold/pallas_call | solution.py:277
  149.3 10.2 %all_to_all.88.parts_ref = f32[16,32,128]{2,1,0:T(8,128)S(1)} all-to-all(f32[16,32,128]{2,1,0:T(8,128)S(1)} %bitcast.54), channel_id=1, replica_groups=mesh['row'=16,'col'=8] {'row'}, dimensions={0} | all-to-all | bytes 524288 | tf_op jit(solution)/shard_map/all_to_all | solution.py:444
  159.5 10.2 %all_to_all.89 = f32[16,32,128]{2,1,0:T(8,128)S(1)} all-to-all(f32[16,32,128]{2,1,0:T(8,128)S(1)} %get-tuple-element.114), channel_id=1, replica_groups=mesh['row'=16,'col'=8] {'row'}, dimensions={0} | all-to-all | bytes 524288 | tf_op jit(solution)/shard_map/all_to_all | solution.py:444
  173.5 4.1 %fold.12 = (f32[128,128]{1,0:T(8,128)S(1)}, bf16[2,256,512]{2,1,0:T(8,128)(2,1)S(1)}, bf16[2,256,512]{2,1,0:T(8,128)(2,1)S(1)}, bf16[2,512,256]{2,1,0:T(8,128)(2,1)S(1)}, bf16[2,512,256]{2,1,0:T(8,128)(2,1)S(1)}) custom-call(s32[2,1,512]{2,1,0:T(1,128)S(1)} %get-tuple-element.87.refs_0_, f32[512,128]{1,0:T(8,128)S(1)} %get-tuple-element.89.refs_1_, ...), custom_call_target="tpu_custom_call" | custom-call | flops 1207959552 | bytes 7340032 | tf_op jit(solution)/shard_map/fold/pallas_call | solution.py:277
  178.1 10.2 %all_to_all.90.parts_ref = f32[16,32,128]{2,1,0:T(8,128)S(1)} all-to-all(f32[16,32,128]{2,1,0:T(8,128)S(1)} %bitcast.55), channel_id=1, replica_groups=mesh['row'=16,'col'=8] {'row'}, dimensions={0} | all-to-all | bytes 524288 | tf_op jit(solution)/shard_map/all_to_all | solution.py:444
  188.3 10.4 %all_to_all.91 = f32[16,32,128]{2,1,0:T(8,128)S(1)} all-to-all(f32[16,32,128]{2,1,0:T(8,128)S(1)} %get-tuple-element.120), channel_id=1, replica_groups=mesh['row'=16,'col'=8] {'row'}, dimensions={0} | all-to-all | bytes 524288 | tf_op jit(solution)/shard_map/all_to_all | solution.py:444
  202.6 4.6 %fold.13 = (f32[128,128]{1,0:T(8,128)S(1)}, bf16[2,256,512]{2,1,0:T(8,128)(2,1)S(1)}, bf16[2,256,512]{2,1,0:T(8,128)(2,1)S(1)}, bf16[2,512,256]{2,1,0:T(8,128)(2,1)S(1)}, bf16[2,512,256]{2,1,0:T(8,128)(2,1)S(1)}) custom-call(s32[2,1,512]{2,1,0:T(1,128)S(1)} %get-tuple-element.87.refs_0_, f32[512,128]{1,0:T(8,128)S(1)} %get-tuple-element.89.refs_1_, ...), custom_call_target="tpu_custom_call" | custom-call | flops 1409286144 | bytes 8388608 | tf_op jit(solution)/shard_map/fold/pallas_call | solution.py:277
  207.7 10.2 %all_to_all.92.parts_ref = f32[16,32,128]{2,1,0:T(8,128)S(1)} all-to-all(f32[16,32,128]{2,1,0:T(8,128)S(1)} %bitcast.56), channel_id=1, replica_groups=mesh['row'=16,'col'=8] {'row'}, dimensions={0} | all-to-all | bytes 524288 | tf_op jit(solution)/shard_map/all_to_all | solution.py:444
  217.9 10.4 %all_to_all.93 = f32[16,32,128]{2,1,0:T(8,128)S(1)} all-to-all(f32[16,32,128]{2,1,0:T(8,128)S(1)} %get-tuple-element.126), channel_id=1, replica_groups=mesh['row'=16,'col'=8] {'row'}, dimensions={0} | all-to-all | bytes 524288 | tf_op jit(solution)/shard_map/all_to_all | solution.py:444
  228.8 29.5 %collective-permute-start.25 = (f32[7,32,128]{2,1,0:T(8,128)S(1)}, f32[7,32,128]{2,1,0:T(8,128)S(1)}, u32[]{:S(2)}, u32[]{:S(2)}) collective-permute-start(f32[7,32,128]{2,1,0:T(8,128)S(1)} %join.1.early_ref), channel_id=1, source_target_pairs={{0,1},{1,0},{2,3},{3,2},{4,5},{5,4},{6,7},{7,6},{8,9},{9,8},{10,11... | collective-permute-start | bytes 344072 | tf_op jit(solution)/shard_map/ppermute | solution.py:432
  265.1 10.2 %all_to_all.94 = f32[16,32,128]{2,1,0:T(8,128)S(1)} all-to-all(f32[16,32,128]{2,1,0:T(8,128)S(1)} %bitcast.57), channel_id=1, replica_groups=mesh['row'=16,'col'=8] {'row'}, dimensions={0} | all-to-all | bytes 524288 | tf_op jit(solution)/shard_map/all_to_all | solution.py:444
  275.2 3.3 %collective-permute-start.29 = (f32[32,128]{1,0:T(8,128)S(1)}, f32[32,128]{1,0:T(8,128)S(1)}, u32[]{:S(2)}, u32[]{:S(2)}) collective-permute-start(f32[32,128]{1,0:T(8,128)S(1)} %reduce_sum.9.last_ref), channel_id=1, source_target_pairs={{0,1},{1,0},{2,3},{3,2},{4,5},{5,4},{6,7},{7,6},{8,9},{9,8},{10,11... | collective-permute-start | bytes 49160 | tf_op jit(solution)/shard_map/ppermute | solution.py:432
  (91 shorter events, 57.2 us)
Async XLA Ops:
  0.0 22.9 %collective-permute-start = (f32[8,512,256]{2,1,0:T(8,128)}, f32[8,512,256]{2,1,0:T(8,128)}, u32[]{:S(2)}, u32[]{:S(2)}) collective-permute-start(f32[8,512,256]{2,1,0:T(8,128)} %refs_4_.11), channel_id=1, source_target_pairs={{0,1},{1,0},{2,3},{3,2},{4,5},{5,4},{6,7},{7,6},{8,9},{9,8},{10,11... | collective-permute-start | bytes 12582920 | tf_op jit(solution)/shard_map/ppermute | solution.py:432
  26.6 22.9 %collective-permute-start.6 = (f32[28,256,512]{2,1,0:T(8,128)}, f32[28,256,512]{2,1,0:T(8,128)}, u32[]{:S(2)}, u32[]{:S(2)}) collective-permute-start(f32[28,256,512]{2,1,0:T(8,128)} %refs_2_.13), channel_id=1, source_target_pairs={{0,1},{1,0},{2,3},{3,2},{4,5},{5,4},{6,7},{7,6},{8,9},{9,8},{10,11... | collective-permute-start | bytes 44040200 | tf_op jit(solution)/shard_map/ppermute | solution.py:432
  26.9 5.0 %collective-permute-start.3 = (f32[128,128]{1,0:T(8,128)S(1)}, f32[128,128]{1,0:T(8,128)S(1)}, u32[]{:S(2)}, u32[]{:S(2)}) collective-permute-start(f32[128,128]{1,0:T(8,128)S(1)} %get-tuple-element.83.refs_0_), channel_id=1, source_target_pairs={{0,2},{1,3},{2,0},{3,1},{4,6},{5,7},{6,4},{7,5},{8,10},{9,11},{10,... | collective-permute-start | bytes 196616 | tf_op jit(solution)/shard_map/ppermute | solution.py:438
  46.0 11.0 %all-to-all-start.2 = ((f32[16,32,128]{2,1,0:T(8,128)}), f32[16,32,128]{2,1,0:T(8,128)S(1)}, u32[]{:S(2)}, u32[]{:S(2)}) async-start(f32[16,32,128]{2,1,0:T(8,128)} %get-tuple-element.86), calls=%async_computation.2 | async-start | bytes 524288 | tf_op jit(solution)/shard_map/all_to_all | solution.py:444
  57.5 5.5 %collective-permute-start.7 = (f32[128,128]{1,0:T(8,128)S(1)}, f32[128,128]{1,0:T(8,128)S(1)}, u32[]{:S(2)}, u32[]{:S(2)}) collective-permute-start(f32[128,128]{1,0:T(8,128)S(1)} %lower.7.refs_0_), channel_id=1, source_target_pairs={{0,2},{1,3},{2,0},{3,1},{4,6},{5,7},{6,4},{7,5},{8,10},{9,11},{10,... | collective-permute-start | bytes 196616 | tf_op jit(solution)/shard_map/ppermute | solution.py:438
  57.9 5.1 %collective-permute-start.8 = (f32[128,128]{1,0:T(8,128)S(1)}, f32[128,128]{1,0:T(8,128)S(1)}, u32[]{:S(2)}, u32[]{:S(2)}) collective-permute-start(f32[128,128]{1,0:T(8,128)S(1)} %lower.7.refs_0_), channel_id=1, source_target_pairs={{0,6},{1,7},{2,4},{3,5},{4,2},{5,3},{6,0},{7,1},{8,14},{9,15},{10,... | collective-permute-start | bytes 196616 | tf_op jit(solution)/shard_map/ppermute | solution.py:438
  58.7 4.6 %collective-permute-start.9 = (f32[128,128]{1,0:T(8,128)S(1)}, f32[128,128]{1,0:T(8,128)S(1)}, u32[]{:S(2)}, u32[]{:S(2)}) collective-permute-start(f32[128,128]{1,0:T(8,128)S(1)} %lower.7.refs_0_), channel_id=1, source_target_pairs={{0,4},{1,5},{2,6},{3,7},{4,0},{5,1},{6,2},{7,3},{8,12},{9,13},{10,... | collective-permute-start | bytes 196616 | tf_op jit(solution)/shard_map/ppermute | solution.py:438
  84.6 6.0 %collective-permute-start.10 = (f32[128,128]{1,0:T(8,128)S(1)}, f32[128,128]{1,0:T(8,128)S(1)}, u32[]{:S(2)}, u32[]{:S(2)}) collective-permute-start(f32[128,128]{1,0:T(8,128)S(1)} %lower.8.refs_0_), channel_id=1, source_target_pairs={{0,2},{1,3},{2,0},{3,1},{4,6},{5,7},{6,4},{7,5},{8,10},{9,11},{10,... | collective-permute-start | bytes 196616 | tf_op jit(solution)/shard_map/ppermute | solution.py:438
  85.5 5.2 %collective-permute-start.11 = (f32[128,128]{1,0:T(8,128)S(1)}, f32[128,128]{1,0:T(8,128)S(1)}, u32[]{:S(2)}, u32[]{:S(2)}) collective-permute-start(f32[128,128]{1,0:T(8,128)S(1)} %lower.8.refs_0_), channel_id=1, source_target_pairs={{0,6},{1,7},{2,4},{3,5},{4,2},{5,3},{6,0},{7,1},{8,14},{9,15},{10,... | collective-permute-start | bytes 196616 | tf_op jit(solution)/shard_map/ppermute | solution.py:438
  87.2 4.9 %collective-permute-start.12 = (f32[128,128]{1,0:T(8,128)S(1)}, f32[128,128]{1,0:T(8,128)S(1)}, u32[]{:S(2)}, u32[]{:S(2)}) collective-permute-start(f32[128,128]{1,0:T(8,128)S(1)} %lower.8.refs_0_), channel_id=1, source_target_pairs={{0,4},{1,5},{2,6},{3,7},{4,0},{5,1},{6,2},{7,3},{8,12},{9,13},{10,... | collective-permute-start | bytes 196616 | tf_op jit(solution)/shard_map/ppermute | solution.py:438
  113.9 6.5 %collective-permute-start.13 = (f32[128,128]{1,0:T(8,128)S(1)}, f32[128,128]{1,0:T(8,128)S(1)}, u32[]{:S(2)}, u32[]{:S(2)}) collective-permute-start(f32[128,128]{1,0:T(8,128)S(1)} %lower.9.refs_0_), channel_id=1, source_target_pairs={{0,2},{1,3},{2,0},{3,1},{4,6},{5,7},{6,4},{7,5},{8,10},{9,11},{10,... | collective-permute-start | bytes 196616 | tf_op jit(solution)/shard_map/ppermute | solution.py:438
  114.4 6.0 %collective-permute-start.14 = (f32[128,128]{1,0:T(8,128)S(1)}, f32[128,128]{1,0:T(8,128)S(1)}, u32[]{:S(2)}, u32[]{:S(2)}) collective-permute-start(f32[128,128]{1,0:T(8,128)S(1)} %lower.9.refs_0_), channel_id=1, source_target_pairs={{0,6},{1,7},{2,4},{3,5},{4,2},{5,3},{6,0},{7,1},{8,14},{9,15},{10,... | collective-permute-start | bytes 196616 | tf_op jit(solution)/shard_map/ppermute | solution.py:438
  115.6 4.8 %collective-permute-start.15 = (f32[128,128]{1,0:T(8,128)S(1)}, f32[128,128]{1,0:T(8,128)S(1)}, u32[]{:S(2)}, u32[]{:S(2)}) collective-permute-start(f32[128,128]{1,0:T(8,128)S(1)} %lower.9.refs_0_), channel_id=1, source_target_pairs={{0,4},{1,5},{2,6},{3,7},{4,0},{5,1},{6,2},{7,3},{8,12},{9,13},{10,... | collective-permute-start | bytes 196616 | tf_op jit(solution)/shard_map/ppermute | solution.py:438
  141.8 6.9 %collective-permute-start.16 = (f32[128,128]{1,0:T(8,128)S(1)}, f32[128,128]{1,0:T(8,128)S(1)}, u32[]{:S(2)}, u32[]{:S(2)}) collective-permute-start(f32[128,128]{1,0:T(8,128)S(1)} %lower.10.refs_0_), channel_id=1, source_target_pairs={{0,2},{1,3},{2,0},{3,1},{4,6},{5,7},{6,4},{7,5},{8,10},{9,11},{10,... | collective-permute-start | bytes 196616 | tf_op jit(solution)/shard_map/ppermute | solution.py:438
  142.2 6.5 %collective-permute-start.17 = (f32[128,128]{1,0:T(8,128)S(1)}, f32[128,128]{1,0:T(8,128)S(1)}, u32[]{:S(2)}, u32[]{:S(2)}) collective-permute-start(f32[128,128]{1,0:T(8,128)S(1)} %lower.10.refs_0_), channel_id=1, source_target_pairs={{0,6},{1,7},{2,4},{3,5},{4,2},{5,3},{6,0},{7,1},{8,14},{9,15},{10,... | collective-permute-start | bytes 196616 | tf_op jit(solution)/shard_map/ppermute | solution.py:438
  143.6 5.1 %collective-permute-start.18 = (f32[128,128]{1,0:T(8,128)S(1)}, f32[128,128]{1,0:T(8,128)S(1)}, u32[]{:S(2)}, u32[]{:S(2)}) collective-permute-start(f32[128,128]{1,0:T(8,128)S(1)} %lower.10.refs_0_), channel_id=1, source_target_pairs={{0,4},{1,5},{2,6},{3,7},{4,0},{5,1},{6,2},{7,3},{8,12},{9,13},{10,... | collective-permute-start | bytes 196616 | tf_op jit(solution)/shard_map/ppermute | solution.py:438
  170.1 7.4 %collective-permute-start.19 = (f32[128,128]{1,0:T(8,128)S(1)}, f32[128,128]{1,0:T(8,128)S(1)}, u32[]{:S(2)}, u32[]{:S(2)}) collective-permute-start(f32[128,128]{1,0:T(8,128)S(1)} %lower.11.refs_0_), channel_id=1, source_target_pairs={{0,2},{1,3},{2,0},{3,1},{4,6},{5,7},{6,4},{7,5},{8,10},{9,11},{10,... | collective-permute-start | bytes 196616 | tf_op jit(solution)/shard_map/ppermute | solution.py:438
  170.6 6.9 %collective-permute-start.20 = (f32[128,128]{1,0:T(8,128)S(1)}, f32[128,128]{1,0:T(8,128)S(1)}, u32[]{:S(2)}, u32[]{:S(2)}) collective-permute-start(f32[128,128]{1,0:T(8,128)S(1)} %lower.11.refs_0_), channel_id=1, source_target_pairs={{0,6},{1,7},{2,4},{3,5},{4,2},{5,3},{6,0},{7,1},{8,14},{9,15},{10,... | collective-permute-start | bytes 196616 | tf_op jit(solution)/shard_map/ppermute | solution.py:438
  172.3 5.2 %collective-permute-start.21 = (f32[128,128]{1,0:T(8,128)S(1)}, f32[128,128]{1,0:T(8,128)S(1)}, u32[]{:S(2)}, u32[]{:S(2)}) collective-permute-start(f32[128,128]{1,0:T(8,128)S(1)} %lower.11.refs_0_), channel_id=1, source_target_pairs={{0,4},{1,5},{2,6},{3,7},{4,0},{5,1},{6,2},{7,3},{8,12},{9,13},{10,... | collective-permute-start | bytes 196616 | tf_op jit(solution)/shard_map/ppermute | solution.py:438
  199.2 7.9 %collective-permute-start.22 = (f32[128,128]{1,0:T(8,128)S(1)}, f32[128,128]{1,0:T(8,128)S(1)}, u32[]{:S(2)}, u32[]{:S(2)}) collective-permute-start(f32[128,128]{1,0:T(8,128)S(1)} %lower.12.refs_0_), channel_id=1, source_target_pairs={{0,2},{1,3},{2,0},{3,1},{4,6},{5,7},{6,4},{7,5},{8,10},{9,11},{10,... | collective-permute-start | bytes 196616 | tf_op jit(solution)/shard_map/ppermute | solution.py:438
  199.7 7.4 %collective-permute-start.23 = (f32[128,128]{1,0:T(8,128)S(1)}, f32[128,128]{1,0:T(8,128)S(1)}, u32[]{:S(2)}, u32[]{:S(2)}) collective-permute-start(f32[128,128]{1,0:T(8,128)S(1)} %lower.12.refs_0_), channel_id=1, source_target_pairs={{0,6},{1,7},{2,4},{3,5},{4,2},{5,3},{6,0},{7,1},{8,14},{9,15},{10,... | collective-permute-start | bytes 196616 | tf_op jit(solution)/shard_map/ppermute | solution.py:438
  201.4 5.7 %collective-permute-start.24 = (f32[128,128]{1,0:T(8,128)S(1)}, f32[128,128]{1,0:T(8,128)S(1)}, u32[]{:S(2)}, u32[]{:S(2)}) collective-permute-start(f32[128,128]{1,0:T(8,128)S(1)} %lower.12.refs_0_), channel_id=1, source_target_pairs={{0,4},{1,5},{2,6},{3,7},{4,0},{5,1},{6,2},{7,3},{8,12},{9,13},{10,... | collective-permute-start | bytes 196616 | tf_op jit(solution)/shard_map/ppermute | solution.py:438
  228.8 34.1 %collective-permute-start.25 = (f32[7,32,128]{2,1,0:T(8,128)S(1)}, f32[7,32,128]{2,1,0:T(8,128)S(1)}, u32[]{:S(2)}, u32[]{:S(2)}) collective-permute-start(f32[7,32,128]{2,1,0:T(8,128)S(1)} %join.1.early_ref), channel_id=1, source_target_pairs={{0,1},{1,0},{2,3},{3,2},{4,5},{5,4},{6,7},{7,6},{8,9},{9,8},{10,11... | collective-permute-start | bytes 344072 | tf_op jit(solution)/shard_map/ppermute | solution.py:432
  259.9 4.6 %collective-permute-start.28 = (f32[128,128]{1,0:T(8,128)S(1)}, f32[128,128]{1,0:T(8,128)S(1)}, u32[]{:S(2)}, u32[]{:S(2)}) collective-permute-start(f32[128,128]{1,0:T(8,128)S(1)} %lower.13.refs_0_), channel_id=1, source_target_pairs={{0,4},{1,5},{2,6},{3,7},{4,0},{5,1},{6,2},{7,3},{8,12},{9,13},{10,... | collective-permute-start | bytes 196616 | tf_op jit(solution)/shard_map/ppermute | solution.py:438
  (8 other events, 26.5 us)

commit v9 on v8

--- a/solution.py
+++ b/solution.py
@@ -201,8 +201,9 @@
         high_ref[side], low_ref[side] = split(tiles[first + side])
 
 
-def fold_kernel(block, with_diag, *refs):
+def fold_kernel(block, with_diag, skip, ahead, *refs):
     earlier = block - 1
+    later, count = ahead
     refs = list(refs)
     targets_ref, slots_ref = refs[:2]
     lowers = refs[2:4]
@@ -210,18 +211,24 @@
     at = 4 + len(diags)
     shares = refs[at : at + earlier]
     at += earlier
+    carried = refs[at : at + 1] if skip else []
+    at += len(carried)
     started_ref, lower_high, lower_low = refs[at : at + 3]
     at += 3
     diag_outs = refs[at : at + 2] if with_diag else []
     at += len(diag_outs)
+    ahead_outs = refs[at : at + 1] if count else []
+    at += len(ahead_outs)
     totals, tiles, held, sems, share_sems = refs[at : at + 5]
     base = block * (block - 1) // 2
 
-    for j in range(block):
+    wanted = [base + j for j in range(skip, block)]
+    wanted += [later * (later - 1) // 2 + j for j in range(count)]
+    for index, pair in enumerate(wanted):
         for side in range(2):
-            at_tile = 2 * j + side
+            at_tile = 2 * index + side
             pltpu.make_async_copy(
-                lowers[side].at[base + j], tiles.at[at_tile], sems.at[at_tile]
+                lowers[side].at[pair], tiles.at[at_tile], sems.at[at_tile]
             ).start()
     for j in range(earlier):
         pltpu.make_async_copy(shares[j], held.at[j], share_sems.at[j]).start()
@@ -243,51 +250,69 @@
     fill_interface(block, targets_ref, slots_ref[...], totals)
     for j in range(earlier):
         pltpu.make_async_copy(shares[j], held.at[j], share_sems.at[j]).wait()
-    if earlier:
-
-        @pl.loop(0, earlier)
+    if skip:
+        totals[...] = totals[...] + carried[0][...]
+
+    def subtract(total_ref, at_tile, share):
+        loaded(at_tile).wait()
+        loaded(at_tile + 1).wait()
+        high, low = split(both_sides(tiles[pl.ds(at_tile, 2)]))
+        total_ref[...] = total_ref[...] - split_product(high, low, held[share]).reshape(
+            total_ref.shape
+        )
+
+    if earlier > skip:
+
+        @pl.loop(skip, earlier)
         def _(j):
-            loaded(2 * j).wait()
-            loaded(2 * j + 1).wait()
-            high, low = split(both_sides(tiles[pl.ds(2 * j, 2)]))
-            totals[...] = totals[...] - split_product(high, low, held[j]).reshape(totals.shape)
+            subtract(totals, 2 * (j - skip), j)
 
     started_ref[...] = packed(totals[0], totals[1])
-    split_sides(loaded, tiles, 2 * earlier, lower_high, lower_low)
+    split_sides(loaded, tiles, 2 * (earlier - skip), lower_high, lower_low)
+    if count:
+        ahead_outs[0][...] = jnp.zeros(totals.shape, F32)
+
+        @pl.loop(0, count)
+        def _(j):
+            subtract(ahead_outs[0], 2 * (block - skip + j), j)
+
     if with_diag:
         split_sides(diag_loaded, diag_tiles, 0, *diag_outs)
 
 
-def fold(block, targets, slots, lowers, diags, shares):
+def fold(block, targets, slots, lowers, diags, shares, carried=(), skip=0, ahead=(0, 0)):
+    n_pairs = block - skip + ahead[1]
     _, rows, columns = lowers[0].shape
     rotor = slots.shape[1]
     shapes = [jax.ShapeDtypeStruct((rows // 2, rotor), F32)]
     shapes += [jax.ShapeDtypeStruct((2, rows, columns), BF16)] * 2
     scratch = [
         pltpu.VMEM((2, rows, rotor), F32),
-        pltpu.VMEM((2 * block, rows, columns), F32),
+        pltpu.VMEM((2 * n_pairs, rows, columns), F32),
         pltpu.VMEM((max(block - 1, 1), columns, rotor), F32),
-        pltpu.SemaphoreType.DMA((2 * block,)),
+        pltpu.SemaphoreType.DMA((2 * n_pairs,)),
         pltpu.SemaphoreType.DMA((block,)),
     ]
     if diags:
         _, out_rows, depth = diags[0].shape
         shapes += [jax.ShapeDtypeStruct((2, out_rows, depth), BF16)] * 2
         scratch += [pltpu.VMEM((2, out_rows, depth), F32), pltpu.SemaphoreType.DMA((2,))]
-    return pl.pallas_call(
-        functools.partial(fold_kernel, block, bool(diags)),
+    if ahead[1]:
+        shapes += [jax.ShapeDtypeStruct((2, rows, rotor), F32)]
+    return pl.pallas_call(
+        functools.partial(fold_kernel, block, bool(diags), skip, ahead),
         out_shape=shapes,
-        in_specs=[VMEM] * 2 + [HBM] * (2 + len(diags)) + [VMEM] * len(shares),
+        in_specs=[VMEM] * 2 + [HBM] * (2 + len(diags)) + [VMEM] * (len(shares) + len(carried)),
         out_specs=[VMEM] * len(shapes),
         scratch_shapes=scratch,
         compiler_params=kernel_params(WIDE_LIMIT),
         cost_estimate=pl.CostEstimate(
-            flops=12 * block * rows * columns * rotor,
-            bytes_accessed=8 * (block + 1) * rows * columns,
+            flops=12 * n_pairs * rows * columns * rotor,
+            bytes_accessed=8 * (n_pairs + 1) * rows * columns,
             transcendentals=0,
         ),
         name="fold",
-    )(targets, slots, *lowers, *diags, *shares)
+    )(targets, slots, *lowers, *diags, *shares, *carried)
 
 
 def prepare_kernel(block, own_hbm, other_hbm, high_ref, low_ref, diags, sems):
@@ -463,6 +488,7 @@
 
     shares = []
     pieces = []
+    waiting = {}
     residual, slots, targets = first_residual(
         core, targets, other_targets, received, other_core(received), tile_rows
     )
@@ -474,9 +500,21 @@
             residual, pieces = lax.optimization_barrier((residual, pieces))
         residuals = along_x(residual)
         if later < blocks:
+            ahead = {2: (blocks - 2, 1), 3: (blocks - 1, 2)}.get(later, (0, 0))
+            carried = waiting.pop(later, None)
             started, lower_high, lower_low, *diag_tiles = fold(
-                later, targets, slots, lowers, diags if block else (), shares
+                later,
+                targets,
+                slots,
+                lowers,
+                diags if block else (),
+                shares,
+                () if carried is None else (carried[0],),
+                0 if carried is None else carried[1],
+                ahead,
             )
+            if ahead[1]:
+                waiting[ahead[0]] = (diag_tiles.pop(), ahead[1])
         if block == 0 or later == blocks:
             diag_tiles = prepare(block, diags)
         if later == blocks:

time: 281 us -> 281 us (level)
  transfers between devices with their start and end apart: 31 -> 31, of which waited for: 8 -> 9; matrix products, arithmetic and copies ran while one was open for 0% -> 0% of each run, Pallas kernels for 11% -> 11%
where the time goes in v9:
time: 281 us; the launch traced here: 280 us
  blocking collectives  160 us (57%)
  starting transfers between devices  64.6 us (23%)
  Pallas kernels  38.9 us (14%)
  waiting for transfers between devices  13.6 us (5%)
    all_to_all x15, blocking collectives, per_row(): return lax.all_to_all(value, 'row', 0, 0, tiled=True)  160 us
    ppermute x6, starting transfers between devices, other_core(): return lax.ppermute(value, 'col', [(i, i ^ 1) for i in range(peers)])  34.1 us
    ppermute x24, starting transfers between devices, along_x(): lax.ppermute(value, 'col', [(i, i ^ apart) for i in range(peers)])  26.9 us
    pallas_call x7, Pallas kernels, fold(): pl.pallas_call(functools.partial(fold_kernel, block, bool(diags), skip, a...  22.3 us
    all_to_all x1, waiting for transfers between devices, per_row(): return lax.all_to_all(value, 'row', 0, 0, tiled=True)  6.17 us
  transfers between devices with their start and end apart: 31, of which 9 were waited for; matrix products, arithmetic and copies ran while one was open for 0% of the time, Pallas kernels for 11%

profile of v9, /device:TPU:1, one launch (start us, length us, event | category | flops | bytes accessed | tf_op | source)
XLA Modules:
  0.0 280.3 jit_solution(9001704481918409675)
XLA Ops:
  2.1 4.4 %pick.1 = (f32[16,32,128]{2,1,0:T(8,128)}, s32[1,512]{1,0:T(1,128)}) custom-call(s32[1]{0:T(128)} %bitcast.core_ref, s32[1]{0:T(128)S(6)} %copy.10.stride_hbm, s32[1,16]{1,0:T(1,128)} %counts_hbm.1, s32[1,16,32]{2,1,0:T(8,128)} %source_hbm.1, s32[16,32]{1,0:T(8,128)} %bitcast.59, f32[2048,128]{1,0:T(8,128)} %field_hbm.1, f32[2,2048,128]{2,1,0:T(8,128)} %nu_hbm.1), custom_call_target="tpu_custom_call" | custom-call | tf_op jit(solution)/shard_map/pick/pallas_call | solution.py:105
  6.4 16.4 %all_to_all.80 = f32[16,32,128]{2,1,0:T(8,128)S(1)} all-to-all(f32[16,32,128]{2,1,0:T(8,128)} %get-tuple-element.79), channel_id=1, replica_groups=mesh['row'=16,'col'=8] {'row'}, dimensions={0} | all-to-all | bytes 524288 | tf_op jit(solution)/shard_map/all_to_all | solution.py:469
  35.0 10.2 %all_to_all.81.parts_ref = f32[16,32,128]{2,1,0:T(8,128)S(1)} all-to-all(f32[16,32,128]{2,1,0:T(8,128)S(1)} %bitcast.50), channel_id=1, replica_groups=mesh['row'=16,'col'=8] {'row'}, dimensions={0} | all-to-all | bytes 524288 | tf_op jit(solution)/shard_map/all_to_all | solution.py:469
  45.9 3.5 %all-to-all-start.2 = ((f32[16,32,128]{2,1,0:T(8,128)}), f32[16,32,128]{2,1,0:T(8,128)S(1)}, u32[]{:S(2)}, u32[]{:S(2)}) async-start(f32[16,32,128]{2,1,0:T(8,128)} %get-tuple-element.88), calls=%async_computation.2 | async-start | bytes 524288 | tf_op jit(solution)/shard_map/all_to_all | solution.py:469
  50.8 6.2 %all-to-all-done.2 = f32[16,32,128]{2,1,0:T(8,128)S(1)} async-done(((f32[16,32,128]{2,1,0:T(8,128)}), f32[16,32,128]{2,1,0:T(8,128)S(1)}, u32[]{:S(2)}, u32[]{:S(2)}) %all-to-all-start.2) | async-done | bytes 262176 | tf_op jit(solution)/shard_map/all_to_all | solution.py:469
  64.0 10.2 %all_to_all.82.parts_ref = f32[16,32,128]{2,1,0:T(8,128)S(1)} all-to-all(f32[16,32,128]{2,1,0:T(8,128)S(1)} %bitcast.51), channel_id=1, replica_groups=mesh['row'=16,'col'=8] {'row'}, dimensions={0} | all-to-all | bytes 524288 | tf_op jit(solution)/shard_map/all_to_all | solution.py:469
  74.2 10.2 %all_to_all.83 = f32[16,32,128]{2,1,0:T(8,128)S(1)} all-to-all(f32[16,32,128]{2,1,0:T(8,128)S(1)} %get-tuple-element.98), channel_id=1, replica_groups=mesh['row'=16,'col'=8] {'row'}, dimensions={0} | all-to-all | bytes 524288 | tf_op jit(solution)/shard_map/all_to_all | solution.py:469
  88.2 3.6 %fold.9 = (f32[128,128]{1,0:T(8,128)S(1)}, bf16[2,256,512]{2,1,0:T(8,128)(2,1)S(1)}, bf16[2,256,512]{2,1,0:T(8,128)(2,1)S(1)}, bf16[2,512,256]{2,1,0:T(8,128)(2,...) custom-call(s32[2,1,512]{2,1,0:T(1,128)S(1)} %get-tuple-element.89.refs_0_, ...), custom_call_target="tpu_custom_call" | custom-call | flops 1006632960 | bytes 6291456 | tf_op jit(solution)/shard_map/fold/pallas_call | solution.py:302
  92.6 10.1 %all_to_all.84.parts_ref = f32[16,32,128]{2,1,0:T(8,128)S(1)} all-to-all(f32[16,32,128]{2,1,0:T(8,128)S(1)} %bitcast.52), channel_id=1, replica_groups=mesh['row'=16,'col'=8] {'row'}, dimensions={0} | all-to-all | bytes 524288 | tf_op jit(solution)/shard_map/all_to_all | solution.py:469
  102.8 10.7 %all_to_all.85 = f32[16,32,128]{2,1,0:T(8,128)S(1)} all-to-all(f32[16,32,128]{2,1,0:T(8,128)S(1)} %get-tuple-element.104), channel_id=1, replica_groups=mesh['row'=16,'col'=8] {'row'}, dimensions={0} | all-to-all | bytes 524288 | tf_op jit(solution)/shard_map/all_to_all | solution.py:469
  121.6 10.4 %all_to_all.86.parts_ref = f32[16,32,128]{2,1,0:T(8,128)S(1)} all-to-all(f32[16,32,128]{2,1,0:T(8,128)S(1)} %bitcast.53), channel_id=1, replica_groups=mesh['row'=16,'col'=8] {'row'}, dimensions={0} | all-to-all | bytes 524288 | tf_op jit(solution)/shard_map/all_to_all | solution.py:469
  132.1 10.5 %all_to_all.87 = f32[16,32,128]{2,1,0:T(8,128)S(1)} all-to-all(f32[16,32,128]{2,1,0:T(8,128)S(1)} %get-tuple-element.110), channel_id=1, replica_groups=mesh['row'=16,'col'=8] {'row'}, dimensions={0} | all-to-all | bytes 524288 | tf_op jit(solution)/shard_map/all_to_all | solution.py:469
  146.3 3.6 %fold.11 = (f32[128,128]{1,0:T(8,128)S(1)}, bf16[2,256,512]{2,1,0:T(8,128)(2,1)S(1)}, bf16[2,256,512]{2,1,0:T(8,128)(2,1)S(1)}, bf16[2,512,256]{2,1,0:T(8,128)(2,1)S(1)}, bf16[2,512,256]{2,1,0:T(8,128)(2,1)S(1)}) custom-call(s32[2,1,512]{2,1,0:T(1,128)S(1)} %get-tuple-element.89.refs_0_, f32[512,128]{1,0:T(8,128)S(1)} %get-tuple-element.91.refs_1_, ...), custom_call_target="tpu_custom_call" | custom-call | flops 1006632960 | bytes 6291456 | tf_op jit(solution)/shard_map/fold/pallas_call | solution.py:302
  150.5 10.2 %all_to_all.88.parts_ref = f32[16,32,128]{2,1,0:T(8,128)S(1)} all-to-all(f32[16,32,128]{2,1,0:T(8,128)S(1)} %bitcast.54), channel_id=1, replica_groups=mesh['row'=16,'col'=8] {'row'}, dimensions={0} | all-to-all | bytes 524288 | tf_op jit(solution)/shard_map/all_to_all | solution.py:469
  160.7 10.2 %all_to_all.89 = f32[16,32,128]{2,1,0:T(8,128)S(1)} all-to-all(f32[16,32,128]{2,1,0:T(8,128)S(1)} %get-tuple-element.116), channel_id=1, replica_groups=mesh['row'=16,'col'=8] {'row'}, dimensions={0} | all-to-all | bytes 524288 | tf_op jit(solution)/shard_map/all_to_all | solution.py:469
  174.7 3.6 %fold.12 = (f32[128,128]{1,0:T(8,128)S(1)}, bf16[2,256,512]{2,1,0:T(8,128)(2,1)S(1)}, bf16[2,256,512]{2,1,0:T(8,128)(2,1)S(1)}, bf16[2,512,256]{2,1,0:T(8,128)(2,1)S(1)}, bf16[2,512,256]{2,1,0:T(8,128)(2,1)S(1)}) custom-call(s32[2,1,512]{2,1,0:T(1,128)S(1)} %get-tuple-element.89.refs_0_, f32[512,128]{1,0:T(8,128)S(1)} %get-tuple-element.91.refs_1_, ...), custom_call_target="tpu_custom_call" | custom-call | flops 1006632960 | bytes 6291456 | tf_op jit(solution)/shard_map/fold/pallas_call | solution.py:302
  178.8 10.3 %all_to_all.90.parts_ref = f32[16,32,128]{2,1,0:T(8,128)S(1)} all-to-all(f32[16,32,128]{2,1,0:T(8,128)S(1)} %bitcast.55), channel_id=1, replica_groups=mesh['row'=16,'col'=8] {'row'}, dimensions={0} | all-to-all | bytes 524288 | tf_op jit(solution)/shard_map/all_to_all | solution.py:469
  189.2 10.3 %all_to_all.91 = f32[16,32,128]{2,1,0:T(8,128)S(1)} all-to-all(f32[16,32,128]{2,1,0:T(8,128)S(1)} %get-tuple-element.123), channel_id=1, replica_groups=mesh['row'=16,'col'=8] {'row'}, dimensions={0} | all-to-all | bytes 524288 | tf_op jit(solution)/shard_map/all_to_all | solution.py:469
  203.3 4.4 %fold.13 = (f32[128,128]{1,0:T(8,128)S(1)}, bf16[2,256,512]{2,1,0:T(8,128)(2,1)S(1)}, bf16[2,256,512]{2,1,0:T(8,128)(2,1)S(1)}, bf16[2,512,256]{2,1,0:T(8,128)(2,1)S(1)}, bf16[2,512,256]{2,1,0:T(8,128)(2,1)}) custom-call(s32[2,1,512]{2,1,0:T(1,128)S(1)} %get-tuple-element.89.refs_0_, f32[512,128]{1,0:T(8,128)S(1)} %get-tuple-element.91.refs_1_, ...), custom_call_target="tpu_custom_call" | custom-call | flops 1006632960 | bytes 6291456 | tf_op jit(solution)/shard_map/fold/pallas_call | solution.py:302
  209.3 10.5 %all_to_all.92.parts_ref = f32[16,32,128]{2,1,0:T(8,128)S(1)} all-to-all(f32[16,32,128]{2,1,0:T(8,128)S(1)} %bitcast.56), channel_id=1, replica_groups=mesh['row'=16,'col'=8] {'row'}, dimensions={0} | all-to-all | bytes 524288 | tf_op jit(solution)/shard_map/all_to_all | solution.py:469
  219.8 10.1 %all_to_all.93 = f32[16,32,128]{2,1,0:T(8,128)S(1)} all-to-all(f32[16,32,128]{2,1,0:T(8,128)S(1)} %get-tuple-element.130), channel_id=1, replica_groups=mesh['row'=16,'col'=8] {'row'}, dimensions={0} | all-to-all | bytes 524288 | tf_op jit(solution)/shard_map/all_to_all | solution.py:469
  230.5 28.1 %collective-permute-start.25 = (f32[7,32,128]{2,1,0:T(8,128)S(1)}, f32[7,32,128]{2,1,0:T(8,128)S(1)}, u32[]{:S(2)}, u32[]{:S(2)}) collective-permute-start(f32[7,32,128]{2,1,0:T(8,128)S(1)} %join.1.early_ref), channel_id=1, source_target_pairs={{0,1},{1,0},{2,3},{3,2},{4,5},{5,4},{6,7},{7,6},{8,9},{9,8},{10,11... | collective-permute-start | bytes 344072 | tf_op jit(solution)/shard_map/ppermute | solution.py:457
  265.3 10.2 %all_to_all.94 = f32[16,32,128]{2,1,0:T(8,128)S(1)} all-to-all(f32[16,32,128]{2,1,0:T(8,128)S(1)} %bitcast.57), channel_id=1, replica_groups=mesh['row'=16,'col'=8] {'row'}, dimensions={0} | all-to-all | bytes 524288 | tf_op jit(solution)/shard_map/all_to_all | solution.py:469
  275.5 3.3 %collective-permute-start.29 = (f32[32,128]{1,0:T(8,128)S(1)}, f32[32,128]{1,0:T(8,128)S(1)}, u32[]{:S(2)}, u32[]{:S(2)}) collective-permute-start(f32[32,128]{1,0:T(8,128)S(1)} %reduce_sum.9.last_ref), channel_id=1, source_target_pairs={{0,1},{1,0},{2,3},{3,2},{4,5},{5,4},{6,7},{7,6},{8,9},{9,8},{10,11... | collective-permute-start | bytes 49160 | tf_op jit(solution)/shard_map/ppermute | solution.py:457
  (93 shorter events, 58.3 us)
Async XLA Ops:
  0.0 22.8 %collective-permute-start = (f32[8,512,256]{2,1,0:T(8,128)}, f32[8,512,256]{2,1,0:T(8,128)}, u32[]{:S(2)}, u32[]{:S(2)}) collective-permute-start(f32[8,512,256]{2,1,0:T(8,128)} %refs_4_.11), channel_id=1, source_target_pairs={{0,1},{1,0},{2,3},{3,2},{4,5},{5,4},{6,7},{7,6},{8,9},{9,8},{10,11... | collective-permute-start | bytes 12582920 | tf_op jit(solution)/shard_map/ppermute | solution.py:457
  26.6 22.9 %collective-permute-start.6 = (f32[28,256,512]{2,1,0:T(8,128)}, f32[28,256,512]{2,1,0:T(8,128)}, u32[]{:S(2)}, u32[]{:S(2)}) collective-permute-start(f32[28,256,512]{2,1,0:T(8,128)} %refs_2_.13), channel_id=1, source_target_pairs={{0,1},{1,0},{2,3},{3,2},{4,5},{5,4},{6,7},{7,6},{8,9},{9,8},{10,11... | collective-permute-start | bytes 44040200 | tf_op jit(solution)/shard_map/ppermute | solution.py:457
  26.9 5.0 %collective-permute-start.3 = (f32[128,128]{1,0:T(8,128)S(1)}, f32[128,128]{1,0:T(8,128)S(1)}, u32[]{:S(2)}, u32[]{:S(2)}) collective-permute-start(f32[128,128]{1,0:T(8,128)S(1)} %get-tuple-element.85.refs_0_), channel_id=1, source_target_pairs={{0,2},{1,3},{2,0},{3,1},{4,6},{5,7},{6,4},{7,5},{8,10},{9,11},{10,... | collective-permute-start | bytes 196616 | tf_op jit(solution)/shard_map/ppermute | solution.py:463
  29.9 4.6 %collective-permute-start.5 = (f32[128,128]{1,0:T(8,128)S(1)}, f32[128,128]{1,0:T(8,128)S(1)}, u32[]{:S(2)}, u32[]{:S(2)}) collective-permute-start(f32[128,128]{1,0:T(8,128)S(1)} %get-tuple-element.85.refs_0_), channel_id=1, source_target_pairs={{0,4},{1,5},{2,6},{3,7},{4,0},{5,1},{6,2},{7,3},{8,12},{9,13},{10,... | collective-permute-start | bytes 196616 | tf_op jit(solution)/shard_map/ppermute | solution.py:463
  45.9 11.0 %all-to-all-start.2 = ((f32[16,32,128]{2,1,0:T(8,128)}), f32[16,32,128]{2,1,0:T(8,128)S(1)}, u32[]{:S(2)}, u32[]{:S(2)}) async-start(f32[16,32,128]{2,1,0:T(8,128)} %get-tuple-element.88), calls=%async_computation.2 | async-start | bytes 524288 | tf_op jit(solution)/shard_map/all_to_all | solution.py:469
  57.5 5.9 %collective-permute-start.7 = (f32[128,128]{1,0:T(8,128)S(1)}, f32[128,128]{1,0:T(8,128)S(1)}, u32[]{:S(2)}, u32[]{:S(2)}) collective-permute-start(f32[128,128]{1,0:T(8,128)S(1)} %lower.7.refs_0_), channel_id=1, source_target_pairs={{0,2},{1,3},{2,0},{3,1},{4,6},{5,7},{6,4},{7,5},{8,10},{9,11},{10,... | collective-permute-start | bytes 196616 | tf_op jit(solution)/shard_map/ppermute | solution.py:463
  57.9 5.6 %collective-permute-start.8 = (f32[128,128]{1,0:T(8,128)S(1)}, f32[128,128]{1,0:T(8,128)S(1)}, u32[]{:S(2)}, u32[]{:S(2)}) collective-permute-start(f32[128,128]{1,0:T(8,128)S(1)} %lower.7.refs_0_), channel_id=1, source_target_pairs={{0,6},{1,7},{2,4},{3,5},{4,2},{5,3},{6,0},{7,1},{8,14},{9,15},{10,... | collective-permute-start | bytes 196616 | tf_op jit(solution)/shard_map/ppermute | solution.py:463
  58.7 4.8 %collective-permute-start.9 = (f32[128,128]{1,0:T(8,128)S(1)}, f32[128,128]{1,0:T(8,128)S(1)}, u32[]{:S(2)}, u32[]{:S(2)}) collective-permute-start(f32[128,128]{1,0:T(8,128)S(1)} %lower.7.refs_0_), channel_id=1, source_target_pairs={{0,4},{1,5},{2,6},{3,7},{4,0},{5,1},{6,2},{7,3},{8,12},{9,13},{10,... | collective-permute-start | bytes 196616 | tf_op jit(solution)/shard_map/ppermute | solution.py:463
  84.8 6.9 %collective-permute-start.10 = (f32[128,128]{1,0:T(8,128)S(1)}, f32[128,128]{1,0:T(8,128)S(1)}, u32[]{:S(2)}, u32[]{:S(2)}) collective-permute-start(f32[128,128]{1,0:T(8,128)S(1)} %lower.8.refs_0_), channel_id=1, source_target_pairs={{0,2},{1,3},{2,0},{3,1},{4,6},{5,7},{6,4},{7,5},{8,10},{9,11},{10,... | collective-permute-start | bytes 196616 | tf_op jit(solution)/shard_map/ppermute | solution.py:463
  85.5 6.3 %collective-permute-start.11 = (f32[128,128]{1,0:T(8,128)S(1)}, f32[128,128]{1,0:T(8,128)S(1)}, u32[]{:S(2)}, u32[]{:S(2)}) collective-permute-start(f32[128,128]{1,0:T(8,128)S(1)} %lower.8.refs_0_), channel_id=1, source_target_pairs={{0,6},{1,7},{2,4},{3,5},{4,2},{5,3},{6,0},{7,1},{8,14},{9,15},{10,... | collective-permute-start | bytes 196616 | tf_op jit(solution)/shard_map/ppermute | solution.py:463
  87.2 4.9 %collective-permute-start.12 = (f32[128,128]{1,0:T(8,128)S(1)}, f32[128,128]{1,0:T(8,128)S(1)}, u32[]{:S(2)}, u32[]{:S(2)}) collective-permute-start(f32[128,128]{1,0:T(8,128)S(1)} %lower.8.refs_0_), channel_id=1, source_target_pairs={{0,4},{1,5},{2,6},{3,7},{4,0},{5,1},{6,2},{7,3},{8,12},{9,13},{10,... | collective-permute-start | bytes 196616 | tf_op jit(solution)/shard_map/ppermute | solution.py:463
  113.9 6.5 %collective-permute-start.13 = (f32[128,128]{1,0:T(8,128)S(1)}, f32[128,128]{1,0:T(8,128)S(1)}, u32[]{:S(2)}, u32[]{:S(2)}) collective-permute-start(f32[128,128]{1,0:T(8,128)S(1)} %lower.9.refs_0_), channel_id=1, source_target_pairs={{0,2},{1,3},{2,0},{3,1},{4,6},{5,7},{6,4},{7,5},{8,10},{9,11},{10,... | collective-permute-start | bytes 196616 | tf_op jit(solution)/shard_map/ppermute | solution.py:463
  114.4 6.0 %collective-permute-start.14 = (f32[128,128]{1,0:T(8,128)S(1)}, f32[128,128]{1,0:T(8,128)S(1)}, u32[]{:S(2)}, u32[]{:S(2)}) collective-permute-start(f32[128,128]{1,0:T(8,128)S(1)} %lower.9.refs_0_), channel_id=1, source_target_pairs={{0,6},{1,7},{2,4},{3,5},{4,2},{5,3},{6,0},{7,1},{8,14},{9,15},{10,... | collective-permute-start | bytes 196616 | tf_op jit(solution)/shard_map/ppermute | solution.py:463
  143.0 6.9 %collective-permute-start.16 = (f32[128,128]{1,0:T(8,128)S(1)}, f32[128,128]{1,0:T(8,128)S(1)}, u32[]{:S(2)}, u32[]{:S(2)}) collective-permute-start(f32[128,128]{1,0:T(8,128)S(1)} %lower.10.refs_0_), channel_id=1, source_target_pairs={{0,2},{1,3},{2,0},{3,1},{4,6},{5,7},{6,4},{7,5},{8,10},{9,11},{10,... | collective-permute-start | bytes 196616 | tf_op jit(solution)/shard_map/ppermute | solution.py:463
  143.1 6.8 %collective-permute-start.17 = (f32[128,128]{1,0:T(8,128)S(1)}, f32[128,128]{1,0:T(8,128)S(1)}, u32[]{:S(2)}, u32[]{:S(2)}) collective-permute-start(f32[128,128]{1,0:T(8,128)S(1)} %lower.10.refs_0_), channel_id=1, source_target_pairs={{0,6},{1,7},{2,4},{3,5},{4,2},{5,3},{6,0},{7,1},{8,14},{9,15},{10,... | collective-permute-start | bytes 196616 | tf_op jit(solution)/shard_map/ppermute | solution.py:463
  144.6 5.4 %collective-permute-start.18 = (f32[128,128]{1,0:T(8,128)S(1)}, f32[128,128]{1,0:T(8,128)S(1)}, u32[]{:S(2)}, u32[]{:S(2)}) collective-permute-start(f32[128,128]{1,0:T(8,128)S(1)} %lower.10.refs_0_), channel_id=1, source_target_pairs={{0,4},{1,5},{2,6},{3,7},{4,0},{5,1},{6,2},{7,3},{8,12},{9,13},{10,... | collective-permute-start | bytes 196616 | tf_op jit(solution)/shard_map/ppermute | solution.py:463
  171.3 7.0 %collective-permute-start.19 = (f32[128,128]{1,0:T(8,128)S(1)}, f32[128,128]{1,0:T(8,128)S(1)}, u32[]{:S(2)}, u32[]{:S(2)}) collective-permute-start(f32[128,128]{1,0:T(8,128)S(1)} %lower.11.refs_0_), channel_id=1, source_target_pairs={{0,2},{1,3},{2,0},{3,1},{4,6},{5,7},{6,4},{7,5},{8,10},{9,11},{10,... | collective-permute-start | bytes 196616 | tf_op jit(solution)/shard_map/ppermute | solution.py:463
  171.5 6.8 %collective-permute-start.20 = (f32[128,128]{1,0:T(8,128)S(1)}, f32[128,128]{1,0:T(8,128)S(1)}, u32[]{:S(2)}, u32[]{:S(2)}) collective-permute-start(f32[128,128]{1,0:T(8,128)S(1)} %lower.11.refs_0_), channel_id=1, source_target_pairs={{0,6},{1,7},{2,4},{3,5},{4,2},{5,3},{6,0},{7,1},{8,14},{9,15},{10,... | collective-permute-start | bytes 196616 | tf_op jit(solution)/shard_map/ppermute | solution.py:463
  172.9 5.4 %collective-permute-start.21 = (f32[128,128]{1,0:T(8,128)S(1)}, f32[128,128]{1,0:T(8,128)S(1)}, u32[]{:S(2)}, u32[]{:S(2)}) collective-permute-start(f32[128,128]{1,0:T(8,128)S(1)} %lower.11.refs_0_), channel_id=1, source_target_pairs={{0,4},{1,5},{2,6},{3,7},{4,0},{5,1},{6,2},{7,3},{8,12},{9,13},{10,... | collective-permute-start | bytes 196616 | tf_op jit(solution)/shard_map/ppermute | solution.py:463
  200.0 7.8 %collective-permute-start.22 = (f32[128,128]{1,0:T(8,128)S(1)}, f32[128,128]{1,0:T(8,128)S(1)}, u32[]{:S(2)}, u32[]{:S(2)}) collective-permute-start(f32[128,128]{1,0:T(8,128)S(1)} %lower.12.refs_0_), channel_id=1, source_target_pairs={{0,2},{1,3},{2,0},{3,1},{4,6},{5,7},{6,4},{7,5},{8,10},{9,11},{10,... | collective-permute-start | bytes 196616 | tf_op jit(solution)/shard_map/ppermute | solution.py:463
  200.2 7.6 %collective-permute-start.23 = (f32[128,128]{1,0:T(8,128)S(1)}, f32[128,128]{1,0:T(8,128)S(1)}, u32[]{:S(2)}, u32[]{:S(2)}) collective-permute-start(f32[128,128]{1,0:T(8,128)S(1)} %lower.12.refs_0_), channel_id=1, source_target_pairs={{0,6},{1,7},{2,4},{3,5},{4,2},{5,3},{6,0},{7,1},{8,14},{9,15},{10,... | collective-permute-start | bytes 196616 | tf_op jit(solution)/shard_map/ppermute | solution.py:463
  201.6 6.2 %collective-permute-start.24 = (f32[128,128]{1,0:T(8,128)S(1)}, f32[128,128]{1,0:T(8,128)S(1)}, u32[]{:S(2)}, u32[]{:S(2)}) collective-permute-start(f32[128,128]{1,0:T(8,128)S(1)} %lower.12.refs_0_), channel_id=1, source_target_pairs={{0,4},{1,5},{2,6},{3,7},{4,0},{5,1},{6,2},{7,3},{8,12},{9,13},{10,... | collective-permute-start | bytes 196616 | tf_op jit(solution)/shard_map/ppermute | solution.py:463
  230.5 32.7 %collective-permute-start.25 = (f32[7,32,128]{2,1,0:T(8,128)S(1)}, f32[7,32,128]{2,1,0:T(8,128)S(1)}, u32[]{:S(2)}, u32[]{:S(2)}) collective-permute-start(f32[7,32,128]{2,1,0:T(8,128)S(1)} %join.1.early_ref), channel_id=1, source_target_pairs={{0,1},{1,0},{2,3},{3,2},{4,5},{5,4},{6,7},{7,6},{8,9},{9,8},{10,11... | collective-permute-start | bytes 344072 | tf_op jit(solution)/shard_map/ppermute | solution.py:457
  260.1 4.7 %collective-permute-start.28 = (f32[128,128]{1,0:T(8,128)S(1)}, f32[128,128]{1,0:T(8,128)S(1)}, u32[]{:S(2)}, u32[]{:S(2)}) collective-permute-start(f32[128,128]{1,0:T(8,128)S(1)} %lower.13.refs_0_), channel_id=1, source_target_pairs={{0,4},{1,5},{2,6},{3,7},{4,0},{5,1},{6,2},{7,3},{8,12},{9,13},{10,... | collective-permute-start | bytes 196616 | tf_op jit(solution)/shard_map/ppermute | solution.py:463
  (9 other events, 27.5 us)

commit v10 on v9

--- a/solution.py
+++ b/solution.py
@@ -76,7 +76,7 @@
         load.wait()
     stride = stride_ref[0]
     slots = source_ref.shape[2]
-    chunk = 64
+    chunk = 256
     for at_part in range(parts):
         for load in loads[at_part]:
             load.wait()

time: 281 us -> 281 us (level)
  transfers between devices with their start and end apart: 31 -> 31, of which waited for: 9 -> 8; matrix products, arithmetic and copies ran while one was open for 0% -> 0% of each run, Pallas kernels for 11% -> 11%
where the time goes in v10:
time: 281 us; the launch traced here: 280 us
  blocking collectives  160 us (57%)
  starting transfers between devices  64.6 us (23%)
  Pallas kernels  38.9 us (14%)
  waiting for transfers between devices  13.6 us (5%)
    all_to_all x15, blocking collectives, per_row(): return lax.all_to_all(value, 'row', 0, 0, tiled=True)  160 us
    ppermute x6, starting transfers between devices, other_core(): return lax.ppermute(value, 'col', [(i, i ^ 1) for i in range(peers)])  34.2 us
    ppermute x24, starting transfers between devices, along_x(): lax.ppermute(value, 'col', [(i, i ^ apart) for i in range(peers)])  26.9 us
    pallas_call x7, Pallas kernels, fold(): pl.pallas_call(functools.partial(fold_kernel, block, bool(diags), skip, a...  22.3 us
    all_to_all x1, waiting for transfers between devices, per_row(): return lax.all_to_all(value, 'row', 0, 0, tiled=True)  6.17 us
  transfers between devices with their start and end apart: 31, of which 8 were waited for; matrix products, arithmetic and copies ran while one was open for 0% of the time, Pallas kernels for 11%

profile of v10, /device:TPU:1, one launch (start us, length us, event | category | flops | bytes accessed | tf_op | source)
XLA Modules:
  0.0 280.3 jit_solution(10735270926949699827)
XLA Ops:
  2.1 4.3 %pick.1 = (f32[16,32,128]{2,1,0:T(8,128)}, s32[1,512]{1,0:T(1,128)}) custom-call(s32[1]{0:T(128)} %bitcast.core_ref, s32[1]{0:T(128)S(6)} %copy.10.stride_hbm, s32[1,16]{1,0:T(1,128)} %counts_hbm.1, s32[1,16,32]{2,1,0:T(8,128)} %source_hbm.1, s32[16,32]{1,0:T(8,128)} %bitcast.59, f32[2048,128]{1,0:T(8,128)} %field_hbm.1, f32[2,2048,128]{2,1,0:T(8,128)} %nu_hbm.1), custom_call_target="tpu_custom_call" | custom-call | tf_op jit(solution)/shard_map/pick/pallas_call | solution.py:105
  6.4 16.4 %all_to_all.80 = f32[16,32,128]{2,1,0:T(8,128)S(1)} all-to-all(f32[16,32,128]{2,1,0:T(8,128)} %get-tuple-element.79), channel_id=1, replica_groups=mesh['row'=16,'col'=8] {'row'}, dimensions={0} | all-to-all | bytes 524288 | tf_op jit(solution)/shard_map/all_to_all | solution.py:469
  35.0 10.2 %all_to_all.81.parts_ref = f32[16,32,128]{2,1,0:T(8,128)S(1)} all-to-all(f32[16,32,128]{2,1,0:T(8,128)S(1)} %bitcast.50), channel_id=1, replica_groups=mesh['row'=16,'col'=8] {'row'}, dimensions={0} | all-to-all | bytes 524288 | tf_op jit(solution)/shard_map/all_to_all | solution.py:469
  45.9 3.5 %all-to-all-start.2 = ((f32[16,32,128]{2,1,0:T(8,128)}), f32[16,32,128]{2,1,0:T(8,128)S(1)}, u32[]{:S(2)}, u32[]{:S(2)}) async-start(f32[16,32,128]{2,1,0:T(8,128)} %get-tuple-element.88), calls=%async_computation.2 | async-start | bytes 524288 | tf_op jit(solution)/shard_map/all_to_all | solution.py:469
  50.8 6.2 %all-to-all-done.2 = f32[16,32,128]{2,1,0:T(8,128)S(1)} async-done(((f32[16,32,128]{2,1,0:T(8,128)}), f32[16,32,128]{2,1,0:T(8,128)S(1)}, u32[]{:S(2)}, u32[]{:S(2)}) %all-to-all-start.2) | async-done | bytes 262176 | tf_op jit(solution)/shard_map/all_to_all | solution.py:469
  63.9 10.2 %all_to_all.82.parts_ref = f32[16,32,128]{2,1,0:T(8,128)S(1)} all-to-all(f32[16,32,128]{2,1,0:T(8,128)S(1)} %bitcast.51), channel_id=1, replica_groups=mesh['row'=16,'col'=8] {'row'}, dimensions={0} | all-to-all | bytes 524288 | tf_op jit(solution)/shard_map/all_to_all | solution.py:469
  74.2 10.2 %all_to_all.83 = f32[16,32,128]{2,1,0:T(8,128)S(1)} all-to-all(f32[16,32,128]{2,1,0:T(8,128)S(1)} %get-tuple-element.98), channel_id=1, replica_groups=mesh['row'=16,'col'=8] {'row'}, dimensions={0} | all-to-all | bytes 524288 | tf_op jit(solution)/shard_map/all_to_all | solution.py:469
  88.1 3.6 %fold.9 = (f32[128,128]{1,0:T(8,128)S(1)}, bf16[2,256,512]{2,1,0:T(8,128)(2,1)S(1)}, bf16[2,256,512]{2,1,0:T(8,128)(2,1)S(1)}, bf16[2,512,256]{2,1,0:T(8,128)(2,...) custom-call(s32[2,1,512]{2,1,0:T(1,128)S(1)} %get-tuple-element.89.refs_0_, ...), custom_call_target="tpu_custom_call" | custom-call | flops 1006632960 | bytes 6291456 | tf_op jit(solution)/shard_map/fold/pallas_call | solution.py:302
  92.6 10.1 %all_to_all.84.parts_ref = f32[16,32,128]{2,1,0:T(8,128)S(1)} all-to-all(f32[16,32,128]{2,1,0:T(8,128)S(1)} %bitcast.52), channel_id=1, replica_groups=mesh['row'=16,'col'=8] {'row'}, dimensions={0} | all-to-all | bytes 524288 | tf_op jit(solution)/shard_map/all_to_all | solution.py:469
  102.7 10.7 %all_to_all.85 = f32[16,32,128]{2,1,0:T(8,128)S(1)} all-to-all(f32[16,32,128]{2,1,0:T(8,128)S(1)} %get-tuple-element.104), channel_id=1, replica_groups=mesh['row'=16,'col'=8] {'row'}, dimensions={0} | all-to-all | bytes 524288 | tf_op jit(solution)/shard_map/all_to_all | solution.py:469
  121.6 10.4 %all_to_all.86.parts_ref = f32[16,32,128]{2,1,0:T(8,128)S(1)} all-to-all(f32[16,32,128]{2,1,0:T(8,128)S(1)} %bitcast.53), channel_id=1, replica_groups=mesh['row'=16,'col'=8] {'row'}, dimensions={0} | all-to-all | bytes 524288 | tf_op jit(solution)/shard_map/all_to_all | solution.py:469
  132.0 10.5 %all_to_all.87 = f32[16,32,128]{2,1,0:T(8,128)S(1)} all-to-all(f32[16,32,128]{2,1,0:T(8,128)S(1)} %get-tuple-element.110), channel_id=1, replica_groups=mesh['row'=16,'col'=8] {'row'}, dimensions={0} | all-to-all | bytes 524288 | tf_op jit(solution)/shard_map/all_to_all | solution.py:469
  146.3 3.6 %fold.11 = (f32[128,128]{1,0:T(8,128)S(1)}, bf16[2,256,512]{2,1,0:T(8,128)(2,1)S(1)}, bf16[2,256,512]{2,1,0:T(8,128)(2,1)S(1)}, bf16[2,512,256]{2,1,0:T(8,128)(2,1)S(1)}, bf16[2,512,256]{2,1,0:T(8,128)(2,1)S(1)}) custom-call(s32[2,1,512]{2,1,0:T(1,128)S(1)} %get-tuple-element.89.refs_0_, f32[512,128]{1,0:T(8,128)S(1)} %get-tuple-element.91.refs_1_, ...), custom_call_target="tpu_custom_call" | custom-call | flops 1006632960 | bytes 6291456 | tf_op jit(solution)/shard_map/fold/pallas_call | solution.py:302
  150.5 10.2 %all_to_all.88.parts_ref = f32[16,32,128]{2,1,0:T(8,128)S(1)} all-to-all(f32[16,32,128]{2,1,0:T(8,128)S(1)} %bitcast.54), channel_id=1, replica_groups=mesh['row'=16,'col'=8] {'row'}, dimensions={0} | all-to-all | bytes 524288 | tf_op jit(solution)/shard_map/all_to_all | solution.py:469
  160.7 10.2 %all_to_all.89 = f32[16,32,128]{2,1,0:T(8,128)S(1)} all-to-all(f32[16,32,128]{2,1,0:T(8,128)S(1)} %get-tuple-element.116), channel_id=1, replica_groups=mesh['row'=16,'col'=8] {'row'}, dimensions={0} | all-to-all | bytes 524288 | tf_op jit(solution)/shard_map/all_to_all | solution.py:469
  174.6 3.6 %fold.12 = (f32[128,128]{1,0:T(8,128)S(1)}, bf16[2,256,512]{2,1,0:T(8,128)(2,1)S(1)}, bf16[2,256,512]{2,1,0:T(8,128)(2,1)S(1)}, bf16[2,512,256]{2,1,0:T(8,128)(2,1)S(1)}, bf16[2,512,256]{2,1,0:T(8,128)(2,1)S(1)}) custom-call(s32[2,1,512]{2,1,0:T(1,128)S(1)} %get-tuple-element.89.refs_0_, f32[512,128]{1,0:T(8,128)S(1)} %get-tuple-element.91.refs_1_, ...), custom_call_target="tpu_custom_call" | custom-call | flops 1006632960 | bytes 6291456 | tf_op jit(solution)/shard_map/fold/pallas_call | solution.py:302
  178.8 10.3 %all_to_all.90.parts_ref = f32[16,32,128]{2,1,0:T(8,128)S(1)} all-to-all(f32[16,32,128]{2,1,0:T(8,128)S(1)} %bitcast.55), channel_id=1, replica_groups=mesh['row'=16,'col'=8] {'row'}, dimensions={0} | all-to-all | bytes 524288 | tf_op jit(solution)/shard_map/all_to_all | solution.py:469
  189.1 10.3 %all_to_all.91 = f32[16,32,128]{2,1,0:T(8,128)S(1)} all-to-all(f32[16,32,128]{2,1,0:T(8,128)S(1)} %get-tuple-element.123), channel_id=1, replica_groups=mesh['row'=16,'col'=8] {'row'}, dimensions={0} | all-to-all | bytes 524288 | tf_op jit(solution)/shard_map/all_to_all | solution.py:469
  203.3 4.4 %fold.13 = (f32[128,128]{1,0:T(8,128)S(1)}, bf16[2,256,512]{2,1,0:T(8,128)(2,1)S(1)}, bf16[2,256,512]{2,1,0:T(8,128)(2,1)S(1)}, bf16[2,512,256]{2,1,0:T(8,128)(2,1)S(1)}, bf16[2,512,256]{2,1,0:T(8,128)(2,1)}) custom-call(s32[2,1,512]{2,1,0:T(1,128)S(1)} %get-tuple-element.89.refs_0_, f32[512,128]{1,0:T(8,128)S(1)} %get-tuple-element.91.refs_1_, ...), custom_call_target="tpu_custom_call" | custom-call | flops 1006632960 | bytes 6291456 | tf_op jit(solution)/shard_map/fold/pallas_call | solution.py:302
  209.3 10.5 %all_to_all.92.parts_ref = f32[16,32,128]{2,1,0:T(8,128)S(1)} all-to-all(f32[16,32,128]{2,1,0:T(8,128)S(1)} %bitcast.56), channel_id=1, replica_groups=mesh['row'=16,'col'=8] {'row'}, dimensions={0} | all-to-all | bytes 524288 | tf_op jit(solution)/shard_map/all_to_all | solution.py:469
  219.8 10.1 %all_to_all.93 = f32[16,32,128]{2,1,0:T(8,128)S(1)} all-to-all(f32[16,32,128]{2,1,0:T(8,128)S(1)} %get-tuple-element.130), channel_id=1, replica_groups=mesh['row'=16,'col'=8] {'row'}, dimensions={0} | all-to-all | bytes 524288 | tf_op jit(solution)/shard_map/all_to_all | solution.py:469
  230.5 28.1 %collective-permute-start.25 = (f32[7,32,128]{2,1,0:T(8,128)S(1)}, f32[7,32,128]{2,1,0:T(8,128)S(1)}, u32[]{:S(2)}, u32[]{:S(2)}) collective-permute-start(f32[7,32,128]{2,1,0:T(8,128)S(1)} %join.1.early_ref), channel_id=1, source_target_pairs={{0,1},{1,0},{2,3},{3,2},{4,5},{5,4},{6,7},{7,6},{8,9},{9,8},{10,11... | collective-permute-start | bytes 344072 | tf_op jit(solution)/shard_map/ppermute | solution.py:457
  265.2 10.2 %all_to_all.94 = f32[16,32,128]{2,1,0:T(8,128)S(1)} all-to-all(f32[16,32,128]{2,1,0:T(8,128)S(1)} %bitcast.57), channel_id=1, replica_groups=mesh['row'=16,'col'=8] {'row'}, dimensions={0} | all-to-all | bytes 524288 | tf_op jit(solution)/shard_map/all_to_all | solution.py:469
  275.4 3.3 %collective-permute-start.29 = (f32[32,128]{1,0:T(8,128)S(1)}, f32[32,128]{1,0:T(8,128)S(1)}, u32[]{:S(2)}, u32[]{:S(2)}) collective-permute-start(f32[32,128]{1,0:T(8,128)S(1)} %reduce_sum.9.last_ref), channel_id=1, source_target_pairs={{0,1},{1,0},{2,3},{3,2},{4,5},{5,4},{6,7},{7,6},{8,9},{9,8},{10,11... | collective-permute-start | bytes 49160 | tf_op jit(solution)/shard_map/ppermute | solution.py:457
  (93 shorter events, 58.2 us)
Async XLA Ops:
  0.0 22.8 %collective-permute-start = (f32[8,512,256]{2,1,0:T(8,128)}, f32[8,512,256]{2,1,0:T(8,128)}, u32[]{:S(2)}, u32[]{:S(2)}) collective-permute-start(f32[8,512,256]{2,1,0:T(8,128)} %refs_4_.11), channel_id=1, source_target_pairs={{0,1},{1,0},{2,3},{3,2},{4,5},{5,4},{6,7},{7,6},{8,9},{9,8},{10,11... | collective-permute-start | bytes 12582920 | tf_op jit(solution)/shard_map/ppermute | solution.py:457
  26.6 22.9 %collective-permute-start.6 = (f32[28,256,512]{2,1,0:T(8,128)}, f32[28,256,512]{2,1,0:T(8,128)}, u32[]{:S(2)}, u32[]{:S(2)}) collective-permute-start(f32[28,256,512]{2,1,0:T(8,128)} %refs_2_.13), channel_id=1, source_target_pairs={{0,1},{1,0},{2,3},{3,2},{4,5},{5,4},{6,7},{7,6},{8,9},{9,8},{10,11... | collective-permute-start | bytes 44040200 | tf_op jit(solution)/shard_map/ppermute | solution.py:457
  26.8 5.0 %collective-permute-start.3 = (f32[128,128]{1,0:T(8,128)S(1)}, f32[128,128]{1,0:T(8,128)S(1)}, u32[]{:S(2)}, u32[]{:S(2)}) collective-permute-start(f32[128,128]{1,0:T(8,128)S(1)} %get-tuple-element.85.refs_0_), channel_id=1, source_target_pairs={{0,2},{1,3},{2,0},{3,1},{4,6},{5,7},{6,4},{7,5},{8,10},{9,11},{10,... | collective-permute-start | bytes 196616 | tf_op jit(solution)/shard_map/ppermute | solution.py:463
  29.9 4.6 %collective-permute-start.5 = (f32[128,128]{1,0:T(8,128)S(1)}, f32[128,128]{1,0:T(8,128)S(1)}, u32[]{:S(2)}, u32[]{:S(2)}) collective-permute-start(f32[128,128]{1,0:T(8,128)S(1)} %get-tuple-element.85.refs_0_), channel_id=1, source_target_pairs={{0,4},{1,5},{2,6},{3,7},{4,0},{5,1},{6,2},{7,3},{8,12},{9,13},{10,... | collective-permute-start | bytes 196616 | tf_op jit(solution)/shard_map/ppermute | solution.py:463
  45.9 11.0 %all-to-all-start.2 = ((f32[16,32,128]{2,1,0:T(8,128)}), f32[16,32,128]{2,1,0:T(8,128)S(1)}, u32[]{:S(2)}, u32[]{:S(2)}) async-start(f32[16,32,128]{2,1,0:T(8,128)} %get-tuple-element.88), calls=%async_computation.2 | async-start | bytes 524288 | tf_op jit(solution)/shard_map/all_to_all | solution.py:469
  57.4 5.9 %collective-permute-start.7 = (f32[128,128]{1,0:T(8,128)S(1)}, f32[128,128]{1,0:T(8,128)S(1)}, u32[]{:S(2)}, u32[]{:S(2)}) collective-permute-start(f32[128,128]{1,0:T(8,128)S(1)} %lower.7.refs_0_), channel_id=1, source_target_pairs={{0,2},{1,3},{2,0},{3,1},{4,6},{5,7},{6,4},{7,5},{8,10},{9,11},{10,... | collective-permute-start | bytes 196616 | tf_op jit(solution)/shard_map/ppermute | solution.py:463
  57.8 5.6 %collective-permute-start.8 = (f32[128,128]{1,0:T(8,128)S(1)}, f32[128,128]{1,0:T(8,128)S(1)}, u32[]{:S(2)}, u32[]{:S(2)}) collective-permute-start(f32[128,128]{1,0:T(8,128)S(1)} %lower.7.refs_0_), channel_id=1, source_target_pairs={{0,6},{1,7},{2,4},{3,5},{4,2},{5,3},{6,0},{7,1},{8,14},{9,15},{10,... | collective-permute-start | bytes 196616 | tf_op jit(solution)/shard_map/ppermute | solution.py:463
  58.6 4.8 %collective-permute-start.9 = (f32[128,128]{1,0:T(8,128)S(1)}, f32[128,128]{1,0:T(8,128)S(1)}, u32[]{:S(2)}, u32[]{:S(2)}) collective-permute-start(f32[128,128]{1,0:T(8,128)S(1)} %lower.7.refs_0_), channel_id=1, source_target_pairs={{0,4},{1,5},{2,6},{3,7},{4,0},{5,1},{6,2},{7,3},{8,12},{9,13},{10,... | collective-permute-start | bytes 196616 | tf_op jit(solution)/shard_map/ppermute | solution.py:463
  84.8 6.9 %collective-permute-start.10 = (f32[128,128]{1,0:T(8,128)S(1)}, f32[128,128]{1,0:T(8,128)S(1)}, u32[]{:S(2)}, u32[]{:S(2)}) collective-permute-start(f32[128,128]{1,0:T(8,128)S(1)} %lower.8.refs_0_), channel_id=1, source_target_pairs={{0,2},{1,3},{2,0},{3,1},{4,6},{5,7},{6,4},{7,5},{8,10},{9,11},{10,... | collective-permute-start | bytes 196616 | tf_op jit(solution)/shard_map/ppermute | solution.py:463
  85.4 6.3 %collective-permute-start.11 = (f32[128,128]{1,0:T(8,128)S(1)}, f32[128,128]{1,0:T(8,128)S(1)}, u32[]{:S(2)}, u32[]{:S(2)}) collective-permute-start(f32[128,128]{1,0:T(8,128)S(1)} %lower.8.refs_0_), channel_id=1, source_target_pairs={{0,6},{1,7},{2,4},{3,5},{4,2},{5,3},{6,0},{7,1},{8,14},{9,15},{10,... | collective-permute-start | bytes 196616 | tf_op jit(solution)/shard_map/ppermute | solution.py:463
  87.1 4.9 %collective-permute-start.12 = (f32[128,128]{1,0:T(8,128)S(1)}, f32[128,128]{1,0:T(8,128)S(1)}, u32[]{:S(2)}, u32[]{:S(2)}) collective-permute-start(f32[128,128]{1,0:T(8,128)S(1)} %lower.8.refs_0_), channel_id=1, source_target_pairs={{0,4},{1,5},{2,6},{3,7},{4,0},{5,1},{6,2},{7,3},{8,12},{9,13},{10,... | collective-permute-start | bytes 196616 | tf_op jit(solution)/shard_map/ppermute | solution.py:463
  113.9 6.5 %collective-permute-start.13 = (f32[128,128]{1,0:T(8,128)S(1)}, f32[128,128]{1,0:T(8,128)S(1)}, u32[]{:S(2)}, u32[]{:S(2)}) collective-permute-start(f32[128,128]{1,0:T(8,128)S(1)} %lower.9.refs_0_), channel_id=1, source_target_pairs={{0,2},{1,3},{2,0},{3,1},{4,6},{5,7},{6,4},{7,5},{8,10},{9,11},{10,... | collective-permute-start | bytes 196616 | tf_op jit(solution)/shard_map/ppermute | solution.py:463
  114.3 6.0 %collective-permute-start.14 = (f32[128,128]{1,0:T(8,128)S(1)}, f32[128,128]{1,0:T(8,128)S(1)}, u32[]{:S(2)}, u32[]{:S(2)}) collective-permute-start(f32[128,128]{1,0:T(8,128)S(1)} %lower.9.refs_0_), channel_id=1, source_target_pairs={{0,6},{1,7},{2,4},{3,5},{4,2},{5,3},{6,0},{7,1},{8,14},{9,15},{10,... | collective-permute-start | bytes 196616 | tf_op jit(solution)/shard_map/ppermute | solution.py:463
  143.0 6.9 %collective-permute-start.16 = (f32[128,128]{1,0:T(8,128)S(1)}, f32[128,128]{1,0:T(8,128)S(1)}, u32[]{:S(2)}, u32[]{:S(2)}) collective-permute-start(f32[128,128]{1,0:T(8,128)S(1)} %lower.10.refs_0_), channel_id=1, source_target_pairs={{0,2},{1,3},{2,0},{3,1},{4,6},{5,7},{6,4},{7,5},{8,10},{9,11},{10,... | collective-permute-start | bytes 196616 | tf_op jit(solution)/shard_map/ppermute | solution.py:463
  143.1 6.9 %collective-permute-start.17 = (f32[128,128]{1,0:T(8,128)S(1)}, f32[128,128]{1,0:T(8,128)S(1)}, u32[]{:S(2)}, u32[]{:S(2)}) collective-permute-start(f32[128,128]{1,0:T(8,128)S(1)} %lower.10.refs_0_), channel_id=1, source_target_pairs={{0,6},{1,7},{2,4},{3,5},{4,2},{5,3},{6,0},{7,1},{8,14},{9,15},{10,... | collective-permute-start | bytes 196616 | tf_op jit(solution)/shard_map/ppermute | solution.py:463
  144.6 5.4 %collective-permute-start.18 = (f32[128,128]{1,0:T(8,128)S(1)}, f32[128,128]{1,0:T(8,128)S(1)}, u32[]{:S(2)}, u32[]{:S(2)}) collective-permute-start(f32[128,128]{1,0:T(8,128)S(1)} %lower.10.refs_0_), channel_id=1, source_target_pairs={{0,4},{1,5},{2,6},{3,7},{4,0},{5,1},{6,2},{7,3},{8,12},{9,13},{10,... | collective-permute-start | bytes 196616 | tf_op jit(solution)/shard_map/ppermute | solution.py:463
  171.3 7.0 %collective-permute-start.19 = (f32[128,128]{1,0:T(8,128)S(1)}, f32[128,128]{1,0:T(8,128)S(1)}, u32[]{:S(2)}, u32[]{:S(2)}) collective-permute-start(f32[128,128]{1,0:T(8,128)S(1)} %lower.11.refs_0_), channel_id=1, source_target_pairs={{0,2},{1,3},{2,0},{3,1},{4,6},{5,7},{6,4},{7,5},{8,10},{9,11},{10,... | collective-permute-start | bytes 196616 | tf_op jit(solution)/shard_map/ppermute | solution.py:463
  171.5 6.8 %collective-permute-start.20 = (f32[128,128]{1,0:T(8,128)S(1)}, f32[128,128]{1,0:T(8,128)S(1)}, u32[]{:S(2)}, u32[]{:S(2)}) collective-permute-start(f32[128,128]{1,0:T(8,128)S(1)} %lower.11.refs_0_), channel_id=1, source_target_pairs={{0,6},{1,7},{2,4},{3,5},{4,2},{5,3},{6,0},{7,1},{8,14},{9,15},{10,... | collective-permute-start | bytes 196616 | tf_op jit(solution)/shard_map/ppermute | solution.py:463
  172.9 5.4 %collective-permute-start.21 = (f32[128,128]{1,0:T(8,128)S(1)}, f32[128,128]{1,0:T(8,128)S(1)}, u32[]{:S(2)}, u32[]{:S(2)}) collective-permute-start(f32[128,128]{1,0:T(8,128)S(1)} %lower.11.refs_0_), channel_id=1, source_target_pairs={{0,4},{1,5},{2,6},{3,7},{4,0},{5,1},{6,2},{7,3},{8,12},{9,13},{10,... | collective-permute-start | bytes 196616 | tf_op jit(solution)/shard_map/ppermute | solution.py:463
  199.9 7.8 %collective-permute-start.22 = (f32[128,128]{1,0:T(8,128)S(1)}, f32[128,128]{1,0:T(8,128)S(1)}, u32[]{:S(2)}, u32[]{:S(2)}) collective-permute-start(f32[128,128]{1,0:T(8,128)S(1)} %lower.12.refs_0_), channel_id=1, source_target_pairs={{0,2},{1,3},{2,0},{3,1},{4,6},{5,7},{6,4},{7,5},{8,10},{9,11},{10,... | collective-permute-start | bytes 196616 | tf_op jit(solution)/shard_map/ppermute | solution.py:463
  200.1 7.6 %collective-permute-start.23 = (f32[128,128]{1,0:T(8,128)S(1)}, f32[128,128]{1,0:T(8,128)S(1)}, u32[]{:S(2)}, u32[]{:S(2)}) collective-permute-start(f32[128,128]{1,0:T(8,128)S(1)} %lower.12.refs_0_), channel_id=1, source_target_pairs={{0,6},{1,7},{2,4},{3,5},{4,2},{5,3},{6,0},{7,1},{8,14},{9,15},{10,... | collective-permute-start | bytes 196616 | tf_op jit(solution)/shard_map/ppermute | solution.py:463
  201.6 6.2 %collective-permute-start.24 = (f32[128,128]{1,0:T(8,128)S(1)}, f32[128,128]{1,0:T(8,128)S(1)}, u32[]{:S(2)}, u32[]{:S(2)}) collective-permute-start(f32[128,128]{1,0:T(8,128)S(1)} %lower.12.refs_0_), channel_id=1, source_target_pairs={{0,4},{1,5},{2,6},{3,7},{4,0},{5,1},{6,2},{7,3},{8,12},{9,13},{10,... | collective-permute-start | bytes 196616 | tf_op jit(solution)/shard_map/ppermute | solution.py:463
  230.5 32.7 %collective-permute-start.25 = (f32[7,32,128]{2,1,0:T(8,128)S(1)}, f32[7,32,128]{2,1,0:T(8,128)S(1)}, u32[]{:S(2)}, u32[]{:S(2)}) collective-permute-start(f32[7,32,128]{2,1,0:T(8,128)S(1)} %join.1.early_ref), channel_id=1, source_target_pairs={{0,1},{1,0},{2,3},{3,2},{4,5},{5,4},{6,7},{7,6},{8,9},{9,8},{10,11... | collective-permute-start | bytes 344072 | tf_op jit(solution)/shard_map/ppermute | solution.py:457
  260.1 4.6 %collective-permute-start.28 = (f32[128,128]{1,0:T(8,128)S(1)}, f32[128,128]{1,0:T(8,128)S(1)}, u32[]{:S(2)}, u32[]{:S(2)}) collective-permute-start(f32[128,128]{1,0:T(8,128)S(1)} %lower.13.refs_0_), channel_id=1, source_target_pairs={{0,4},{1,5},{2,6},{3,7},{4,0},{5,1},{6,2},{7,3},{8,12},{9,13},{10,... | collective-permute-start | bytes 196616 | tf_op jit(solution)/shard_map/ppermute | solution.py:463
  (9 other events, 27.6 us)
